TPU v7x, 32 devices: a whole 2x2x4 slice. The times are simulated.
32 devices in a mesh: parts: 2 (over x), wide: 16 (over z, y, core).
Axes of the slice: x: 2, y: 2, z: 4, core: 2. Of those that a mesh axis runs over, the one named last changes fastest.
Arguments:
- tokens: bfloat16 [384, 7168], P(('parts', 'wide')), parts along dimension 0, may hold values from -6 to 6
- expert_ids: int32 [384, 8], P(('parts', 'wide')), parts along dimension 0, may hold values from 0 to 15, as said below
- gates: float32 [384, 8], P(('parts', 'wide')), parts along dimension 0, may hold values from 0.1 to 1
- w_gate: bfloat16 [2, 7168, 8192], P(None, None, 'wide'), may hold values from -0.0625 to 0.0625
- w_up: bfloat16 [2, 7168, 8192], P(None, None, 'wide'), may hold values from -0.0625 to 0.0625
- w_down: bfloat16 [2, 8192, 7168], P(None, 'wide'), may hold values from -0.1875 to 0.1875
Outputs:
- moe_out: bfloat16 [384, 7168], P(('parts', 'wide')), parts along dimension 0
There are 2 independent parts, one for each index of `parts`. A program takes and returns all parts, laid end to end along the dimension named above; an argument that names none is the same for every part. Nothing has to cross between parts.
Inputs may be any that keep to these rules, and one draw needn't show every extreme that they name: `expert_ids`: each row names the 2 experts g * 2 to g * 2 + 1 of each of 4 different groups g, in any order; in each part one group is named by every row.
All inputs are finite; a program needn't handle non-finite values.
Results may differ from a plain program's by a relative error of at most 0.0064.
Values may be sent and summed in bfloat16 or wider, within the bound.
No kernel may reach another device: no remote copies, remote signals or barrier semaphores. Data moves between devices by JAX's collectives and lax.ppermute only.
A program may use at most 128 MiB of HBM per device.

v0:
```python
import jax
import jax.numpy as jnp
from jax import lax
from jax.sharding import PartitionSpec as P

GROUPS = 8
EXP_G = 2


def partner(block, axis, bit):
    count = lax.axis_size(axis)
    route = []
    for low in range(count):
        high = low | 1 << bit
        if high != low and high < count:
            route += [(low, high), (high, low)]
    return lax.ppermute(block, axis, route)


def route_table(expert_ids, gates):
    token_count = expert_ids.shape[0]
    catalog = jnp.arange(GROUPS * EXP_G, dtype=jnp.int32)
    picked = expert_ids[:, :, None] == catalog[None, None, :]
    weight_sum = jnp.sum(jnp.where(picked, gates[:, :, None], 0.0), axis=1)
    return weight_sum.astype(jnp.bfloat16).reshape(token_count, GROUPS, EXP_G)


def selection(expert_ids, wide_count, group_size, slot_count):
    token_count = expert_ids.shape[0]
    group_ids = jnp.arange(GROUPS, dtype=jnp.int32)
    member = jnp.any((expert_ids // EXP_G)[:, :, None] == group_ids[None, None, :], axis=1)
    position = jnp.cumsum(member.astype(jnp.int32), axis=0) - 1
    target = jnp.arange(wide_count, dtype=jnp.int32)
    target_group = (target // group_size)[:, None] == group_ids[None, :]
    target_rank = target % group_size
    member_dest = jnp.any(target_group[:, :, None] & member.T[None, :, :], axis=1)
    position_dest = jnp.sum(jnp.where(target_group[:, :, None], position.T[None, :, :], 0), axis=1)
    stride = token_count // slot_count
    wanted = (
        jnp.arange(slot_count, dtype=jnp.int32)[None, :] * stride + (target_rank % stride)[:, None]
    )
    chosen = member_dest[:, None, :] & (position_dest[:, None, :] == wanted[:, :, None])
    return (chosen, target_group)


def pack(tokens, route_weight, chosen, target_group):
    wide_count, slot_count, token_count = chosen.shape
    pick_table = chosen.astype(jnp.bfloat16).reshape(wide_count * slot_count, token_count)
    packed = jnp.dot(pick_table, tokens, preferred_element_type=jnp.float32).astype(jnp.bfloat16)
    packed = packed.reshape(wide_count, slot_count, tokens.shape[1])
    route_dest = jnp.einsum(
        "dg,tgj->dtj",
        target_group.astype(jnp.float32),
        route_weight.astype(jnp.float32),
        precision=lax.Precision.HIGHEST,
    )
    scaled = jnp.einsum(
        "dst,dtj->dsj", chosen.astype(jnp.float32), route_dest, precision=lax.Precision.HIGHEST
    )
    return (packed, scaled.astype(jnp.bfloat16))


def expert_block(inputs, scales, w_gate, w_up, w_down):
    summed = jnp.zeros((inputs.shape[0], w_down.shape[2]), jnp.float32)
    for expert in range(EXP_G):
        gate_value = jnp.dot(inputs, w_gate[expert], preferred_element_type=jnp.float32)
        lifted = jnp.dot(inputs, w_up[expert], preferred_element_type=jnp.float32)
        hidden = (jax.nn.silu(gate_value) * lifted).astype(jnp.bfloat16)
        summed = summed + scales[:, expert : expert + 1].astype(jnp.float32) * jnp.dot(
            hidden, w_down[expert], preferred_element_type=jnp.float32
        )
    return summed.astype(jnp.bfloat16)


def local(tokens, expert_ids, gates, w_gate, w_up, w_down):
    wide_count = lax.axis_size("wide")
    group_size = wide_count // GROUPS
    token_count = tokens.shape[0]
    model_width = tokens.shape[1]
    route_weight = route_table(expert_ids, gates)
    slot_count = token_count // group_size
    chosen, target_group = selection(expert_ids, wide_count, group_size, slot_count)
    packed, scaled = pack(tokens, route_weight, chosen, target_group)
    arrived, arrived_scale = (
        lax.all_to_all(packed, "wide", split_axis=0, concat_axis=0, tiled=True),
        lax.all_to_all(scaled, "wide", split_axis=0, concat_axis=0, tiled=True),
    )
    my_rank = lax.axis_index("wide") % group_size
    levels = group_size.bit_length() - 1
    held_rows = arrived[None]
    held_scale = arrived_scale[None]
    for level_index in range(levels):
        partner_rows, partner_scale = partner((held_rows, held_scale), "wide", level_index)
        upper_half = my_rank // (1 << level_index) % 2 == 1
        held_rows = jnp.concatenate(
            [
                jnp.where(upper_half, partner_rows, held_rows),
                jnp.where(upper_half, held_rows, partner_rows),
            ],
            0,
        )
        held_scale = jnp.concatenate(
            [
                jnp.where(upper_half, partner_scale, held_scale),
                jnp.where(upper_half, held_scale, partner_scale),
            ],
            0,
        )
    partial_value = expert_block(
        held_rows.reshape(-1, model_width), held_scale.reshape(-1, EXP_G), w_gate, w_up, w_down
    )
    partial_value = partial_value.reshape(group_size, wide_count, slot_count, model_width)
    returned = lax.all_to_all(partial_value, "wide", split_axis=1, concat_axis=1, tiled=True)
    chosen_grouped = chosen.reshape(GROUPS, group_size, slot_count, token_count).transpose(
        1, 0, 2, 3
    )
    pick_rows = jnp.broadcast_to(
        chosen_grouped[:, :, None], (group_size, GROUPS, group_size, slot_count, token_count)
    )
    pick_table = pick_rows.reshape(group_size * wide_count * slot_count, token_count).T.astype(
        jnp.bfloat16
    )
    output = jnp.dot(
        pick_table, returned.reshape(-1, model_width), preferred_element_type=jnp.float32
    )
    return output.astype(jnp.bfloat16)


def solution(mesh):
    return jax.shard_map(
        local,
        mesh=mesh,
        in_specs=(
            P(("parts", "wide"), None),
            P(("parts", "wide"), None),
            P(("parts", "wide"), None),
            P(None, None, "wide"),
            P(None, None, "wide"),
            P(None, "wide", None),
        ),
        out_specs=P(("parts", "wide"), None),
        check_vma=False,
    )
```

profile of v0, /device:TPU:13, one launch (start us, length us, event | category | flops | bytes accessed | tf_op | source)
XLA Modules:
  0.0 191.6 jit_solution(12496329950907122249)
XLA Ops:
  0.0 0.0 copy-start
  0.0 0.8 add_select_fusion
  0.8 0.2 reduce_window_sum.11
  1.0 0.1 copy.54
  1.1 0.1 select_reduce_fusion.1
  1.2 0.1 eq.108
  1.3 0.1 eq.114
  1.4 0.1 copy.51
  1.5 0.1 and_reduce_fusion
  1.6 0.1 and.125
  1.7 0.1 and.129
  1.8 0.1 add.108
  1.9 0.1 add.105
  2.0 0.1 add.109
  2.1 0.0 copy-done
  2.1 0.6 convolution_convert_fusion
  2.6 0.0 copy-start.2
  2.7 0.0 copy-start.3
  2.7 1.5 reshape.140
  4.2 6.6 %all-to-all-start.1 = ((bf16[16,6,7168]{2,1,0:T(8,128)(2,1)}), bf16[16,6,7168]{2,1,0:T(8,128)(2,1)S(1)}, u32[]{:S(2)}, u32[]{:S(2)}) async-start(bf16[16,6,7168]{2,1,0:T(8,128)(2,1)} %reshape.140), calls=%async_computation.1 | async-start | bytes 3670016 | tf_op jit(solution)/shard_map/all_to_all | solution.py:85
  10.8 0.0 copy-done.2
  10.8 0.1 copy.57
  10.8 0.0 copy-done.3
  10.8 0.1 copy.58
  10.9 0.1 select_reduce_fusion
  11.0 0.1 copy.59
  11.1 41.4 %all-to-all-done.1 = bf16[16,6,7168]{2,1,0:T(8,128)(2,1)S(1)} async-done(((bf16[16,6,7168]{2,1,0:T(8,128)(2,1)}), bf16[16,6,7168]{2,1,0:T(8,128)(2,1)S(1)}, u32[]{:S(2)}, u32[]{:S(2)}) %all-to-all-start.1) | async-done | bytes 1376288 | tf_op jit(solution)/shard_map/all_to_all | solution.py:85
  52.6 1.9 copy.64
  54.4 0.2 collective-permute-start.1
  54.6 0.1 broadcast_add_fusion
  54.7 0.2 fusion.34
  54.9 0.1 compare_and_fusion
  55.0 0.8 convolution_convert_fusion.2
  55.8 5.0 %all-to-all-start = ((bf16[16,6,2]{1,2,0:T(2,128)(2,1)}), bf16[16,6,2]{1,2,0:T(2,128)(2,1)S(1)}, u32[]{:S(2)}, u32[]{:S(2)}) async-start(bf16[16,6,2]{1,2,0:T(2,128)(2,1)} %convolution_convert_fusion.2), calls=%async_computation | async-start | bytes 16384 | tf_op jit(solution)/shard_map/all_to_all | solution.py:86
  60.8 3.7 %all-to-all-done = bf16[16,6,2]{1,2,0:T(2,128)(2,1)S(1)} async-done(((bf16[16,6,2]{1,2,0:T(2,128)(2,1)}), bf16[16,6,2]{1,2,0:T(2,128)(2,1)S(1)}, u32[]{:S(2)}, u32[]{:S(2)}) %all-to-all-start) | async-done | bytes 416 | tf_op jit(solution)/shard_map/all_to_all | solution.py:86
  64.5 0.7 collective-permute-start
  65.2 0.8 collective-permute-done
  66.1 0.1 reshape.139
  66.2 0.0 collective-permute-done.1
  66.2 1.7 copy_select_fusion.1
  67.9 2.6 %pad_maximum_fusion = bf16[2,16,6,7168]{3,2,1,0:T(8,128)(2,1)} fusion(bf16[1,16,6,7168]{3,2,1,0:T(8,128)(2,1)S(1)} %get-tuple-element.6, bf16[1,16,6,7168]{3,2,1,0:T(8,128)(2,1)S(1)} %get-tuple-element.5), kind=kLoop, calls=%fused_computation.22 | loop fusion | flops 1376256 | bytes 5505024 | tf_op jit(solution)/shard_map/concatenate | solution.py:95
  70.5 3.2 %reshape.141 = bf16[192,7168]{1,0:T(8,128)(2,1)S(1)} reshape(bf16[2,16,6,7168]{3,2,1,0:T(8,128)(2,1)} %pad_maximum_fusion) | data formatting | bytes 5505024 | tf_op jit(solution)/shard_map/reshape | solution.py:110
  73.7 5.5 %fusion.3 = f32[192,512]{1,0:T(8,128)} fusion(bf16[192,7168]{1,0:T(8,128)(2,1)S(1)} %reshape.141, bf16[2,7168,512]{2,1,0:T(8,128)(2,1)} %param.10), kind=kOutput, calls=%fused_computation.7 | convolution fusion | flops 1409286144 | bytes 10485760 | tf_op jit(solution)/shard_map/dot_general | solution.py:67
  79.2 4.7 %fusion.8 = f32[192,512]{1,0:T(8,128)S(1)} fusion(bf16[192,7168]{1,0:T(8,128)(2,1)S(1)} %reshape.141, bf16[2,7168,512]{2,1,0:T(8,128)(2,1)} %param.10), kind=kOutput, calls=%fused_computation.12 | convolution fusion | flops 1409286144 | bytes 10485760 | tf_op jit(solution)/shard_map/dot_general | solution.py:67
  83.9 10.9 %convolution_multiply_fusion = f32[192,7168]{1,0:T(8,128)} fusion(bf16[2,512,7168]{2,1,0:T(8,128)(2,1)} %param.11, f32[192]{0:T(256)S(1)} %bitcast.69, f32[192,512]{1,0:T(8,128)} %fusion.3, bf16[192,7168]{1,0:T(8,128)(2,1)S(1)} %reshape.141, bf16[2,7168,512]{2,1,0:T(8,128)(2,1)} %param.9), kind=kOutput, calls=%fused_computation | convolution fusion | flops 2820538368 | bytes 23331584 | tf_op jit(solution)/shard_map/dot_general | solution.py:69
  94.8 11.4 %fusion.1 = bf16[192,7168]{1,0:T(8,128)(2,1)} fusion(f32[192,7168]{1,0:T(8,128)} %convolution_multiply_fusion, bf16[2,512,7168]{2,1,0:T(8,128)(2,1)} %param.11, f32[192]{0:T(256)S(1)} %bitcast.68, f32[192,512]{1,0:T(8,128)S(1)} %fusion.8, bf16[192,7168]{1,0:T(8,128)(2,1)S(1)} %reshape.141, bf16[2,7168,512]{2,1,0:T(8,128)(2,1)} %param.9), kind=kOutput, calls=%fused_computation.3 | convolution fusion | flops 2823290880 | bytes 26084096 | tf_op jit(solution)/shard_map/dot_general | solution.py:69
  106.2 4.6 %reshape.142 = bf16[2,16,6,7168]{3,2,1,0:T(8,128)(2,1)} reshape(bf16[192,7168]{1,0:T(8,128)(2,1)} %fusion.1) | data formatting | bytes 5505024 | tf_op jit(solution)/shard_map/reshape | solution.py:112
  110.8 6.4 %copy.67 = bf16[2,16,6,7168]{3,0,2,1:T(2,128)(2,1)} copy(bf16[2,16,6,7168]{3,2,1,0:T(8,128)(2,1)} %reshape.142) | data formatting | bytes 5505024 | tf_op jit(solution)/shard_map/reshape | solution.py:112
  117.2 5.9 %all-to-all-start.2 = ((bf16[2,16,6,7168]{3,0,2,1:T(2,128)(2,1)}), bf16[2,16,6,7168]{3,0,2,1:T(2,128)(2,1)S(1)}, u32[]{:S(2)}, u32[]{:S(2)}) async-start(bf16[2,16,6,7168]{3,0,2,1:T(2,128)(2,1)} %copy.67), calls=%async_computation.2 | async-start | bytes 5505024 | tf_op jit(solution)/shard_map/all_to_all | solution.py:113
  123.2 0.1 copy.55
  123.3 0.1 copy.52
  123.4 0.1 broadcast_add_fusion.1
  123.5 0.1 compare_and_fusion.1
  123.6 61.0 %all-to-all-done.2 = bf16[2,16,6,7168]{3,0,2,1:T(2,128)(2,1)S(1)} async-done(((bf16[2,16,6,7168]{3,0,2,1:T(2,128)(2,1)}), bf16[2,16,6,7168]{3,0,2,1:T(2,128)(2,1)S(1)}, u32[]{:S(2)}, u32[]{:S(2)}) %all-to-all-start.2) | async-done | bytes 2752544 | tf_op jit(solution)/shard_map/all_to_all | solution.py:113
  184.7 0.0 copy-start.1
  184.7 2.5 %copy.68 = bf16[2,16,6,7168]{3,2,1,0:T(8,128)(2,1)} copy(bf16[2,16,6,7168]{3,0,2,1:T(2,128)(2,1)S(1)} %all-to-all-done.2) | data formatting | bytes 5505024 | tf_op jit(solution)/shard_map/all_to_all | solution.py:113
  187.2 3.2 %reshape.143 = bf16[192,7168]{1,0:T(8,128)(2,1)S(1)} reshape(bf16[2,16,6,7168]{3,2,1,0:T(8,128)(2,1)} %copy.68) | data formatting | bytes 5505024 | tf_op jit(solution)/shard_map/reshape | solution.py:124
  190.4 1.2 convolution_convert_fusion.1
  191.6 0.0 copy-done.1
  (19 shorter events, 0.2 us)
Async XLA Ops:
  0.0 2.1 %copy-start = (bf16[12,7168]{1,0:T(8,128)(2,1)S(1)}, bf16[12,7168]{1,0:T(8,128)(2,1)}, u32[]{:S(2)}) copy-start(bf16[12,7168]{1,0:T(8,128)(2,1)} %param.6) | copy-start | bytes 516100
  2.6 8.1 %copy-start.2 = (s32[12,8]{0,1:T(8,128)S(1)}, s32[12,8]{0,1:T(8,128)}, u32[]{:S(2)}) copy-start(s32[12,8]{0,1:T(8,128)} %param.7) | copy-start | bytes 1156
  2.7 8.2 %copy-start.3 = (f32[12,8]{0,1:T(8,128)S(1)}, f32[12,8]{0,1:T(8,128)}, u32[]{:S(2)}) copy-start(f32[12,8]{0,1:T(8,128)} %param.8) | copy-start | bytes 1156
  4.2 48.4 %all-to-all-start.1 = ((bf16[16,6,7168]{2,1,0:T(8,128)(2,1)}), bf16[16,6,7168]{2,1,0:T(8,128)(2,1)S(1)}, u32[]{:S(2)}, u32[]{:S(2)}) async-start(bf16[16,6,7168]{2,1,0:T(8,128)(2,1)} %reshape.140), calls=%async_computation.1 | async-start | bytes 3670016 | tf_op jit(solution)/shard_map/all_to_all | solution.py:85
  54.4 11.8 %collective-permute-start.1 = (bf16[1,16,6,7168]{3,1,2,0:T(8,128)(2,1)}, bf16[1,16,6,7168]{3,1,2,0:T(8,128)(2,1)S(1)}, u32[]{:S(2)}, u32[]{:S(2)}) collective-permute-start(bf16[1,16,6,7168]{3,1,2,0:T(8,128)(2,1)} %copy.64), channel_id=1, source_target_pairs={{0,1},{1,0},{2,3},{3,2},{4,5},{5,4},{6,7},{7,6},{8,9},{9,8},{10,11... | collective-permute-start | bytes 4128776 | tf_op jit(solution)/shard_map/ppermute | solution.py:17
  55.8 8.7 %all-to-all-start = ((bf16[16,6,2]{1,2,0:T(2,128)(2,1)}), bf16[16,6,2]{1,2,0:T(2,128)(2,1)S(1)}, u32[]{:S(2)}, u32[]{:S(2)}) async-start(bf16[16,6,2]{1,2,0:T(2,128)(2,1)} %convolution_convert_fusion.2), calls=%async_computation | async-start | bytes 16384 | tf_op jit(solution)/shard_map/all_to_all | solution.py:86
  64.5 1.5 collective-permute-start
  117.2 67.4 %all-to-all-start.2 = ((bf16[2,16,6,7168]{3,0,2,1:T(2,128)(2,1)}), bf16[2,16,6,7168]{3,0,2,1:T(2,128)(2,1)S(1)}, u32[]{:S(2)}, u32[]{:S(2)}) async-start(bf16[2,16,6,7168]{3,0,2,1:T(2,128)(2,1)} %copy.67), calls=%async_computation.2 | async-start | bytes 5505024 | tf_op jit(solution)/shard_map/all_to_all | solution.py:113
  184.7 7.0 %copy-start.1 = (bf16[12,7168]{1,0:T(8,128)(2,1)S(1)}, bf16[12,7168]{1,0:T(8,128)(2,1)}, u32[]{:S(2)}) copy-start(bf16[12,7168]{1,0:T(8,128)(2,1)} %param.6) | copy-start | bytes 516100
where the time goes:
time: 192 us
  waiting for transfers between devices  107 us (56%)
  matrix products  35.2 us (18%)
  local copies, waits for them, and re-layouts  24.9 us (13%)
  starting transfers between devices  18.4 us (10%)
  other arithmetic  5.96 us (3%)
    all_to_all x1, waiting for transfers between devices, local(): lax.all_to_all(partial_value, 'wide', split_axis=1, concat_axis=1, tiled=...  61 us
    all_to_all x1, waiting for transfers between devices, local(): lax.all_to_all(packed, 'wide', split_axis=0, concat_axis=0, tiled=True)  41.4 us
    dot_general x2, matrix products, expert_block(): jnp.dot(hidden, w_down[expert], preferred_element_type=jnp.float32)  22.3 us
    reshape x2, local copies, waits for them, and re-layouts, local(): partial_value.reshape(group_size, wide_count, slot_count, model_width)  11 us
    dot_general x2, matrix products, expert_block(): lifted = jnp.dot(inputs, w_up[expert], preferred_element_type=jnp.float32)  10.1 us
    all_to_all x1, starting transfers between devices, local(): lax.all_to_all(packed, 'wide', split_axis=0, concat_axis=0, tiled=True)  6.56 us
    all_to_all x1, starting transfers between devices, local(): lax.all_to_all(partial_value, 'wide', split_axis=1, concat_axis=1, tiled=...  5.94 us
    all_to_all x1, starting transfers between devices, local(): lax.all_to_all(scaled, 'wide', split_axis=0, concat_axis=0, tiled=True)  4.99 us
  transfers between devices with their start and end apart: 5, of which 4 were waited for; matrix products, arithmetic and copies ran while one was open for 1% of the time, Pallas kernels for 0%

commit v1 on v0

v1 whole, which is shorter than its diff:
```python
import functools

import jax
import jax.numpy as jnp
from jax import lax
from jax.experimental import pallas as pl
from jax.experimental.pallas import tpu as pltpu
from jax.sharding import PartitionSpec as P

GROUPS = 8
EXP_G = 2
LANES = 128
TILE = 8
MIB = 1 << 20
IN_CHUNKS = 4
OUT_CHUNKS = 4
bf16 = jnp.bfloat16
f32 = jnp.float32


def swap(block, bits, count):
    return lax.ppermute(block, "wide", [(i, i ^ bits) for i in range(count)])


def half_roll(block):
    return pltpu.roll(block, TILE // 2, 0)


def low_half(shape):
    return lax.broadcasted_iota(jnp.int32, shape, 0) < TILE // 2


def unpack_pair(u, v):
    full = (u.shape[0] - TILE) // 2
    u_rest, v_rest = u[2 * full :], v[2 * full :]
    low = low_half(u_rest.shape)
    a = [u[:full], v[:full], jnp.where(low, u_rest, half_roll(v_rest))]
    b = [u[full : 2 * full], v[full : 2 * full], jnp.where(low, half_roll(u_rest), v_rest)]
    return a, b


def pack_pair(a, b):
    full = (a.shape[0] - TILE) // 2
    a_rest, b_rest = a[2 * full :], b[2 * full :]
    low = low_half(a_rest.shape)
    u = [a[:full], b[:full], jnp.where(low, a_rest, half_roll(b_rest))]
    v = [a[full : 2 * full], b[full : 2 * full], jnp.where(low, half_roll(a_rest), b_rest)]
    return u, v


def prepare_kernel(chunks, tokens_ref, ids_ref, gates_ref, *refs):
    outs, rows_ref, route_ref = refs[:chunks], refs[chunks], refs[chunks + 1]
    rows, width = tokens_ref.shape
    full = rows // TILE * TILE
    half = width // chunks // 2
    rows_ref[0:rows, :] = tokens_ref[...].astype(f32)
    catalog = lax.broadcasted_iota(jnp.int32, (rows, LANES), 1)
    weight = jnp.zeros((rows, LANES), f32)
    for k in range(ids_ref.shape[1]):
        weight = weight + jnp.where(ids_ref[:, k : k + 1] == catalog, gates_ref[:, k : k + 1], 0.0)
    route_ref[0:rows, :] = weight

    def packed(a_first, b_first, a_rest, b_rest):
        low = low_half(a_rest.shape)
        rest = jnp.where(low, a_rest, half_roll(b_rest))
        return jnp.concatenate([a_first, b_first, rest], 0).astype(bf16)

    for c in range(chunks):
        a = slice(2 * c * half, (2 * c + 1) * half)
        b = slice((2 * c + 1) * half, (2 * c + 2) * half)
        outs[c][:, 0:half] = packed(
            rows_ref[0:full, a], rows_ref[0:full, b], rows_ref[full : full + TILE, a], rows_ref[full : full + TILE, b]
        )
    outs[0][:, half : half + LANES] = packed(
        route_ref[0:full, :],
        jnp.zeros((full, LANES), f32),
        route_ref[full : full + TILE, :],
        jnp.zeros((TILE, LANES), f32),
    )


def prepare(tokens, expert_ids, gates, chunks):
    rows, width = tokens.shape
    half = width // chunks // 2
    padded = -(-rows // TILE) * TILE
    shapes = [jax.ShapeDtypeStruct((2 * rows, half + (LANES if c == 0 else 0)), bf16) for c in range(chunks)]
    return pl.pallas_call(
        functools.partial(prepare_kernel, chunks),
        out_shape=shapes,
        scratch_shapes=[pltpu.VMEM((padded, width), f32), pltpu.VMEM((padded, LANES), f32)],
    )(tokens, expert_ids, gates)


def unpack_rows(refs, half, unit, lhs_ref, route_ref):
    at = 0
    for ref in refs:
        for start in range(0, ref.shape[0], 4 * unit):
            block = ref[start : start + 4 * unit, :].astype(f32)
            pieces_a, pieces_b = [], []
            for pair in range(2):
                u = block[2 * pair * unit : (2 * pair + 1) * unit]
                v = block[(2 * pair + 1) * unit : (2 * pair + 2) * unit]
                a, b = unpack_pair(u, v)
                pieces_a += a
                pieces_b += b
            rows_a = jnp.concatenate(pieces_a, 0)
            count = rows_a.shape[0]
            lhs_ref[at : at + count, 0:half] = rows_a[:, :half].astype(bf16)
            lhs_ref[at : at + count, half : 2 * half] = jnp.concatenate(pieces_b, 0)[:, :half].astype(bf16)
            if route_ref is not None:
                route_ref[at : at + count, :] = rows_a[:, half:]
            at += count


def down_chunk(hidden, weight_ref, half, unit, keep_ref, send_ref):
    rows = hidden.shape[0]
    depth = weight_ref.shape[1]
    total = None
    for expert in range(EXP_G):
        part = jnp.dot(
            hidden[:, expert * depth : (expert + 1) * depth], weight_ref[expert], preferred_element_type=f32
        )
        total = part if total is None else total + part
    blocks = []
    for at in range(0, rows, unit):
        u, v = pack_pair(total[at : at + unit, :half], total[at : at + unit, half:])
        blocks += u + v
    packed = jnp.concatenate(blocks, 0).astype(bf16)
    keep_ref[...] = packed[:rows]
    send_ref[...] = packed[rows:]


def first_kernel(index, half, unit, first, last, *refs):
    refs = list(refs)
    near_ref, next_ref, other_ref = refs[:3]
    refs = refs[3:]
    if first:
        group_ref = refs.pop(0)
    else:
        prior_ref = refs.pop(0)
        if last:
            scale_ref = refs.pop(0)
    gate_ref, up_ref = refs[:2]
    refs = refs[2:]
    if last:
        down_ref, hidden_ref, keep_ref, send_ref = refs[:4]
        refs = refs[4:]
    else:
        acc_ref = refs.pop(0)
        if first:
            scale_ref = refs.pop(0)
    lhs_ref, weights_ref, sems = refs[:3]
    width = 2 * half
    copies = []
    for expert in range(EXP_G):
        for which, source in enumerate((gate_ref, up_ref)):
            copy = pltpu.make_async_copy(
                source.at[expert, pl.ds(index * width, width), :],
                weights_ref.at[expert, which],
                sems.at[2 * expert + which],
            )
            copy.start()
            copies.append(copy)
    if last:
        down_weights_ref, down_sem = refs[3:5]
        down_copy = pltpu.make_async_copy(down_ref.at[:, :, pl.ds(0, down_weights_ref.shape[2])], down_weights_ref, down_sem)
        down_copy.start()
    route_ref = refs[3] if first else None
    unpack_rows((near_ref, next_ref, other_ref), half, unit, lhs_ref, route_ref)
    if first:
        lane = lax.broadcasted_iota(jnp.int32, route_ref.shape, 1)
        for expert in range(EXP_G):
            chosen = jnp.where(lane == group_ref[0] * EXP_G + expert, route_ref[...], 0.0)
            scale_ref[expert] = jnp.broadcast_to(jnp.sum(chosen, 1, keepdims=True), route_ref.shape)
    depth = gate_ref.shape[2]
    hidden = []
    for expert in range(EXP_G):
        parts = []
        for which in range(2):
            copies[2 * expert + which].wait()
            value = jnp.dot(lhs_ref[...], weights_ref[expert, which], preferred_element_type=f32)
            if not first:
                value = value + prior_ref[expert, which]
            if last:
                parts.append(value)
            else:
                acc_ref[expert, which] = value
        if last:
            gate_value, lifted = parts
            value = gate_value / (1.0 + jnp.exp(-gate_value)) * lifted * scale_ref[expert][:, 0:1]
            hidden_ref[:, expert * depth : (expert + 1) * depth] = value.astype(bf16)
    if last:
        down_copy.wait()
        down_chunk(hidden_ref[...], down_weights_ref, down_weights_ref.shape[2] // 2, unit, keep_ref, send_ref)


def expert_step(index, chunks, blocks, extra, w_gate, w_up, w_down, unit, out_chunks):
    first, last = index == 0, index == chunks - 1
    width = w_gate.shape[1] // chunks
    half = width // 2
    depth = w_gate.shape[2]
    rows = sum(b.shape[0] for b in blocks) // 2
    vmem = pl.BlockSpec(memory_space=pltpu.VMEM)
    hbm = pl.BlockSpec(memory_space=pl.ANY)
    smem = pl.BlockSpec(memory_space=pltpu.SMEM)
    scratch = [
        pltpu.VMEM((rows, width), bf16),
        pltpu.VMEM((EXP_G, 2, width, depth), bf16),
        pltpu.SemaphoreType.DMA((2 * EXP_G,)),
    ]
    args, specs = list(blocks), [vmem] * len(blocks)
    args += list(extra)
    specs += [smem] if first else [vmem] * len(extra)
    args += [w_gate, w_up]
    specs += [hbm, hbm]
    bytes_in = EXP_G * 2 * width * depth * 2
    if last:
        columns = w_down.shape[2] // out_chunks
        args.append(w_down)
        specs.append(hbm)
        shapes = [
            jax.ShapeDtypeStruct((rows, EXP_G * depth), bf16),
            jax.ShapeDtypeStruct((rows, columns // 2), bf16),
            jax.ShapeDtypeStruct((rows, columns // 2), bf16),
        ]
        scratch += [pltpu.VMEM((EXP_G, depth, columns), bf16), pltpu.SemaphoreType.DMA]
        bytes_in += EXP_G * depth * columns * 2
    else:
        shapes = [jax.ShapeDtypeStruct((EXP_G, 2, rows, depth), f32)]
        if first:
            shapes.append(jax.ShapeDtypeStruct((EXP_G, rows, LANES), f32))
            scratch.append(pltpu.VMEM((rows, LANES), f32))
    return pl.pallas_call(
        functools.partial(first_kernel, index, half, unit, first, last),
        out_shape=shapes,
        in_specs=specs,
        out_specs=[vmem] * len(shapes),
        scratch_shapes=scratch,
        compiler_params=pltpu.CompilerParams(vmem_limit_bytes=48 * MIB),
        cost_estimate=pl.CostEstimate(flops=rows * bytes_in, bytes_accessed=bytes_in, transcendentals=0),
    )(*args)


def down_kernel(index, half, unit, hidden_ref, down_ref, keep_ref, send_ref, weights_ref, sem):
    columns = 2 * half
    copy = pltpu.make_async_copy(down_ref.at[:, :, pl.ds(index * columns, columns)], weights_ref, sem)
    copy.start()
    copy.wait()
    down_chunk(hidden_ref[...], weights_ref, half, unit, keep_ref, send_ref)


def down_step(index, chunks, hidden, w_down, unit):
    columns = w_down.shape[2] // chunks
    depth = w_down.shape[1]
    rows = hidden.shape[0]
    vmem = pl.BlockSpec(memory_space=pltpu.VMEM)
    bytes_in = EXP_G * depth * columns * 2
    return pl.pallas_call(
        functools.partial(down_kernel, index, columns // 2, unit),
        out_shape=[jax.ShapeDtypeStruct((rows, columns // 2), bf16)] * 2,
        in_specs=[vmem, pl.BlockSpec(memory_space=pl.ANY)],
        out_specs=[vmem] * 2,
        scratch_shapes=[pltpu.VMEM((EXP_G, depth, columns), bf16), pltpu.SemaphoreType.DMA],
        compiler_params=pltpu.CompilerParams(vmem_limit_bytes=48 * MIB),
        cost_estimate=pl.CostEstimate(flops=rows * bytes_in, bytes_accessed=bytes_in, transcendentals=0),
    )(hidden, w_down)


def finish_kernel(chunks, rows, *refs):
    out_ref, whole_ref = refs[-2:]
    refs = refs[:-2]
    per = len(refs) // chunks
    full = rows // TILE * TILE
    half = refs[0].shape[1]
    for c in range(chunks):
        total = refs[c * per][...].astype(f32)
        for ref in refs[c * per + 1 : (c + 1) * per]:
            total = total + ref[...].astype(f32)
        a = slice(2 * c * half, (2 * c + 1) * half)
        b = slice((2 * c + 1) * half, (2 * c + 2) * half)
        rest = total[2 * full :]
        whole_ref[0:full, a] = total[:full]
        whole_ref[0:full, b] = total[full : 2 * full]
        whole_ref[full : full + TILE, a] = rest
        whole_ref[full : full + TILE, b] = half_roll(rest)
    out_ref[...] = whole_ref[0:rows, :].astype(bf16)


def finish(parts, rows, width):
    chunks = len(parts)
    padded = -(-rows // TILE) * TILE
    return pl.pallas_call(
        functools.partial(finish_kernel, chunks, rows),
        out_shape=jax.ShapeDtypeStruct((rows, width), bf16),
        scratch_shapes=[pltpu.VMEM((padded, width), f32)],
    )(*[p for chunk in parts for p in chunk])


def local(tokens, expert_ids, gates, w_gate, w_up, w_down):
    count = lax.axis_size("wide")
    group_size = count // GROUPS
    far = count // 4
    rows, width = tokens.shape
    unit = 2 * rows
    group = (lax.axis_index("wide") // group_size).astype(jnp.int32).reshape(1)
    chunks = prepare(tokens, expert_ids, gates, IN_CHUNKS)

    state = None
    for c, own in enumerate(chunks):
        line = jnp.concatenate([own] + [swap(own, 4 * f, count) for f in range(1, far)], 0)
        crossed = swap(line, 2, count)
        other = swap(jnp.concatenate([line, crossed], 0), 1, count)
        blocks = (line, crossed, other)
        if c == 0:
            extra = [group]
        elif c < IN_CHUNKS - 1:
            extra = [state]
        else:
            extra = [state, scale]
        result = expert_step(c, IN_CHUNKS, blocks, extra, w_gate, w_up, w_down, unit, OUT_CHUNKS)
        if c == 0:
            state, scale = result
        elif c < IN_CHUNKS - 1:
            state = result[0]
    hidden, keep, send = result

    parts = []
    for c in range(OUT_CHUNKS):
        if c > 0:
            keep, send = down_step(c, OUT_CHUNKS, hidden, w_down, unit)
        got = swap(send, 1, count)
        summed = (keep.astype(f32) + got.astype(f32)).astype(bf16)
        middle = summed.shape[0] // 2
        got = swap(summed[middle:], 2, count)
        summed = (summed[:middle].astype(f32) + got.astype(f32)).astype(bf16)
        pieces = [summed[f * unit : (f + 1) * unit] for f in range(far)]
        parts.append([pieces[0]] + [swap(pieces[f], 4 * f, count) for f in range(1, far)])
    return finish(parts, rows, width)


def solution(mesh):
    return jax.shard_map(
        local,
        mesh=mesh,
        in_specs=(
            P(("parts", "wide"), None),
            P(("parts", "wide"), None),
            P(("parts", "wide"), None),
            P(None, None, "wide"),
            P(None, None, "wide"),
            P(None, "wide", None),
        ),
        out_specs=P(("parts", "wide"), None),
        check_vma=False,
    )
```

time: 192 us -> 114 us (0.59)
  the two profiles are of different devices: /device:TPU:13 before, /device:TPU:0 now
where the time goes in v1:
time: 114 us
  starting transfers between devices  46.4 us (41%)
  waiting for transfers between devices  29 us (25%)
  Pallas kernels  28.8 us (25%)
  local copies, waits for them, and re-layouts  8.49 us (7%)
    ppermute x40, starting transfers between devices, swap(): return lax.ppermute(block, 'wide', [(i, i ^ bits) for i in range(count)])  46.4 us
    ppermute x40, waiting for transfers between devices, swap(): return lax.ppermute(block, 'wide', [(i, i ^ bits) for i in range(count)])  29 us
    pallas_call x4, Pallas kernels, expert_step(): pl.pallas_call(functools.partial(first_kernel, index, half, unit, first,...  16.4 us
    pallas_call x3, Pallas kernels, down_step(): pl.pallas_call(functools.partial(down_kernel, index, columns // 2, unit),...  8.81 us
    unnamed x41, local copies, waits for them, and re-layouts  5.84 us
    slice x4, local copies, waits for them, and re-layouts, local(): pieces = [summed[f * unit:(f + 1) * unit] for f in range(far)]  2.51 us
  transfers between devices with their start and end apart: 40, of which 11 were waited for; matrix products, arithmetic and copies ran while one was open for 5% of the time, Pallas kernels for 15%

profile of v1, /device:TPU:0, one launch (start us, length us, event | category | flops | bytes accessed | tf_op | source)
XLA Modules:
  0.0 113.5 jit_solution(17433578625795013527)
XLA Ops:
  0.0 1.4 %copy.7.ids_ref = s32[12,8]{1,0:T(8,128)} copy(s32[12,8]{0,1:T(8,128)} %param.7) | data formatting | bytes 768 | tf_op args[1]
  1.4 1.4 %copy.8.gates_ref = f32[12,8]{1,0:T(8,128)} copy(f32[12,8]{0,1:T(8,128)} %param.8) | data formatting | bytes 768 | tf_op args[2]
  2.7 1.7 %shard_map.64 = (bf16[24,1024]{1,0:T(8,128)(2,1)}, bf16[24,896]{1,0:T(8,128)(2,1)}, bf16[24,896]{1,0:T(8,128)(2,1)}, bf16[24,896]{1,0:T(8,128)(2,1)}) custom-call(bf16[12,7168]{1,0:T(8,128)(2,1)} %tokens_ref.1, s32[12,8]{1,0:T(8,128)} %copy.7.ids_ref, f32[12,8]{1,0:T(8,128)} %copy.8.gates_ref), custom_call_target="tpu_custom_call" | custom-call | tf_op jit(solution)/shard_map/pallas_call | solution.py:87
  4.4 3.0 %collective-permute-start.15 = (bf16[24,1024]{1,0:T(8,128)(2,1)}, bf16[24,1024]{1,0:T(8,128)(2,1)S(1)}, u32[]{:S(2)}, u32[]{:S(2)}) collective-permute-start(bf16[24,1024]{1,0:T(8,128)(2,1)} %get-tuple-element.23), channel_id=1, source_target_pairs={{0,4},{1,5},{2,6},{3,7},{4,0},{5,1},{6,2},{7,3},{8,12},{9,13},{10,... | collective-permute-start | bytes 147464 | tf_op jit(solution)/shard_map/ppermute | solution.py:22
  7.4 2.6 %collective-permute-start.16 = (bf16[24,1024]{1,0:T(8,128)(2,1)}, bf16[24,1024]{1,0:T(8,128)(2,1)S(1)}, u32[]{:S(2)}, u32[]{:S(2)}) collective-permute-start(bf16[24,1024]{1,0:T(8,128)(2,1)} %get-tuple-element.23), channel_id=1, source_target_pairs={{0,8},{1,9},{2,10},{3,11},{4,12},{5,13},{6,14},{7,15},{8,0},{9,1},... | collective-permute-start | bytes 147464 | tf_op jit(solution)/shard_map/ppermute | solution.py:22
  10.0 0.9 collective-permute-start.10
  10.9 3.5 %collective-permute-start.11 = (bf16[24,896]{1,0:T(8,128)(2,1)}, bf16[24,896]{1,0:T(8,128)(2,1)S(1)}, u32[]{:S(2)}, u32[]{:S(2)}) collective-permute-start(bf16[24,896]{1,0:T(8,128)(2,1)} %get-tuple-element.22), channel_id=1, source_target_pairs={{0,8},{1,9},{2,10},{3,11},{4,12},{5,13},{6,14},{7,15},{8,0},{9,1},... | collective-permute-start | bytes 129032 | tf_op jit(solution)/shard_map/ppermute | solution.py:22
  14.4 0.8 constant_dynamic-update-slice_fusion.35
  15.2 0.8 constant_dynamic-update-slice_fusion.8
  16.0 0.8 constant_dynamic-update-slice_fusion.26
  16.8 1.3 %collective-permute-start.12 = (bf16[24,896]{1,0:T(8,128)(2,1)}, bf16[24,896]{1,0:T(8,128)(2,1)S(1)}, u32[]{:S(2)}, u32[]{:S(2)}) collective-permute-start(bf16[24,896]{1,0:T(8,128)(2,1)} %get-tuple-element.22), channel_id=1, source_target_pairs={{0,12},{1,13},{2,14},{3,15},{4,8},{5,9},{6,10},{7,11},{8,4},{9,5},... | collective-permute-start | bytes 129032 | tf_op jit(solution)/shard_map/ppermute | solution.py:22
  18.3 4.9 %collective-permute-done.12 = bf16[24,896]{1,0:T(8,128)(2,1)S(1)} collective-permute-done((bf16[24,896]{1,0:T(8,128)(2,1)}, bf16[24,896]{1,0:T(8,128)(2,1)S(1)}, u32[]{:S(2)}, u32[]{:S(2)}) %collective-permute-start.12) | collective-permute-done | bytes 43040 | tf_op jit(solution)/shard_map/ppermute | solution.py:22
  23.2 2.3 %collective-permute-start.7 = (bf16[24,896]{1,0:T(8,128)(2,1)}, bf16[24,896]{1,0:T(8,128)(2,1)S(1)}, u32[]{:S(2)}, u32[]{:S(2)}) collective-permute-start(bf16[24,896]{1,0:T(8,128)(2,1)} %get-tuple-element.21), channel_id=1, source_target_pairs={{0,12},{1,13},{2,14},{3,15},{4,8},{5,9},{6,10},{7,11},{8,4},{9,5},... | collective-permute-start | bytes 129032 | tf_op jit(solution)/shard_map/ppermute | solution.py:22
  25.4 2.8 %collective-permute-done.6 = bf16[24,896]{1,0:T(8,128)(2,1)S(1)} collective-permute-done((bf16[24,896]{1,0:T(8,128)(2,1)}, bf16[24,896]{1,0:T(8,128)(2,1)S(1)}, u32[]{:S(2)}, u32[]{:S(2)}) %collective-permute-start.6) | collective-permute-done | bytes 43040 | tf_op jit(solution)/shard_map/ppermute | solution.py:22
  28.3 1.2 %collective-permute-done.7 = bf16[24,896]{1,0:T(8,128)(2,1)S(1)} collective-permute-done((bf16[24,896]{1,0:T(8,128)(2,1)}, bf16[24,896]{1,0:T(8,128)(2,1)S(1)}, u32[]{:S(2)}, u32[]{:S(2)}) %collective-permute-start.7) | collective-permute-done | bytes 43040 | tf_op jit(solution)/shard_map/ppermute | solution.py:22
  29.5 2.3 %collective-permute-start.1 = (bf16[24,896]{1,0:T(8,128)(2,1)}, bf16[24,896]{1,0:T(8,128)(2,1)S(1)}, u32[]{:S(2)}, u32[]{:S(2)}) collective-permute-start(bf16[24,896]{1,0:T(8,128)(2,1)} %get-tuple-element.20), channel_id=1, source_target_pairs={{0,8},{1,9},{2,10},{3,11},{4,12},{5,13},{6,14},{7,15},{8,0},{9,1},... | collective-permute-start | bytes 129032 | tf_op jit(solution)/shard_map/ppermute | solution.py:22
  31.8 1.0 collective-permute-start.2
  32.9 1.6 %collective-permute-start.13 = (bf16[96,896]{1,0:T(8,128)(2,1)S(1)}, bf16[96,896]{1,0:T(8,128)(2,1)S(1)}, u32[]{:S(2)}, u32[]{:S(2)}) collective-permute-start(bf16[96,896]{1,0:T(8,128)(2,1)S(1)} %get-tuple-element.60.refs_0_), channel_id=1, source_target_pairs={{0,2},{1,3},{2,0},{3,1},{4,6},{5,7},{6,4},{7,5},{8,10},{9,11},{10,... | collective-permute-start | bytes 516104 | tf_op jit(solution)/shard_map/ppermute | solution.py:22
  34.5 0.6 collective-permute-start.8
  35.0 1.6 %collective-permute-start.18 = (bf16[96,1024]{1,0:T(8,128)(2,1)S(1)}, bf16[96,1024]{1,0:T(8,128)(2,1)S(1)}, u32[]{:S(2)}, u32[]{:S(2)}) collective-permute-start(bf16[96,1024]{1,0:T(8,128)(2,1)S(1)} %get-tuple-element.52.refs_0_), channel_id=1, source_target_pairs={{0,2},{1,3},{2,0},{3,1},{4,6},{5,7},{6,4},{7,5},{8,10},{9,11},{10,... | collective-permute-start | bytes 589832 | tf_op jit(solution)/shard_map/ppermute | solution.py:22
  36.7 5.6 %collective-permute-done.18.refs_1_ = bf16[96,1024]{1,0:T(8,128)(2,1)S(1)} collective-permute-done((bf16[96,1024]{1,0:T(8,128)(2,1)S(1)}, bf16[96,1024]{1,0:T(8,128)(2,1)S(1)}, u32[]{:S(2)}, u32[]{:S(2)}) %collective-permute-start.18) | collective-permute-done | bytes 196640 | tf_op jit(solution)/shard_map/ppermute | solution.py:22
  42.4 1.6 %collective-permute-start.3 = (bf16[96,896]{1,0:T(8,128)(2,1)S(1)}, bf16[96,896]{1,0:T(8,128)(2,1)S(1)}, u32[]{:S(2)}, u32[]{:S(2)}) collective-permute-start(bf16[96,896]{1,0:T(8,128)(2,1)S(1)} %get-tuple-element.76.refs_0_), channel_id=1, source_target_pairs={{0,2},{1,3},{2,0},{3,1},{4,6},{5,7},{6,4},{7,5},{8,10},{9,11},{10,... | collective-permute-start | bytes 516104 | tf_op jit(solution)/shard_map/ppermute | solution.py:22
  44.0 0.3 collective-permute-start.14
  44.3 0.4 collective-permute-start.9
  44.7 4.5 %collective-permute-done.3.refs_1_ = bf16[96,896]{1,0:T(8,128)(2,1)S(1)} collective-permute-done((bf16[96,896]{1,0:T(8,128)(2,1)S(1)}, bf16[96,896]{1,0:T(8,128)(2,1)S(1)}, u32[]{:S(2)}, u32[]{:S(2)}) %collective-permute-start.3) | collective-permute-done | bytes 172064 | tf_op jit(solution)/shard_map/ppermute | solution.py:22
  49.4 3.7 %shard_map.65 = (f32[2,2,192,512]{3,2,1,0:T(8,128)S(1)}, f32[2,192,128]{2,1,0:T(8,128)S(1)}) custom-call(bf16[96,1024]{1,0:T(8,128)(2,1)S(1)} %get-tuple-element.52.refs_0_, bf16[96,1024]{1,0:T(8,128)(2,1)S(1)} %collective-permute-done.18.refs_1_, bf16[192,1024]{1,0:T(8,128)(2,1)S(1)} %collective-permute-done.19.refs_2_, s32[1]{0:T(128)} %bitcast.refs_3_, ...), custom_call_target="tpu_custom_call" | custom-call | flops 1409286144 | bytes 7340032 | tf_op jit(solution)/shard_map/pallas_call | solution.py:233
  53.1 3.7 %shard_map.66.refs_3_ = f32[2,2,192,512]{3,2,1,0:T(8,128)S(1)} custom-call(bf16[96,896]{1,0:T(8,128)(2,1)S(1)} %get-tuple-element.60.refs_0_, bf16[96,896]{1,0:T(8,128)(2,1)S(1)} %collective-permute-done.13.refs_1_, bf16[192,896]{1,0:T(8,128)(2,1)S(1)} %collective-permute-done.14.refs_2_, f32[2,2,192,512]{3,2,1,0:T(8,128)S(1)} %get-tuple-element.24.refs_3_, ...), custom_call_target="tpu_custom_call" | custom-call | flops 1409286144 | bytes 7340032 | tf_op jit(solution)/shard_map/pallas_call | solution.py:233
  56.9 3.7 %shard_map.67.refs_3_ = f32[2,2,192,512]{3,2,1,0:T(8,128)S(1)} custom-call(bf16[96,896]{1,0:T(8,128)(2,1)S(1)} %get-tuple-element.68.refs_0_, bf16[96,896]{1,0:T(8,128)(2,1)S(1)} %collective-permute-done.8.refs_1_, bf16[192,896]{1,0:T(8,128)(2,1)S(1)} %collective-permute-done.9.refs_2_, f32[2,2,192,512]{3,2,1,0:T(8,128)S(1)} %shard_map.66.refs_3_, ...), custom_call_target="tpu_custom_call" | custom-call | flops 1409286144 | bytes 7340032 | tf_op jit(solution)/shard_map/pallas_call | solution.py:233
  60.6 5.3 %shard_map.68 = (bf16[192,1024]{1,0:T(8,128)(2,1)S(1)}, bf16[192,896]{1,0:T(8,128)(2,1)S(1)}, bf16[192,896]{1,0:T(8,128)(2,1)S(1)}) custom-call(bf16[96,896]{1,0:T(8,128)(2,1)S(1)} %get-tuple-element.76.refs_0_, bf16[96,896]{1,0:T(8,128)(2,1)S(1)} %collective-permute-done.3.refs_1_, bf16[192,896]{1,0:T(8,128)(2,1)S(1)} %collective-permute-done.4.refs_2_, ...), custom_call_target="tpu_custom_call" | custom-call | flops 2113929216 | bytes 11010048 | tf_op jit(solution)/shard_map/pallas_call | solution.py:233
  65.8 2.9 %shard_map.71 = (bf16[192,896]{1,0:T(8,128)(2,1)S(1)}, bf16[192,896]{1,0:T(8,128)(2,1)S(1)}) custom-call(bf16[192,1024]{1,0:T(8,128)(2,1)S(1)} %get-tuple-element.28.hidden_ref, bf16[2,512,7168]{2,1,0:T(8,128)(2,1)} %down_ref.5), custom_call_target="tpu_custom_call" | custom-call | flops 704643072 | bytes 3670016 | tf_op jit(solution)/shard_map/pallas_call | solution.py:258
  68.8 0.6 collective-permute-start.35
  69.4 2.9 %shard_map.70 = (bf16[192,896]{1,0:T(8,128)(2,1)S(1)}, bf16[192,896]{1,0:T(8,128)(2,1)S(1)}) custom-call(bf16[192,1024]{1,0:T(8,128)(2,1)S(1)} %get-tuple-element.28.hidden_ref, bf16[2,512,7168]{2,1,0:T(8,128)(2,1)} %down_ref.5), custom_call_target="tpu_custom_call" | custom-call | flops 704643072 | bytes 3670016 | tf_op jit(solution)/shard_map/pallas_call | solution.py:258
  72.4 2.9 %shard_map.69 = (bf16[192,896]{1,0:T(8,128)(2,1)S(1)}, bf16[192,896]{1,0:T(8,128)(2,1)S(1)}) custom-call(bf16[192,1024]{1,0:T(8,128)(2,1)S(1)} %get-tuple-element.28.hidden_ref, bf16[2,512,7168]{2,1,0:T(8,128)(2,1)} %down_ref.5), custom_call_target="tpu_custom_call" | custom-call | flops 704643072 | bytes 3670016 | tf_op jit(solution)/shard_map/pallas_call | solution.py:258
  75.3 0.6 collective-permute-start.25
  76.0 0.1 add_convert_fusion
  76.1 1.6 %collective-permute-start.36 = (bf16[96,896]{1,0:T(8,128)(2,1)S(1)}, bf16[96,896]{1,0:T(8,128)(2,1)S(1)}, u32[]{:S(2)}, u32[]{:S(2)}) collective-permute-start(bf16[96,896]{1,0:T(8,128)(2,1)S(1)} %slice.115), channel_id=1, source_target_pairs={{0,2},{1,3},{2,0},{3,1},{4,6},{5,7},{6,4},{7,5},{8,10},{9,11},{10,... | collective-permute-start | bytes 516104 | tf_op jit(solution)/shard_map/ppermute | solution.py:22
  77.7 0.1 add_convert_fusion.1
  77.8 0.6 collective-permute-start.31
  78.3 0.1 add_convert_fusion.2
  78.5 1.6 %collective-permute-start.26 = (bf16[96,896]{1,0:T(8,128)(2,1)S(1)}, bf16[96,896]{1,0:T(8,128)(2,1)S(1)}, u32[]{:S(2)}, u32[]{:S(2)}) collective-permute-start(bf16[96,896]{1,0:T(8,128)(2,1)S(1)} %slice.103), channel_id=1, source_target_pairs={{0,2},{1,3},{2,0},{3,1},{4,6},{5,7},{6,4},{7,5},{8,10},{9,11},{10,... | collective-permute-start | bytes 516104 | tf_op jit(solution)/shard_map/ppermute | solution.py:22
  80.0 0.1 add_convert_fusion.3
  80.2 0.6 collective-permute-start.21
  80.7 2.6 %collective-permute-done.36 = bf16[96,896]{1,0:T(8,128)(2,1)S(1)} collective-permute-done((bf16[96,896]{1,0:T(8,128)(2,1)S(1)}, bf16[96,896]{1,0:T(8,128)(2,1)S(1)}, u32[]{:S(2)}, u32[]{:S(2)}) %collective-permute-start.36) | collective-permute-done | bytes 172064 | tf_op jit(solution)/shard_map/ppermute | solution.py:22
  83.4 0.6 fusion
  84.0 0.2 collective-permute-start.37
  84.2 3.2 %collective-permute-start.38 = (bf16[24,896]{1,0:T(8,128)(2,1)S(1)}, bf16[24,896]{1,0:T(8,128)(2,1)S(1)}, u32[]{:S(2)}, u32[]{:S(2)}) collective-permute-start(bf16[24,896]{1,0:T(8,128)(2,1)S(1)} %get-tuple-element.36), channel_id=1, source_target_pairs={{0,8},{1,9},{2,10},{3,11},{4,12},{5,13},{6,14},{7,15},{8,0},{9,1},... | collective-permute-start | bytes 129032 | tf_op jit(solution)/shard_map/ppermute | solution.py:22
  87.4 2.4 %collective-permute-start.39 = (bf16[24,896]{1,0:T(8,128)(2,1)S(1)}, bf16[24,896]{1,0:T(8,128)(2,1)S(1)}, u32[]{:S(2)}, u32[]{:S(2)}) collective-permute-start(bf16[24,896]{1,0:T(8,128)(2,1)S(1)} %get-tuple-element.35), channel_id=1, source_target_pairs={{0,12},{1,13},{2,14},{3,15},{4,8},{5,9},{6,10},{7,11},{8,4},{9,5},... | collective-permute-start | bytes 129032 | tf_op jit(solution)/shard_map/ppermute | solution.py:22
  89.9 0.6 fusion.1
  90.5 0.2 collective-permute-done.26
  90.7 0.2 collective-permute-start.32
  91.0 3.0 %collective-permute-done.21 = bf16[96,896]{1,0:T(8,128)(2,1)S(1)} collective-permute-done((bf16[96,896]{1,0:T(8,128)(2,1)S(1)}, bf16[96,896]{1,0:T(8,128)(2,1)S(1)}, u32[]{:S(2)}, u32[]{:S(2)}) %collective-permute-start.21) | collective-permute-done | bytes 172064 | tf_op jit(solution)/shard_map/ppermute | solution.py:22
  93.9 1.2 %collective-permute-start.33 = (bf16[24,896]{1,0:T(8,128)(2,1)S(1)}, bf16[24,896]{1,0:T(8,128)(2,1)S(1)}, u32[]{:S(2)}, u32[]{:S(2)}) collective-permute-start(bf16[24,896]{1,0:T(8,128)(2,1)S(1)} %get-tuple-element.40), channel_id=1, source_target_pairs={{0,8},{1,9},{2,10},{3,11},{4,12},{5,13},{6,14},{7,15},{8,0},{9,1},... | collective-permute-start | bytes 129032 | tf_op jit(solution)/shard_map/ppermute | solution.py:22
  95.2 0.6 fusion.2
  95.8 1.7 %collective-permute-start.34 = (bf16[24,896]{1,0:T(8,128)(2,1)S(1)}, bf16[24,896]{1,0:T(8,128)(2,1)S(1)}, u32[]{:S(2)}, u32[]{:S(2)}) collective-permute-start(bf16[24,896]{1,0:T(8,128)(2,1)S(1)} %get-tuple-element.39), channel_id=1, source_target_pairs={{0,12},{1,13},{2,14},{3,15},{4,8},{5,9},{6,10},{7,11},{8,4},{9,5},... | collective-permute-start | bytes 129032 | tf_op jit(solution)/shard_map/ppermute | solution.py:22
  97.4 0.7 collective-permute-start.27
  98.1 0.6 fusion.3
  98.7 2.1 %collective-permute-start.28 = (bf16[24,896]{1,0:T(8,128)(2,1)S(1)}, bf16[24,896]{1,0:T(8,128)(2,1)S(1)}, u32[]{:S(2)}, u32[]{:S(2)}) collective-permute-start(bf16[24,896]{1,0:T(8,128)(2,1)S(1)} %get-tuple-element.44), channel_id=1, source_target_pairs={{0,8},{1,9},{2,10},{3,11},{4,12},{5,13},{6,14},{7,15},{8,0},{9,1},... | collective-permute-start | bytes 129032 | tf_op jit(solution)/shard_map/ppermute | solution.py:22
  100.8 1.7 %collective-permute-start.29 = (bf16[24,896]{1,0:T(8,128)(2,1)S(1)}, bf16[24,896]{1,0:T(8,128)(2,1)S(1)}, u32[]{:S(2)}, u32[]{:S(2)}) collective-permute-start(bf16[24,896]{1,0:T(8,128)(2,1)S(1)} %get-tuple-element.43), channel_id=1, source_target_pairs={{0,12},{1,13},{2,14},{3,15},{4,8},{5,9},{6,10},{7,11},{8,4},{9,5},... | collective-permute-start | bytes 129032 | tf_op jit(solution)/shard_map/ppermute | solution.py:22
  102.5 2.7 %collective-permute-start.23 = (bf16[24,896]{1,0:T(8,128)(2,1)S(1)}, bf16[24,896]{1,0:T(8,128)(2,1)S(1)}, u32[]{:S(2)}, u32[]{:S(2)}) collective-permute-start(bf16[24,896]{1,0:T(8,128)(2,1)S(1)} %get-tuple-element.48), channel_id=1, source_target_pairs={{0,8},{1,9},{2,10},{3,11},{4,12},{5,13},{6,14},{7,15},{8,0},{9,1},... | collective-permute-start | bytes 129032 | tf_op jit(solution)/shard_map/ppermute | solution.py:22
  105.2 1.7 %collective-permute-start.24 = (bf16[24,896]{1,0:T(8,128)(2,1)S(1)}, bf16[24,896]{1,0:T(8,128)(2,1)S(1)}, u32[]{:S(2)}, u32[]{:S(2)}) collective-permute-start(bf16[24,896]{1,0:T(8,128)(2,1)S(1)} %get-tuple-element.47), channel_id=1, source_target_pairs={{0,12},{1,13},{2,14},{3,15},{4,8},{5,9},{6,10},{7,11},{8,4},{9,5},... | collective-permute-start | bytes 129032 | tf_op jit(solution)/shard_map/ppermute | solution.py:22
  107.0 1.0 collective-permute-done.23.refs_2_
  108.0 3.1 %collective-permute-done.24.refs_3_ = bf16[24,896]{1,0:T(8,128)(2,1)S(1)} collective-permute-done((bf16[24,896]{1,0:T(8,128)(2,1)S(1)}, bf16[24,896]{1,0:T(8,128)(2,1)S(1)}, u32[]{:S(2)}, u32[]{:S(2)}) %collective-permute-start.24) | collective-permute-done | bytes 43040 | tf_op jit(solution)/shard_map/ppermute | solution.py:22
  111.1 0.5 copy-done.11
  111.7 1.9 %shard_map.72 = bf16[12,7168]{1,0:T(8,128)(2,1)} custom-call(bf16[24,896]{1,0:T(8,128)(2,1)} %get-tuple-element.50.refs_0_, bf16[24,896]{1,0:T(8,128)(2,1)} %copy-done.9, bf16[24,896]{1,0:T(8,128)(2,1)} %copy-done.10, bf16[24,896]{1,0:T(8,128)(2,1)} %copy-done.11, bf16[24,896]{1,0:T(8,128)(2,1)} %get-tuple-element.46.refs_4_, bf16[24,896]{1,0:T(8,128)(2,1)} %copy-done.6, ...), custom_call_target="tpu_custom_call" | custom-call | tf_op jit(solution)/shard_map/pallas_call | solution.py:292
  (86 shorter events, 1.0 us)
Async XLA Ops:
  4.4 27.4 %collective-permute-start.15 = (bf16[24,1024]{1,0:T(8,128)(2,1)}, bf16[24,1024]{1,0:T(8,128)(2,1)S(1)}, u32[]{:S(2)}, u32[]{:S(2)}) collective-permute-start(bf16[24,1024]{1,0:T(8,128)(2,1)} %get-tuple-element.23), channel_id=1, source_target_pairs={{0,4},{1,5},{2,6},{3,7},{4,0},{5,1},{6,2},{7,3},{8,12},{9,13},{10,... | collective-permute-start | bytes 147464 | tf_op jit(solution)/shard_map/ppermute | solution.py:22
  7.4 25.4 %collective-permute-start.16 = (bf16[24,1024]{1,0:T(8,128)(2,1)}, bf16[24,1024]{1,0:T(8,128)(2,1)S(1)}, u32[]{:S(2)}, u32[]{:S(2)}) collective-permute-start(bf16[24,1024]{1,0:T(8,128)(2,1)} %get-tuple-element.23), channel_id=1, source_target_pairs={{0,8},{1,9},{2,10},{3,11},{4,12},{5,13},{6,14},{7,15},{8,0},{9,1},... | collective-permute-start | bytes 147464 | tf_op jit(solution)/shard_map/ppermute | solution.py:22
  10.0 24.4 %collective-permute-start.17 = (bf16[24,1024]{1,0:T(8,128)(2,1)}, bf16[24,1024]{1,0:T(8,128)(2,1)S(1)}, u32[]{:S(2)}, u32[]{:S(2)}) collective-permute-start(bf16[24,1024]{1,0:T(8,128)(2,1)} %get-tuple-element.23), channel_id=1, source_target_pairs={{0,12},{1,13},{2,14},{3,15},{4,8},{5,9},{6,10},{7,11},{8,4},{9,5},... | collective-permute-start | bytes 147464 | tf_op jit(solution)/shard_map/ppermute | solution.py:22
  10.0 6.8 %collective-permute-start.10 = (bf16[24,896]{1,0:T(8,128)(2,1)}, bf16[24,896]{1,0:T(8,128)(2,1)S(1)}, u32[]{:S(2)}, u32[]{:S(2)}) collective-permute-start(bf16[24,896]{1,0:T(8,128)(2,1)} %get-tuple-element.22), channel_id=1, source_target_pairs={{0,4},{1,5},{2,6},{3,7},{4,0},{5,1},{6,2},{7,3},{8,12},{9,13},{10,... | collective-permute-start | bytes 129032 | tf_op jit(solution)/shard_map/ppermute | solution.py:22
  10.9 7.2 %collective-permute-start.11 = (bf16[24,896]{1,0:T(8,128)(2,1)}, bf16[24,896]{1,0:T(8,128)(2,1)S(1)}, u32[]{:S(2)}, u32[]{:S(2)}) collective-permute-start(bf16[24,896]{1,0:T(8,128)(2,1)} %get-tuple-element.22), channel_id=1, source_target_pairs={{0,8},{1,9},{2,10},{3,11},{4,12},{5,13},{6,14},{7,15},{8,0},{9,1},... | collective-permute-start | bytes 129032 | tf_op jit(solution)/shard_map/ppermute | solution.py:22
  16.8 6.3 %collective-permute-start.12 = (bf16[24,896]{1,0:T(8,128)(2,1)}, bf16[24,896]{1,0:T(8,128)(2,1)S(1)}, u32[]{:S(2)}, u32[]{:S(2)}) collective-permute-start(bf16[24,896]{1,0:T(8,128)(2,1)} %get-tuple-element.22), channel_id=1, source_target_pairs={{0,12},{1,13},{2,14},{3,15},{4,8},{5,9},{6,10},{7,11},{8,4},{9,5},... | collective-permute-start | bytes 129032 | tf_op jit(solution)/shard_map/ppermute | solution.py:22
  18.2 5.0 %collective-permute-start.5 = (bf16[24,896]{1,0:T(8,128)(2,1)}, bf16[24,896]{1,0:T(8,128)(2,1)S(1)}, u32[]{:S(2)}, u32[]{:S(2)}) collective-permute-start(bf16[24,896]{1,0:T(8,128)(2,1)} %get-tuple-element.21), channel_id=1, source_target_pairs={{0,4},{1,5},{2,6},{3,7},{4,0},{5,1},{6,2},{7,3},{8,12},{9,13},{10,... | collective-permute-start | bytes 129032 | tf_op jit(solution)/shard_map/ppermute | solution.py:22
  23.1 5.1 %collective-permute-start.6 = (bf16[24,896]{1,0:T(8,128)(2,1)}, bf16[24,896]{1,0:T(8,128)(2,1)S(1)}, u32[]{:S(2)}, u32[]{:S(2)}) collective-permute-start(bf16[24,896]{1,0:T(8,128)(2,1)} %get-tuple-element.21), channel_id=1, source_target_pairs={{0,8},{1,9},{2,10},{3,11},{4,12},{5,13},{6,14},{7,15},{8,0},{9,1},... | collective-permute-start | bytes 129032 | tf_op jit(solution)/shard_map/ppermute | solution.py:22
  23.2 6.3 %collective-permute-start.7 = (bf16[24,896]{1,0:T(8,128)(2,1)}, bf16[24,896]{1,0:T(8,128)(2,1)S(1)}, u32[]{:S(2)}, u32[]{:S(2)}) collective-permute-start(bf16[24,896]{1,0:T(8,128)(2,1)} %get-tuple-element.21), channel_id=1, source_target_pairs={{0,12},{1,13},{2,14},{3,15},{4,8},{5,9},{6,10},{7,11},{8,4},{9,5},... | collective-permute-start | bytes 129032 | tf_op jit(solution)/shard_map/ppermute | solution.py:22
  28.3 6.8 %collective-permute-start = (bf16[24,896]{1,0:T(8,128)(2,1)}, bf16[24,896]{1,0:T(8,128)(2,1)S(1)}, u32[]{:S(2)}, u32[]{:S(2)}) collective-permute-start(bf16[24,896]{1,0:T(8,128)(2,1)} %get-tuple-element.20), channel_id=1, source_target_pairs={{0,4},{1,5},{2,6},{3,7},{4,0},{5,1},{6,2},{7,3},{8,12},{9,13},{10,... | collective-permute-start | bytes 129032 | tf_op jit(solution)/shard_map/ppermute | solution.py:22
  29.5 7.2 %collective-permute-start.1 = (bf16[24,896]{1,0:T(8,128)(2,1)}, bf16[24,896]{1,0:T(8,128)(2,1)S(1)}, u32[]{:S(2)}, u32[]{:S(2)}) collective-permute-start(bf16[24,896]{1,0:T(8,128)(2,1)} %get-tuple-element.20), channel_id=1, source_target_pairs={{0,8},{1,9},{2,10},{3,11},{4,12},{5,13},{6,14},{7,15},{8,0},{9,1},... | collective-permute-start | bytes 129032 | tf_op jit(solution)/shard_map/ppermute | solution.py:22
  31.8 10.6 %collective-permute-start.2 = (bf16[24,896]{1,0:T(8,128)(2,1)}, bf16[24,896]{1,0:T(8,128)(2,1)S(1)}, u32[]{:S(2)}, u32[]{:S(2)}) collective-permute-start(bf16[24,896]{1,0:T(8,128)(2,1)} %get-tuple-element.20), channel_id=1, source_target_pairs={{0,12},{1,13},{2,14},{3,15},{4,8},{5,9},{6,10},{7,11},{8,4},{9,5},... | collective-permute-start | bytes 129032 | tf_op jit(solution)/shard_map/ppermute | solution.py:22
  32.9 11.1 %collective-permute-start.13 = (bf16[96,896]{1,0:T(8,128)(2,1)S(1)}, bf16[96,896]{1,0:T(8,128)(2,1)S(1)}, u32[]{:S(2)}, u32[]{:S(2)}) collective-permute-start(bf16[96,896]{1,0:T(8,128)(2,1)S(1)} %get-tuple-element.60.refs_0_), channel_id=1, source_target_pairs={{0,2},{1,3},{2,0},{3,1},{4,6},{5,7},{6,4},{7,5},{8,10},{9,11},{10,... | collective-permute-start | bytes 516104 | tf_op jit(solution)/shard_map/ppermute | solution.py:22
  34.5 9.8 %collective-permute-start.8 = (bf16[96,896]{1,0:T(8,128)(2,1)S(1)}, bf16[96,896]{1,0:T(8,128)(2,1)S(1)}, u32[]{:S(2)}, u32[]{:S(2)}) collective-permute-start(bf16[96,896]{1,0:T(8,128)(2,1)S(1)} %get-tuple-element.68.refs_0_), channel_id=1, source_target_pairs={{0,2},{1,3},{2,0},{3,1},{4,6},{5,7},{6,4},{7,5},{8,10},{9,11},{10,... | collective-permute-start | bytes 516104 | tf_op jit(solution)/shard_map/ppermute | solution.py:22
  35.0 7.2 %collective-permute-start.18 = (bf16[96,1024]{1,0:T(8,128)(2,1)S(1)}, bf16[96,1024]{1,0:T(8,128)(2,1)S(1)}, u32[]{:S(2)}, u32[]{:S(2)}) collective-permute-start(bf16[96,1024]{1,0:T(8,128)(2,1)S(1)} %get-tuple-element.52.refs_0_), channel_id=1, source_target_pairs={{0,2},{1,3},{2,0},{3,1},{4,6},{5,7},{6,4},{7,5},{8,10},{9,11},{10,... | collective-permute-start | bytes 589832 | tf_op jit(solution)/shard_map/ppermute | solution.py:22
  42.3 7.0 %collective-permute-start.19 = (bf16[192,1024]{1,0:T(8,128)(2,1)S(1)}, bf16[192,1024]{1,0:T(8,128)(2,1)S(1)}, u32[]{:S(2)}, u32[]{:S(2)}) collective-permute-start(bf16[192,1024]{1,0:T(8,128)(2,1)S(1)} %constant_dynamic-update-slice_fusion.31), channel_id=1, source_target_pairs={{0,1},{1,0},{2,3},{3,2},{4,5},{5,4},{6,7},{7,6},{8,9},{9,8},{10,11... | collective-permute-start | bytes 1179656 | tf_op jit(solution)/shard_map/ppermute | solution.py:22
  42.4 6.8 %collective-permute-start.3 = (bf16[96,896]{1,0:T(8,128)(2,1)S(1)}, bf16[96,896]{1,0:T(8,128)(2,1)S(1)}, u32[]{:S(2)}, u32[]{:S(2)}) collective-permute-start(bf16[96,896]{1,0:T(8,128)(2,1)S(1)} %get-tuple-element.76.refs_0_), channel_id=1, source_target_pairs={{0,2},{1,3},{2,0},{3,1},{4,6},{5,7},{6,4},{7,5},{8,10},{9,11},{10,... | collective-permute-start | bytes 516104 | tf_op jit(solution)/shard_map/ppermute | solution.py:22
  44.0 9.1 %collective-permute-start.14 = (bf16[192,896]{1,0:T(8,128)(2,1)S(1)}, bf16[192,896]{1,0:T(8,128)(2,1)S(1)}, u32[]{:S(2)}, u32[]{:S(2)}) collective-permute-start(bf16[192,896]{1,0:T(8,128)(2,1)S(1)} %constant_dynamic-update-slice_fusion.22), channel_id=1, source_target_pairs={{0,1},{1,0},{2,3},{3,2},{4,5},{5,4},{6,7},{7,6},{8,9},{9,8},{10,11... | collective-permute-start | bytes 1032200 | tf_op jit(solution)/shard_map/ppermute | solution.py:22
  44.3 12.5 %collective-permute-start.9 = (bf16[192,896]{1,0:T(8,128)(2,1)S(1)}, bf16[192,896]{1,0:T(8,128)(2,1)S(1)}, u32[]{:S(2)}, u32[]{:S(2)}) collective-permute-start(bf16[192,896]{1,0:T(8,128)(2,1)S(1)} %constant_dynamic-update-slice_fusion.13), channel_id=1, source_target_pairs={{0,1},{1,0},{2,3},{3,2},{4,5},{5,4},{6,7},{7,6},{8,9},{9,8},{10,11... | collective-permute-start | bytes 1032200 | tf_op jit(solution)/shard_map/ppermute | solution.py:22
  49.3 11.3 %collective-permute-start.4 = (bf16[192,896]{1,0:T(8,128)(2,1)S(1)}, bf16[192,896]{1,0:T(8,128)(2,1)S(1)}, u32[]{:S(2)}, u32[]{:S(2)}) collective-permute-start(bf16[192,896]{1,0:T(8,128)(2,1)S(1)} %constant_dynamic-update-slice_fusion.4), channel_id=1, source_target_pairs={{0,1},{1,0},{2,3},{3,2},{4,5},{5,4},{6,7},{7,6},{8,9},{9,8},{10,11... | collective-permute-start | bytes 1032200 | tf_op jit(solution)/shard_map/ppermute | solution.py:22
  68.8 7.2 %collective-permute-start.35 = (bf16[192,896]{1,0:T(8,128)(2,1)S(1)}, bf16[192,896]{1,0:T(8,128)(2,1)S(1)}, u32[]{:S(2)}, u32[]{:S(2)}) collective-permute-start(bf16[192,896]{1,0:T(8,128)(2,1)S(1)} %get-tuple-element.34), channel_id=1, source_target_pairs={{0,1},{1,0},{2,3},{3,2},{4,5},{5,4},{6,7},{7,6},{8,9},{9,8},{10,11... | collective-permute-start | bytes 1032200 | tf_op jit(solution)/shard_map/ppermute | solution.py:22
  72.3 5.4 %collective-permute-start.30 = (bf16[192,896]{1,0:T(8,128)(2,1)S(1)}, bf16[192,896]{1,0:T(8,128)(2,1)S(1)}, u32[]{:S(2)}, u32[]{:S(2)}) collective-permute-start(bf16[192,896]{1,0:T(8,128)(2,1)S(1)} %get-tuple-element.32), channel_id=1, source_target_pairs={{0,1},{1,0},{2,3},{3,2},{4,5},{5,4},{6,7},{7,6},{8,9},{9,8},{10,11... | collective-permute-start | bytes 1032200 | tf_op jit(solution)/shard_map/ppermute | solution.py:22
  75.3 3.0 %collective-permute-start.25 = (bf16[192,896]{1,0:T(8,128)(2,1)S(1)}, bf16[192,896]{1,0:T(8,128)(2,1)S(1)}, u32[]{:S(2)}, u32[]{:S(2)}) collective-permute-start(bf16[192,896]{1,0:T(8,128)(2,1)S(1)} %get-tuple-element.30), channel_id=1, source_target_pairs={{0,1},{1,0},{2,3},{3,2},{4,5},{5,4},{6,7},{7,6},{8,9},{9,8},{10,11... | collective-permute-start | bytes 1032200 | tf_op jit(solution)/shard_map/ppermute | solution.py:22
  75.9 4.2 %collective-permute-start.20 = (bf16[192,896]{1,0:T(8,128)(2,1)S(1)}, bf16[192,896]{1,0:T(8,128)(2,1)S(1)}, u32[]{:S(2)}, u32[]{:S(2)}) collective-permute-start(bf16[192,896]{1,0:T(8,128)(2,1)S(1)} %get-tuple-element.27), channel_id=1, source_target_pairs={{0,1},{1,0},{2,3},{3,2},{4,5},{5,4},{6,7},{7,6},{8,9},{9,8},{10,11... | collective-permute-start | bytes 1032200 | tf_op jit(solution)/shard_map/ppermute | solution.py:22
  76.1 7.2 %collective-permute-start.36 = (bf16[96,896]{1,0:T(8,128)(2,1)S(1)}, bf16[96,896]{1,0:T(8,128)(2,1)S(1)}, u32[]{:S(2)}, u32[]{:S(2)}) collective-permute-start(bf16[96,896]{1,0:T(8,128)(2,1)S(1)} %slice.115), channel_id=1, source_target_pairs={{0,2},{1,3},{2,0},{3,1},{4,6},{5,7},{6,4},{7,5},{8,10},{9,11},{10,... | collective-permute-start | bytes 516104 | tf_op jit(solution)/shard_map/ppermute | solution.py:22
  77.8 9.6 %collective-permute-start.31 = (bf16[96,896]{1,0:T(8,128)(2,1)S(1)}, bf16[96,896]{1,0:T(8,128)(2,1)S(1)}, u32[]{:S(2)}, u32[]{:S(2)}) collective-permute-start(bf16[96,896]{1,0:T(8,128)(2,1)S(1)} %slice.109), channel_id=1, source_target_pairs={{0,2},{1,3},{2,0},{3,1},{4,6},{5,7},{6,4},{7,5},{8,10},{9,11},{10,... | collective-permute-start | bytes 516104 | tf_op jit(solution)/shard_map/ppermute | solution.py:22
  78.5 12.2 %collective-permute-start.26 = (bf16[96,896]{1,0:T(8,128)(2,1)S(1)}, bf16[96,896]{1,0:T(8,128)(2,1)S(1)}, u32[]{:S(2)}, u32[]{:S(2)}) collective-permute-start(bf16[96,896]{1,0:T(8,128)(2,1)S(1)} %slice.103), channel_id=1, source_target_pairs={{0,2},{1,3},{2,0},{3,1},{4,6},{5,7},{6,4},{7,5},{8,10},{9,11},{10,... | collective-permute-start | bytes 516104 | tf_op jit(solution)/shard_map/ppermute | solution.py:22
  80.2 13.8 %collective-permute-start.21 = (bf16[96,896]{1,0:T(8,128)(2,1)S(1)}, bf16[96,896]{1,0:T(8,128)(2,1)S(1)}, u32[]{:S(2)}, u32[]{:S(2)}) collective-permute-start(bf16[96,896]{1,0:T(8,128)(2,1)S(1)} %slice.97), channel_id=1, source_target_pairs={{0,2},{1,3},{2,0},{3,1},{4,6},{5,7},{6,4},{7,5},{8,10},{9,11},{10,... | collective-permute-start | bytes 516104 | tf_op jit(solution)/shard_map/ppermute | solution.py:22
  84.0 11.8 %collective-permute-start.37 = (bf16[24,896]{1,0:T(8,128)(2,1)S(1)}, bf16[24,896]{1,0:T(8,128)(2,1)S(1)}, u32[]{:S(2)}, u32[]{:S(2)}) collective-permute-start(bf16[24,896]{1,0:T(8,128)(2,1)S(1)} %get-tuple-element.37), channel_id=1, source_target_pairs={{0,4},{1,5},{2,6},{3,7},{4,0},{5,1},{6,2},{7,3},{8,12},{9,13},{10,... | collective-permute-start | bytes 129032 | tf_op jit(solution)/shard_map/ppermute | solution.py:22
  84.2 13.2 %collective-permute-start.38 = (bf16[24,896]{1,0:T(8,128)(2,1)S(1)}, bf16[24,896]{1,0:T(8,128)(2,1)S(1)}, u32[]{:S(2)}, u32[]{:S(2)}) collective-permute-start(bf16[24,896]{1,0:T(8,128)(2,1)S(1)} %get-tuple-element.36), channel_id=1, source_target_pairs={{0,8},{1,9},{2,10},{3,11},{4,12},{5,13},{6,14},{7,15},{8,0},{9,1},... | collective-permute-start | bytes 129032 | tf_op jit(solution)/shard_map/ppermute | solution.py:22
  87.4 11.3 %collective-permute-start.39 = (bf16[24,896]{1,0:T(8,128)(2,1)S(1)}, bf16[24,896]{1,0:T(8,128)(2,1)S(1)}, u32[]{:S(2)}, u32[]{:S(2)}) collective-permute-start(bf16[24,896]{1,0:T(8,128)(2,1)S(1)} %get-tuple-element.35), channel_id=1, source_target_pairs={{0,12},{1,13},{2,14},{3,15},{4,8},{5,9},{6,10},{7,11},{8,4},{9,5},... | collective-permute-start | bytes 129032 | tf_op jit(solution)/shard_map/ppermute | solution.py:22
  90.7 10.1 %collective-permute-start.32 = (bf16[24,896]{1,0:T(8,128)(2,1)S(1)}, bf16[24,896]{1,0:T(8,128)(2,1)S(1)}, u32[]{:S(2)}, u32[]{:S(2)}) collective-permute-start(bf16[24,896]{1,0:T(8,128)(2,1)S(1)} %get-tuple-element.41), channel_id=1, source_target_pairs={{0,4},{1,5},{2,6},{3,7},{4,0},{5,1},{6,2},{7,3},{8,12},{9,13},{10,... | collective-permute-start | bytes 129032 | tf_op jit(solution)/shard_map/ppermute | solution.py:22
  93.9 8.6 %collective-permute-start.33 = (bf16[24,896]{1,0:T(8,128)(2,1)S(1)}, bf16[24,896]{1,0:T(8,128)(2,1)S(1)}, u32[]{:S(2)}, u32[]{:S(2)}) collective-permute-start(bf16[24,896]{1,0:T(8,128)(2,1)S(1)} %get-tuple-element.40), channel_id=1, source_target_pairs={{0,8},{1,9},{2,10},{3,11},{4,12},{5,13},{6,14},{7,15},{8,0},{9,1},... | collective-permute-start | bytes 129032 | tf_op jit(solution)/shard_map/ppermute | solution.py:22
  95.8 15.3 %copy-start = (bf16[24,896]{1,0:T(8,128)(2,1)}, bf16[24,896]{1,0:T(8,128)(2,1)S(1)}, u32[]{:S(2)}) copy-start(bf16[24,896]{1,0:T(8,128)(2,1)S(1)} %collective-permute-done.37.refs_13_) | copy-start | bytes 129028
  95.8 6.7 %collective-permute-start.34 = (bf16[24,896]{1,0:T(8,128)(2,1)S(1)}, bf16[24,896]{1,0:T(8,128)(2,1)S(1)}, u32[]{:S(2)}, u32[]{:S(2)}) collective-permute-start(bf16[24,896]{1,0:T(8,128)(2,1)S(1)} %get-tuple-element.39), channel_id=1, source_target_pairs={{0,12},{1,13},{2,14},{3,15},{4,8},{5,9},{6,10},{7,11},{8,4},{9,5},... | collective-permute-start | bytes 129032 | tf_op jit(solution)/shard_map/ppermute | solution.py:22
  97.4 13.6 %copy-start.1 = (bf16[24,896]{1,0:T(8,128)(2,1)}, bf16[24,896]{1,0:T(8,128)(2,1)S(1)}, u32[]{:S(2)}) copy-start(bf16[24,896]{1,0:T(8,128)(2,1)S(1)} %collective-permute-done.38.refs_14_) | copy-start | bytes 129028
  97.4 7.8 %collective-permute-start.27 = (bf16[24,896]{1,0:T(8,128)(2,1)S(1)}, bf16[24,896]{1,0:T(8,128)(2,1)S(1)}, u32[]{:S(2)}, u32[]{:S(2)}) collective-permute-start(bf16[24,896]{1,0:T(8,128)(2,1)S(1)} %get-tuple-element.45), channel_id=1, source_target_pairs={{0,4},{1,5},{2,6},{3,7},{4,0},{5,1},{6,2},{7,3},{8,12},{9,13},{10,... | collective-permute-start | bytes 129032 | tf_op jit(solution)/shard_map/ppermute | solution.py:22
  98.7 12.3 %copy-start.2 = (bf16[24,896]{1,0:T(8,128)(2,1)}, bf16[24,896]{1,0:T(8,128)(2,1)S(1)}, u32[]{:S(2)}) copy-start(bf16[24,896]{1,0:T(8,128)(2,1)S(1)} %collective-permute-done.39.refs_15_) | copy-start | bytes 129028
  98.7 8.2 %collective-permute-start.28 = (bf16[24,896]{1,0:T(8,128)(2,1)S(1)}, bf16[24,896]{1,0:T(8,128)(2,1)S(1)}, u32[]{:S(2)}, u32[]{:S(2)}) collective-permute-start(bf16[24,896]{1,0:T(8,128)(2,1)S(1)} %get-tuple-element.44), channel_id=1, source_target_pairs={{0,8},{1,9},{2,10},{3,11},{4,12},{5,13},{6,14},{7,15},{8,0},{9,1},... | collective-permute-start | bytes 129032 | tf_op jit(solution)/shard_map/ppermute | solution.py:22
  100.8 10.2 %copy-start.3 = (bf16[24,896]{1,0:T(8,128)(2,1)}, bf16[24,896]{1,0:T(8,128)(2,1)S(1)}, u32[]{:S(2)}) copy-start(bf16[24,896]{1,0:T(8,128)(2,1)S(1)} %collective-permute-done.32.refs_9_) | copy-start | bytes 129028
  100.8 6.1 %collective-permute-start.29 = (bf16[24,896]{1,0:T(8,128)(2,1)S(1)}, bf16[24,896]{1,0:T(8,128)(2,1)S(1)}, u32[]{:S(2)}, u32[]{:S(2)}) collective-permute-start(bf16[24,896]{1,0:T(8,128)(2,1)S(1)} %get-tuple-element.43), channel_id=1, source_target_pairs={{0,12},{1,13},{2,14},{3,15},{4,8},{5,9},{6,10},{7,11},{8,4},{9,5},... | collective-permute-start | bytes 129032 | tf_op jit(solution)/shard_map/ppermute | solution.py:22
  102.5 8.6 %copy-start.4 = (bf16[24,896]{1,0:T(8,128)(2,1)}, bf16[24,896]{1,0:T(8,128)(2,1)S(1)}, u32[]{:S(2)}) copy-start(bf16[24,896]{1,0:T(8,128)(2,1)S(1)} %collective-permute-done.33.refs_10_) | copy-start | bytes 129028
  102.5 4.5 %collective-permute-start.22 = (bf16[24,896]{1,0:T(8,128)(2,1)S(1)}, bf16[24,896]{1,0:T(8,128)(2,1)S(1)}, u32[]{:S(2)}, u32[]{:S(2)}) collective-permute-start(bf16[24,896]{1,0:T(8,128)(2,1)S(1)} %get-tuple-element.49), channel_id=1, source_target_pairs={{0,4},{1,5},{2,6},{3,7},{4,0},{5,1},{6,2},{7,3},{8,12},{9,13},{10,... | collective-permute-start | bytes 129032 | tf_op jit(solution)/shard_map/ppermute | solution.py:22
  102.5 8.6 %copy-start.5 = (bf16[24,896]{1,0:T(8,128)(2,1)}, bf16[24,896]{1,0:T(8,128)(2,1)S(1)}, u32[]{:S(2)}) copy-start(bf16[24,896]{1,0:T(8,128)(2,1)S(1)} %collective-permute-done.34.refs_11_) | copy-start | bytes 129028
  102.5 5.5 %collective-permute-start.23 = (bf16[24,896]{1,0:T(8,128)(2,1)S(1)}, bf16[24,896]{1,0:T(8,128)(2,1)S(1)}, u32[]{:S(2)}, u32[]{:S(2)}) collective-permute-start(bf16[24,896]{1,0:T(8,128)(2,1)S(1)} %get-tuple-element.48), channel_id=1, source_target_pairs={{0,8},{1,9},{2,10},{3,11},{4,12},{5,13},{6,14},{7,15},{8,0},{9,1},... | collective-permute-start | bytes 129032 | tf_op jit(solution)/shard_map/ppermute | solution.py:22
  105.2 5.9 %copy-start.6 = (bf16[24,896]{1,0:T(8,128)(2,1)}, bf16[24,896]{1,0:T(8,128)(2,1)S(1)}, u32[]{:S(2)}) copy-start(bf16[24,896]{1,0:T(8,128)(2,1)S(1)} %collective-permute-done.27.refs_5_) | copy-start | bytes 129028
  105.2 5.8 %collective-permute-start.24 = (bf16[24,896]{1,0:T(8,128)(2,1)S(1)}, bf16[24,896]{1,0:T(8,128)(2,1)S(1)}, u32[]{:S(2)}, u32[]{:S(2)}) collective-permute-start(bf16[24,896]{1,0:T(8,128)(2,1)S(1)} %get-tuple-element.47), channel_id=1, source_target_pairs={{0,12},{1,13},{2,14},{3,15},{4,8},{5,9},{6,10},{7,11},{8,4},{9,5},... | collective-permute-start | bytes 129032 | tf_op jit(solution)/shard_map/ppermute | solution.py:22
  106.9 4.2 %copy-start.7 = (bf16[24,896]{1,0:T(8,128)(2,1)}, bf16[24,896]{1,0:T(8,128)(2,1)S(1)}, u32[]{:S(2)}) copy-start(bf16[24,896]{1,0:T(8,128)(2,1)S(1)} %collective-permute-done.28.refs_6_) | copy-start | bytes 129028
  106.9 4.2 %copy-start.8 = (bf16[24,896]{1,0:T(8,128)(2,1)}, bf16[24,896]{1,0:T(8,128)(2,1)S(1)}, u32[]{:S(2)}) copy-start(bf16[24,896]{1,0:T(8,128)(2,1)S(1)} %collective-permute-done.29.refs_7_) | copy-start | bytes 129028
  107.0 4.2 %copy-start.9 = (bf16[24,896]{1,0:T(8,128)(2,1)}, bf16[24,896]{1,0:T(8,128)(2,1)S(1)}, u32[]{:S(2)}) copy-start(bf16[24,896]{1,0:T(8,128)(2,1)S(1)} %collective-permute-done.22.refs_1_) | copy-start | bytes 129028
  108.0 3.1 %copy-start.10 = (bf16[24,896]{1,0:T(8,128)(2,1)}, bf16[24,896]{1,0:T(8,128)(2,1)S(1)}, u32[]{:S(2)}) copy-start(bf16[24,896]{1,0:T(8,128)(2,1)S(1)} %collective-permute-done.23.refs_2_) | copy-start | bytes 129028
  111.1 0.6 copy-start.11

commit v2 on v1

v2 whole, which is shorter than its diff:
```python
import functools

import jax
import jax.numpy as jnp
from jax import lax
from jax.experimental import pallas as pl
from jax.experimental.pallas import tpu as pltpu
from jax.sharding import PartitionSpec as P

GROUPS = 8
EXP_G = 2
LANES = 128
TILE = 8
MIB = 1 << 20
IN_SHARES = (1, 1)
OUT_SHARES = (1, 1)
bf16 = jnp.bfloat16
f32 = jnp.float32


def swap(block, bits, count):
    return lax.ppermute(block, "wide", [(i, i ^ bits) for i in range(count)])


def half_roll(block):
    return pltpu.roll(block, TILE // 2, 0)


def low_half(shape):
    return lax.broadcasted_iota(jnp.int32, shape, 0) < TILE // 2


def unpack_pair(u, v):
    full = (u.shape[0] - TILE) // 2
    u_rest, v_rest = u[2 * full :], v[2 * full :]
    low = low_half(u_rest.shape)
    a = [u[:full], v[:full], jnp.where(low, u_rest, half_roll(v_rest))]
    b = [u[full : 2 * full], v[full : 2 * full], jnp.where(low, half_roll(u_rest), v_rest)]
    return a, b


def pack_pair(a, b):
    full = (a.shape[0] - TILE) // 2
    a_rest, b_rest = a[2 * full :], b[2 * full :]
    low = low_half(a_rest.shape)
    u = [a[:full], b[:full], jnp.where(low, a_rest, half_roll(b_rest))]
    v = [a[full : 2 * full], b[full : 2 * full], jnp.where(low, half_roll(a_rest), b_rest)]
    return u, v


def packed(a_first, b_first, a_rest, b_rest):
    low = low_half(a_rest.shape)
    return jnp.concatenate([a_first, b_first, jnp.where(low, a_rest, half_roll(b_rest))], 0).astype(bf16)


def pack_columns(rows_ref, start, half):
    full = rows_ref.shape[0] - TILE
    a, b = slice(start, start + half), slice(start + half, start + 2 * half)
    return packed(rows_ref[:full, a], rows_ref[:full, b], rows_ref[full:, a], rows_ref[full:, b])


def prepare_first_kernel(bounds, tokens_ref, *refs):
    rows_ref = refs[-1]
    rows_ref[0 : tokens_ref.shape[0], :] = tokens_ref[...].astype(f32)
    for out_ref, (start, half) in zip(refs[:-1], bounds, strict=True):
        out_ref[...] = pack_columns(rows_ref, start, half)


def prepare_last_kernel(start, half, tokens_ref, ids_ref, gates_ref, out_ref, rows_ref, route_ref):
    rows = tokens_ref.shape[0]
    rows_ref[0:rows, :] = tokens_ref[...].astype(f32)
    out_ref[:, :half] = pack_columns(rows_ref, start, half)
    experts = GROUPS * EXP_G
    catalog = lax.broadcasted_iota(jnp.int32, (experts, rows), 0)
    weight = jnp.zeros((experts, rows), f32)
    for k in range(ids_ref.shape[0]):
        weight = weight + jnp.where(ids_ref[k : k + 1, :] == catalog, gates_ref[k : k + 1, :], 0.0)
    row = lax.broadcasted_iota(jnp.int32, (experts, LANES), 0)
    eye = (row == lax.broadcasted_iota(jnp.int32, (experts, LANES), 1)).astype(bf16)
    route_ref[0:rows, :] = lax.dot_general(
        weight.astype(bf16), eye, (((0,), (0,)), ((), ())), preferred_element_type=f32
    )
    full = rows // TILE * TILE
    none = jnp.zeros((TILE, LANES), f32)
    out_ref[:, half:] = packed(route_ref[:full, :], jnp.zeros((full, LANES), f32), route_ref[full:, :], none)


def prepare(tokens, expert_ids, gates, bounds):
    rows, width = tokens.shape
    padded = -(-rows // TILE) * TILE
    first = pl.pallas_call(
        functools.partial(prepare_first_kernel, bounds[:-1]),
        out_shape=[jax.ShapeDtypeStruct((2 * rows, half), bf16) for _, half in bounds[:-1]],
        scratch_shapes=[pltpu.VMEM((padded, width), f32)],
    )(tokens)
    start, half = bounds[-1]
    last = pl.pallas_call(
        functools.partial(prepare_last_kernel, start, half),
        out_shape=jax.ShapeDtypeStruct((2 * rows, half + LANES), bf16),
        scratch_shapes=[pltpu.VMEM((padded, width), f32), pltpu.VMEM((padded, LANES), f32)],
    )(tokens, expert_ids.T, gates.T)
    return list(first) + [last]


def cut(width, shares):
    step = 2 * LANES
    blocks = width // step
    ends = [round(blocks * sum(shares[: i + 1]) / sum(shares)) for i in range(len(shares))]
    return [(step * low, LANES * (high - low)) for low, high in zip([0] + ends[:-1], ends, strict=True)]


def unpack_rows(refs, half, unit, lhs_ref, route_ref):
    at = 0
    for ref in refs:
        for start in range(0, ref.shape[0], 4 * unit):
            block = ref[start : start + 4 * unit, :].astype(f32)
            pieces_a, pieces_b = [], []
            for pair in range(2):
                u = block[2 * pair * unit : (2 * pair + 1) * unit]
                v = block[(2 * pair + 1) * unit : (2 * pair + 2) * unit]
                a, b = unpack_pair(u, v)
                pieces_a += a
                pieces_b += b
            rows_a = jnp.concatenate(pieces_a, 0)
            count = rows_a.shape[0]
            lhs_ref[at : at + count, 0:half] = rows_a[:, :half].astype(bf16)
            lhs_ref[at : at + count, half : 2 * half] = jnp.concatenate(pieces_b, 0)[:, :half].astype(bf16)
            if route_ref is not None:
                route_ref[at : at + count, :] = rows_a[:, half:]
            at += count


def down_chunk(hidden, weight_ref, half, unit, keep_ref, send_ref):
    rows = hidden.shape[0]
    depth = weight_ref.shape[1]
    total = None
    for expert in range(EXP_G):
        part = jnp.dot(
            hidden[:, expert * depth : (expert + 1) * depth], weight_ref[expert], preferred_element_type=f32
        )
        total = part if total is None else total + part
    blocks = []
    for at in range(0, rows, unit):
        u, v = pack_pair(total[at : at + unit, :half], total[at : at + unit, half:])
        blocks += u + v
    packed = jnp.concatenate(blocks, 0).astype(bf16)
    keep_ref[...] = packed[:rows]
    send_ref[...] = packed[rows:]


def first_kernel(start, half, unit, first, last, *refs):
    refs = list(refs)
    blocks = refs[:3]
    refs = refs[3:]
    group_ref = refs.pop(0) if last else None
    prior_ref = None if first else refs.pop(0)
    gate_ref, up_ref = refs[:2]
    refs = refs[2:]
    if last:
        down_ref, hidden_ref, keep_ref, send_ref = refs[:4]
        refs = refs[4:]
    else:
        acc_ref = refs.pop(0)
    lhs_ref, weights_ref, sems = refs[:3]
    copies = []
    for expert in range(EXP_G):
        for which, source in enumerate((gate_ref, up_ref)):
            copy = pltpu.make_async_copy(
                source.at[expert, pl.ds(start, 2 * half), :], weights_ref.at[expert, which], sems.at[2 * expert + which]
            )
            copy.start()
            copies.append(copy)
    if last:
        down_weights_ref, down_sem, route_ref = refs[3:6]
        down_copy = pltpu.make_async_copy(
            down_ref.at[:, :, pl.ds(0, down_weights_ref.shape[2])], down_weights_ref, down_sem
        )
        down_copy.start()
    unpack_rows(blocks, half, unit, lhs_ref, route_ref if last else None)
    depth = gate_ref.shape[2]
    if last:
        lane = lax.broadcasted_iota(jnp.int32, route_ref.shape, 1)
    for expert in range(EXP_G):
        parts = []
        for which in range(2):
            copies[2 * expert + which].wait()
            value = jnp.dot(lhs_ref[...], weights_ref[expert, which], preferred_element_type=f32)
            if not first:
                value = value + prior_ref[expert, which]
            if last:
                parts.append(value)
            else:
                acc_ref[expert, which] = value
        if last:
            chosen = jnp.where(lane == group_ref[0] * EXP_G + expert, route_ref[...], 0.0)
            gate_value, lifted = parts
            value = gate_value / (1.0 + jnp.exp(-gate_value)) * lifted * jnp.sum(chosen, 1, keepdims=True)
            hidden_ref[:, expert * depth : (expert + 1) * depth] = value.astype(bf16)
    if last:
        down_copy.wait()
        down_chunk(hidden_ref[...], down_weights_ref, down_weights_ref.shape[2] // 2, unit, keep_ref, send_ref)


def expert_step(bounds, index, blocks, extra, w_gate, w_up, w_down, unit, out_half):
    first, last = index == 0, index == len(bounds) - 1
    start, half = bounds[index]
    width = 2 * half
    depth = w_gate.shape[2]
    rows = sum(b.shape[0] for b in blocks) // 2
    vmem = pl.BlockSpec(memory_space=pltpu.VMEM)
    hbm = pl.BlockSpec(memory_space=pl.ANY)
    smem = pl.BlockSpec(memory_space=pltpu.SMEM)
    scratch = [
        pltpu.VMEM((rows, width), bf16),
        pltpu.VMEM((EXP_G, 2, width, depth), bf16),
        pltpu.SemaphoreType.DMA((2 * EXP_G,)),
    ]
    args = [*blocks, *extra, w_gate, w_up]
    specs = [vmem] * len(blocks) + ([smem] if last else []) + ([] if first else [vmem]) + [hbm, hbm]
    bytes_in = EXP_G * 2 * width * depth * 2
    if last:
        columns = 2 * out_half
        args.append(w_down)
        specs.append(hbm)
        shapes = [jax.ShapeDtypeStruct((rows, EXP_G * depth), bf16)] + [jax.ShapeDtypeStruct((rows, out_half), bf16)] * 2
        scratch += [
            pltpu.VMEM((EXP_G, depth, columns), bf16),
            pltpu.SemaphoreType.DMA,
            pltpu.VMEM((rows, LANES), f32),
        ]
        bytes_in += EXP_G * depth * columns * 2
    else:
        shapes = [jax.ShapeDtypeStruct((EXP_G, 2, rows, depth), f32)]
    return pl.pallas_call(
        functools.partial(first_kernel, start, half, unit, first, last),
        out_shape=shapes,
        in_specs=specs,
        out_specs=[vmem] * len(shapes),
        scratch_shapes=scratch,
        compiler_params=pltpu.CompilerParams(vmem_limit_bytes=48 * MIB),
        cost_estimate=pl.CostEstimate(flops=rows * bytes_in, bytes_accessed=bytes_in, transcendentals=0),
    )(*args)


def down_kernel(start, half, unit, hidden_ref, down_ref, keep_ref, send_ref, weights_ref, sem):
    copy = pltpu.make_async_copy(down_ref.at[:, :, pl.ds(start, 2 * half)], weights_ref, sem)
    copy.start()
    copy.wait()
    down_chunk(hidden_ref[...], weights_ref, half, unit, keep_ref, send_ref)


def down_step(start, half, hidden, w_down, unit):
    depth = w_down.shape[1]
    rows = hidden.shape[0]
    vmem = pl.BlockSpec(memory_space=pltpu.VMEM)
    bytes_in = EXP_G * depth * 2 * half * 2
    return pl.pallas_call(
        functools.partial(down_kernel, start, half, unit),
        out_shape=[jax.ShapeDtypeStruct((rows, half), bf16)] * 2,
        in_specs=[vmem, pl.BlockSpec(memory_space=pl.ANY)],
        out_specs=[vmem] * 2,
        scratch_shapes=[pltpu.VMEM((EXP_G, depth, 2 * half), bf16), pltpu.SemaphoreType.DMA],
        compiler_params=pltpu.CompilerParams(vmem_limit_bytes=48 * MIB),
        cost_estimate=pl.CostEstimate(flops=rows * bytes_in, bytes_accessed=bytes_in, transcendentals=0),
    )(hidden, w_down)


def finish_kernel(bounds, rows, *refs):
    out_ref, whole_ref = refs[-2:]
    refs = refs[:-2]
    per = len(refs) // len(bounds)
    full = rows // TILE * TILE
    for c, (start, half) in enumerate(bounds):
        total = refs[c * per][...].astype(f32)
        for ref in refs[c * per + 1 : (c + 1) * per]:
            total = total + ref[...].astype(f32)
        a, b = slice(start, start + half), slice(start + half, start + 2 * half)
        rest = total[2 * full :]
        whole_ref[:full, a] = total[:full]
        whole_ref[:full, b] = total[full : 2 * full]
        whole_ref[full:, a] = rest
        whole_ref[full:, b] = half_roll(rest)
    out_ref[...] = whole_ref[0:rows, :].astype(bf16)


def finish(parts, bounds, rows, width):
    padded = -(-rows // TILE) * TILE
    return pl.pallas_call(
        functools.partial(finish_kernel, bounds, rows),
        out_shape=jax.ShapeDtypeStruct((rows, width), bf16),
        scratch_shapes=[pltpu.VMEM((padded, width), f32)],
    )(*[p for chunk in parts for p in chunk])


def local(tokens, expert_ids, gates, w_gate, w_up, w_down):
    count = lax.axis_size("wide")
    group_size = count // GROUPS
    far = count // 4
    rows, width = tokens.shape
    unit = 2 * rows
    group = (lax.axis_index("wide") // group_size).astype(jnp.int32).reshape(1)
    bounds = cut(width, IN_SHARES)
    out_bounds = cut(width, OUT_SHARES)
    chunks = prepare(tokens, expert_ids, gates, bounds)

    state = []
    for c, own in enumerate(chunks):
        line = jnp.concatenate([own] + [swap(own, 4 * f, count) for f in range(1, far)], 0)
        crossed = swap(line, 2, count)
        other = swap(jnp.concatenate([line, crossed], 0), 1, count)
        extra = [*([group] if c == len(chunks) - 1 else []), *state]
        state = expert_step(
            bounds, c, (line, crossed, other), extra, w_gate, w_up, w_down, unit, out_bounds[0][1]
        )
    hidden, keep, send = state

    parts = []
    for c, (start, half) in enumerate(out_bounds):
        if c > 0:
            keep, send = down_step(start, half, hidden, w_down, unit)
        got = swap(send, 1, count)
        summed = (keep.astype(f32) + got.astype(f32)).astype(bf16)
        middle = summed.shape[0] // 2
        got = swap(summed[middle:], 2, count)
        summed = (summed[:middle].astype(f32) + got.astype(f32)).astype(bf16)
        pieces = [summed[f * unit : (f + 1) * unit] for f in range(far)]
        parts.append([pieces[0]] + [swap(pieces[f], 4 * f, count) for f in range(1, far)])
    return finish(parts, out_bounds, rows, width)


def solution(mesh):
    return jax.shard_map(
        local,
        mesh=mesh,
        in_specs=(
            P(("parts", "wide"), None),
            P(("parts", "wide"), None),
            P(("parts", "wide"), None),
            P(None, None, "wide"),
            P(None, None, "wide"),
            P(None, "wide", None),
        ),
        out_specs=P(("parts", "wide"), None),
        check_vma=False,
    )
```

time: 114 us -> 87.9 us (0.77)
  starting transfers between devices: 46.4 us -> 25.5 us
  Pallas kernels: 28.8 us -> 25.2 us
  local copies, waits for them, and re-layouts: 8.49 us -> 7.17 us
    ppermute x40 -> x20, starting transfers between devices: 46.4 us -> 25.5 us  [swap(): return lax.ppermute(block, 'wide', [(i, i ^ bits) for i in range(count)])]
    pallas_call x9 -> x6, Pallas kernels: 28.8 us -> 25.2 us  [the longest x2 15.2 us: expert_step(): pl.pallas_call(functools.partial(first_kernel, start, half, unit, first,...]
    slice x4 -> x2, local copies, waits for them, and re-layouts: 2.51 us -> 1.33 us  [local(): pieces = [summed[f * unit:(f + 1) * unit] for f in range(far)]]
    ppermute x40 -> x20, waiting for transfers between devices: 29 us -> 28 us  [swap(): return lax.ppermute(block, 'wide', [(i, i ^ bits) for i in range(count)])]
    unnamed x41 -> x22, local copies, waits for them, and re-layouts: 5.84 us -> 5.01 us
  transfers between devices with their start and end apart: 40 -> 20, of which waited for: 11 -> 9; matrix products, arithmetic and copies ran while one was open for 5% -> 9% of each run, Pallas kernels for 15% -> 14%
where the time goes in v2:
time: 87.9 us; the launch traced here: 87.5 us
  waiting for transfers between devices  28 us (32%)
  starting transfers between devices  25.5 us (29%)
  Pallas kernels  25.2 us (29%)
  local copies, waits for them, and re-layouts  7.17 us (8%)
  other arithmetic  1.43 us (2%)
    ppermute x20, waiting for transfers between devices, swap(): return lax.ppermute(block, 'wide', [(i, i ^ bits) for i in range(count)])  28 us
    ppermute x20, starting transfers between devices, swap(): return lax.ppermute(block, 'wide', [(i, i ^ bits) for i in range(count)])  25.5 us
    pallas_call x2, Pallas kernels, expert_step(): pl.pallas_call(functools.partial(first_kernel, start, half, unit, first,...  15.2 us
    unnamed x22, local copies, waits for them, and re-layouts  5.01 us
    pallas_call x1, Pallas kernels, down_step(): pl.pallas_call(functools.partial(down_kernel, start, half, unit), out_sha...  4.7 us
    pallas_call x1, Pallas kernels, finish(): pl.pallas_call(functools.partial(finish_kernel, bounds, rows), out_shape=...  1.99 us
    pallas_call x1, Pallas kernels, prepare(): pl.pallas_call(functools.partial(prepare_last_kernel, start, half), out_s...  1.78 us
  transfers between devices with their start and end apart: 20, of which 9 were waited for; matrix products, arithmetic and copies ran while one was open for 9% of the time, Pallas kernels for 14%

profile of v2, /device:TPU:0, one launch (start us, length us, event | category | flops | bytes accessed | tf_op | source)
XLA Modules:
  0.0 87.5 jit_solution(3718815782957218924)
XLA Ops:
  0.0 1.6 %shard_map.65 = bf16[24,1792]{1,0:T(8,128)(2,1)} custom-call(bf16[12,7168]{1,0:T(8,128)(2,1)} %tokens_ref.3), custom_call_target="tpu_custom_call" | custom-call | tf_op jit(solution)/shard_map/pallas_call | solution.py:91
  1.6 5.0 %collective-permute-start.7 = (bf16[24,1792]{1,0:T(8,128)(2,1)}, bf16[24,1792]{1,0:T(8,128)(2,1)S(1)}, u32[]{:S(2)}, u32[]{:S(2)}) collective-permute-start(bf16[24,1792]{1,0:T(8,128)(2,1)} %shard_map.65), channel_id=1, source_target_pairs={{0,12},{1,13},{2,14},{3,15},{4,8},{5,9},{6,10},{7,11},{8,4},{9,5},... | collective-permute-start | bytes 258056 | tf_op jit(solution)/shard_map/ppermute | solution.py:22
  6.6 0.0 collective-permute-start.6
  6.6 0.6 collective-permute-start.5
  7.2 1.8 %shard_map.64 = bf16[24,1920]{1,0:T(8,128)(2,1)} custom-call(bf16[12,7168]{1,0:T(8,128)(2,1)} %tokens_ref.3, s32[8,12]{1,0:T(8,128)} %bitcast.3, f32[8,12]{1,0:T(8,128)} %bitcast.4), custom_call_target="tpu_custom_call" | custom-call | tf_op jit(solution)/shard_map/pallas_call | solution.py:97
  9.0 3.8 %collective-permute-start.2 = (bf16[24,1920]{1,0:T(8,128)(2,1)}, bf16[24,1920]{1,0:T(8,128)(2,1)S(1)}, u32[]{:S(2)}, u32[]{:S(2)}) collective-permute-start(bf16[24,1920]{1,0:T(8,128)(2,1)} %shard_map.64), channel_id=1, source_target_pairs={{0,12},{1,13},{2,14},{3,15},{4,8},{5,9},{6,10},{7,11},{8,4},{9,5},... | collective-permute-start | bytes 276488 | tf_op jit(solution)/shard_map/ppermute | solution.py:22
  12.8 0.0 collective-permute-start.1
  12.8 0.9 %constant_dynamic-update-slice_fusion.9 = bf16[192,1792]{1,0:T(8,128)(2,1)S(1)} fusion(bf16[24,1792]{1,0:T(8,128)(2,1)} %shard_map.65), kind=kLoop, calls=%fused_computation.15 | loop fusion | bytes 172032
  13.7 1.5 %constant_dynamic-update-slice_fusion.4 = bf16[192,1920]{1,0:T(8,128)(2,1)} fusion(bf16[24,1920]{1,0:T(8,128)(2,1)} %shard_map.64), kind=kLoop, calls=%fused_computation.10 | loop fusion | bytes 184320
  15.3 0.0 collective-permute-done.7
  15.3 0.6 collective-permute-start
  15.8 3.1 %collective-permute-done.6 = bf16[24,1792]{1,0:T(8,128)(2,1)S(1)} collective-permute-done((bf16[24,1792]{1,0:T(8,128)(2,1)}, bf16[24,1792]{1,0:T(8,128)(2,1)S(1)}, u32[]{:S(2)}, u32[]{:S(2)}) %collective-permute-start.6) | collective-permute-done | bytes 86048 | tf_op jit(solution)/shard_map/ppermute | solution.py:22
  18.9 0.0 collective-permute-done.5
  18.9 0.9 %pad_maximum_fusion.1.refs_0_ = bf16[96,1792]{1,0:T(8,128)(2,1)S(1)} fusion(bf16[24,1792]{1,0:T(8,128)(2,1)S(1)} %collective-permute-done.7, bf16[24,1792]{1,0:T(8,128)(2,1)S(1)} %collective-permute-done.6, bf16[24,1792]{1,0:T(8,128)(2,1)S(1)} %collective-permute-done.5, bf16[24,1792]{1,0:T(8,128)(2,1)} %shard_map.65), kind=kLoop, calls=%fused_computation.5 | loop fusion | flops 1376256 | bytes 688128 | tf_op jit(solution)/shard_map/concatenate | solution.py:308
  19.8 1.5 %collective-permute-start.8 = (bf16[96,1792]{1,0:T(8,128)(2,1)S(1)}, bf16[96,1792]{1,0:T(8,128)(2,1)S(1)}, u32[]{:S(2)}, u32[]{:S(2)}) collective-permute-start(bf16[96,1792]{1,0:T(8,128)(2,1)S(1)} %pad_maximum_fusion.1.refs_0_), channel_id=1, source_target_pairs={{0,2},{1,3},{2,0},{3,1},{4,6},{5,7},{6,4},{7,5},{8,10},{9,11},{10,... | collective-permute-start | bytes 1032200 | tf_op jit(solution)/shard_map/ppermute | solution.py:22
  21.3 0.0 collective-permute-done.2
  21.4 0.6 collective-permute-done.1
  22.0 0.0 collective-permute-done
  22.0 0.0 copy-done
  22.0 1.6 %collective-permute-start.3 = (bf16[96,1920]{1,0:T(8,128)(2,1)S(1)}, bf16[96,1920]{1,0:T(8,128)(2,1)S(1)}, u32[]{:S(2)}, u32[]{:S(2)}) collective-permute-start(bf16[96,1920]{1,0:T(8,128)(2,1)S(1)} %pad_maximum_fusion.refs_0_), channel_id=1, source_target_pairs={{0,2},{1,3},{2,0},{3,1},{4,6},{5,7},{6,4},{7,5},{8,10},{9,11},{10,... | collective-permute-start | bytes 1105928 | tf_op jit(solution)/shard_map/ppermute | solution.py:22
  23.6 0.6 constant_dynamic-update-slice_fusion.3
  24.3 0.6 constant_dynamic-update-slice_fusion.2
  24.9 0.6 constant_dynamic-update-slice_fusion.1
  25.5 5.0 %collective-permute-done.8.refs_1_ = bf16[96,1792]{1,0:T(8,128)(2,1)S(1)} collective-permute-done((bf16[96,1792]{1,0:T(8,128)(2,1)S(1)}, bf16[96,1792]{1,0:T(8,128)(2,1)S(1)}, u32[]{:S(2)}, u32[]{:S(2)}) %collective-permute-start.8) | collective-permute-done | bytes 344096 | tf_op jit(solution)/shard_map/ppermute | solution.py:22
  30.5 0.1 collective-permute-start.9
  30.6 4.5 %collective-permute-done.3.refs_1_ = bf16[96,1920]{1,0:T(8,128)(2,1)S(1)} collective-permute-done((bf16[96,1920]{1,0:T(8,128)(2,1)S(1)}, bf16[96,1920]{1,0:T(8,128)(2,1)S(1)}, u32[]{:S(2)}, u32[]{:S(2)}) %collective-permute-start.3) | collective-permute-done | bytes 368672 | tf_op jit(solution)/shard_map/ppermute | solution.py:22
  35.1 0.8 constant_dynamic-update-slice_fusion
  35.8 0.0 collective-permute-start.4
  35.8 0.0 collective-permute-done.9.refs_2_
  35.8 6.2 %shard_map.66.refs_4_ = f32[2,2,192,512]{3,2,1,0:T(8,128)S(1)} custom-call(bf16[96,1792]{1,0:T(8,128)(2,1)S(1)} %pad_maximum_fusion.1.refs_0_, bf16[96,1792]{1,0:T(8,128)(2,1)S(1)} %collective-permute-done.8.refs_1_, bf16[192,1792]{1,0:T(8,128)(2,1)S(1)} %collective-permute-done.9.refs_2_, bf16[2,7168,512]{2,1,0:T(8,128)(2,1)} %refs_5_.1, ...), custom_call_target="tpu_custom_call" | custom-call | flops 2818572288 | bytes 14680064 | tf_op jit(solution)/shard_map/pallas_call | solution.py:234
  42.0 0.0 collective-permute-done.4.refs_2_
  42.0 9.0 %shard_map.67 = (bf16[192,1024]{1,0:T(8,128)(2,1)S(1)}, bf16[192,1792]{1,0:T(8,128)(2,1)S(1)}, bf16[192,1792]{1,0:T(8,128)(2,1)S(1)}) custom-call(bf16[96,1920]{1,0:T(8,128)(2,1)S(1)} %pad_maximum_fusion.refs_0_, bf16[96,1920]{1,0:T(8,128)(2,1)S(1)} %collective-permute-done.3.refs_1_, bf16[192,1920]{1,0:T(8,128)(2,1)S(1)} %collective-permute-done.4.refs_2_, ...), custom_call_target="tpu_custom_call" | custom-call | flops 4227858432 | bytes 22020096 | tf_op jit(solution)/shard_map/pallas_call | solution.py:234
  51.0 0.6 collective-permute-start.10
  51.6 4.7 %shard_map.68 = (bf16[192,1792]{1,0:T(8,128)(2,1)S(1)}, bf16[192,1792]{1,0:T(8,128)(2,1)S(1)}) custom-call(bf16[192,1024]{1,0:T(8,128)(2,1)S(1)} %get-tuple-element.12.hidden_ref, bf16[2,512,7168]{2,1,0:T(8,128)(2,1)} %down_ref.1), custom_call_target="tpu_custom_call" | custom-call | flops 1409286144 | bytes 7340032 | tf_op jit(solution)/shard_map/pallas_call | solution.py:257
  56.3 0.1 collective-permute-start.15
  56.4 0.0 collective-permute-done.10
  56.4 0.2 add_convert_fusion.1
  56.6 1.5 %collective-permute-start.11 = (bf16[96,1792]{1,0:T(8,128)(2,1)S(1)}, bf16[96,1792]{1,0:T(8,128)(2,1)S(1)}, u32[]{:S(2)}, u32[]{:S(2)}) collective-permute-start(bf16[96,1792]{1,0:T(8,128)(2,1)S(1)} %slice.49), channel_id=1, source_target_pairs={{0,2},{1,3},{2,0},{3,1},{4,6},{5,7},{6,4},{7,5},{8,10},{9,11},{10,... | collective-permute-start | bytes 1032200 | tf_op jit(solution)/shard_map/ppermute | solution.py:22
  58.1 0.4 collective-permute-done.15
  58.5 0.2 add_convert_fusion
  58.7 1.5 %collective-permute-start.16 = (bf16[96,1792]{1,0:T(8,128)(2,1)S(1)}, bf16[96,1792]{1,0:T(8,128)(2,1)S(1)}, u32[]{:S(2)}, u32[]{:S(2)}) collective-permute-start(bf16[96,1792]{1,0:T(8,128)(2,1)S(1)} %slice.55), channel_id=1, source_target_pairs={{0,2},{1,3},{2,0},{3,1},{4,6},{5,7},{6,4},{7,5},{8,10},{9,11},{10,... | collective-permute-start | bytes 1032200 | tf_op jit(solution)/shard_map/ppermute | solution.py:22
  60.2 7.3 %collective-permute-done.11 = bf16[96,1792]{1,0:T(8,128)(2,1)S(1)} collective-permute-done((bf16[96,1792]{1,0:T(8,128)(2,1)S(1)}, bf16[96,1792]{1,0:T(8,128)(2,1)S(1)}, u32[]{:S(2)}, u32[]{:S(2)}) %collective-permute-start.11) | collective-permute-done | bytes 344096 | tf_op jit(solution)/shard_map/ppermute | solution.py:22
  67.5 0.1 add_convert_fusion.3
  67.6 0.7 fusion.1
  68.3 2.1 %collective-permute-start.14 = (bf16[24,1792]{1,0:T(8,128)(2,1)S(1)}, bf16[24,1792]{1,0:T(8,128)(2,1)S(1)}, u32[]{:S(2)}, u32[]{:S(2)}) collective-permute-start(bf16[24,1792]{1,0:T(8,128)(2,1)S(1)} %get-tuple-element.19), channel_id=1, source_target_pairs={{0,12},{1,13},{2,14},{3,15},{4,8},{5,9},{6,10},{7,11},{8,4},{9,5},... | collective-permute-start | bytes 258056 | tf_op jit(solution)/shard_map/ppermute | solution.py:22
  70.4 0.0 collective-permute-start.13
  70.4 2.3 %collective-permute-start.12 = (bf16[24,1792]{1,0:T(8,128)(2,1)S(1)}, bf16[24,1792]{1,0:T(8,128)(2,1)S(1)}, u32[]{:S(2)}, u32[]{:S(2)}) collective-permute-start(bf16[24,1792]{1,0:T(8,128)(2,1)S(1)} %get-tuple-element.21), channel_id=1, source_target_pairs={{0,4},{1,5},{2,6},{3,7},{4,0},{5,1},{6,2},{7,3},{8,12},{9,13},{10,... | collective-permute-start | bytes 258056 | tf_op jit(solution)/shard_map/ppermute | solution.py:22
  72.6 1.8 %collective-permute-done.16 = bf16[96,1792]{1,0:T(8,128)(2,1)S(1)} collective-permute-done((bf16[96,1792]{1,0:T(8,128)(2,1)S(1)}, bf16[96,1792]{1,0:T(8,128)(2,1)S(1)}, u32[]{:S(2)}, u32[]{:S(2)}) %collective-permute-start.16) | collective-permute-done | bytes 344096 | tf_op jit(solution)/shard_map/ppermute | solution.py:22
  74.5 0.1 add_convert_fusion.2
  74.6 0.7 fusion
  75.2 2.1 %collective-permute-start.19 = (bf16[24,1792]{1,0:T(8,128)(2,1)S(1)}, bf16[24,1792]{1,0:T(8,128)(2,1)S(1)}, u32[]{:S(2)}, u32[]{:S(2)}) collective-permute-start(bf16[24,1792]{1,0:T(8,128)(2,1)S(1)} %get-tuple-element.15), channel_id=1, source_target_pairs={{0,12},{1,13},{2,14},{3,15},{4,8},{5,9},{6,10},{7,11},{8,4},{9,5},... | collective-permute-start | bytes 258056 | tf_op jit(solution)/shard_map/ppermute | solution.py:22
  77.3 0.0 collective-permute-start.18
  77.3 0.0 collective-permute-done.14.refs_3_
  77.3 2.3 %collective-permute-start.17 = (bf16[24,1792]{1,0:T(8,128)(2,1)S(1)}, bf16[24,1792]{1,0:T(8,128)(2,1)S(1)}, u32[]{:S(2)}, u32[]{:S(2)}) collective-permute-start(bf16[24,1792]{1,0:T(8,128)(2,1)S(1)} %get-tuple-element.17), channel_id=1, source_target_pairs={{0,4},{1,5},{2,6},{3,7},{4,0},{5,1},{6,2},{7,3},{8,12},{9,13},{10,... | collective-permute-start | bytes 258056 | tf_op jit(solution)/shard_map/ppermute | solution.py:22
  79.6 0.0 collective-permute-done.13.refs_2_
  79.6 0.0 collective-permute-done.12.refs_1_
  79.6 0.0 copy-start.3
  79.6 2.9 %collective-permute-done.19.refs_7_ = bf16[24,1792]{1,0:T(8,128)(2,1)S(1)} collective-permute-done((bf16[24,1792]{1,0:T(8,128)(2,1)S(1)}, bf16[24,1792]{1,0:T(8,128)(2,1)S(1)}, u32[]{:S(2)}, u32[]{:S(2)}) %collective-permute-start.19) | collective-permute-done | bytes 86048 | tf_op jit(solution)/shard_map/ppermute | solution.py:22
  82.5 2.3 %collective-permute-done.18.refs_6_ = bf16[24,1792]{1,0:T(8,128)(2,1)S(1)} collective-permute-done((bf16[24,1792]{1,0:T(8,128)(2,1)S(1)}, bf16[24,1792]{1,0:T(8,128)(2,1)S(1)}, u32[]{:S(2)}, u32[]{:S(2)}) %collective-permute-start.18) | collective-permute-done | bytes 86048 | tf_op jit(solution)/shard_map/ppermute | solution.py:22
  84.9 0.0 collective-permute-done.17.refs_5_
  84.9 0.0 copy-done.1
  84.9 0.6 copy-done.5
  85.5 0.0 copy-done.6
  85.5 2.0 %shard_map.69 = bf16[12,7168]{1,0:T(8,128)(2,1)} custom-call(bf16[24,1792]{1,0:T(8,128)(2,1)} %get-tuple-element.22.refs_0_, bf16[24,1792]{1,0:T(8,128)(2,1)} %copy-done.3, bf16[24,1792]{1,0:T(8,128)(2,1)} %copy-done.2, bf16[24,1792]{1,0:T(8,128)(2,1)} %copy-done.1, bf16[24,1792]{1,0:T(8,128)(2,1)} %get-tuple-element.18.refs_4_, bf16[24,1792]{1,0:T(8,128)(2,1)} %copy-done.6, ...), custom_call_target="tpu_custom_call" | custom-call | tf_op jit(solution)/shard_map/pallas_call | solution.py:288
  (16 shorter events, 0.1 us)
Async XLA Ops:
  1.6 13.7 %collective-permute-start.7 = (bf16[24,1792]{1,0:T(8,128)(2,1)}, bf16[24,1792]{1,0:T(8,128)(2,1)S(1)}, u32[]{:S(2)}, u32[]{:S(2)}) collective-permute-start(bf16[24,1792]{1,0:T(8,128)(2,1)} %shard_map.65), channel_id=1, source_target_pairs={{0,12},{1,13},{2,14},{3,15},{4,8},{5,9},{6,10},{7,11},{8,4},{9,5},... | collective-permute-start | bytes 258056 | tf_op jit(solution)/shard_map/ppermute | solution.py:22
  6.6 12.3 %collective-permute-start.6 = (bf16[24,1792]{1,0:T(8,128)(2,1)}, bf16[24,1792]{1,0:T(8,128)(2,1)S(1)}, u32[]{:S(2)}, u32[]{:S(2)}) collective-permute-start(bf16[24,1792]{1,0:T(8,128)(2,1)} %shard_map.65), channel_id=1, source_target_pairs={{0,8},{1,9},{2,10},{3,11},{4,12},{5,13},{6,14},{7,15},{8,0},{9,1},... | collective-permute-start | bytes 258056 | tf_op jit(solution)/shard_map/ppermute | solution.py:22
  6.6 12.3 %collective-permute-start.5 = (bf16[24,1792]{1,0:T(8,128)(2,1)}, bf16[24,1792]{1,0:T(8,128)(2,1)S(1)}, u32[]{:S(2)}, u32[]{:S(2)}) collective-permute-start(bf16[24,1792]{1,0:T(8,128)(2,1)} %shard_map.65), channel_id=1, source_target_pairs={{0,4},{1,5},{2,6},{3,7},{4,0},{5,1},{6,2},{7,3},{8,12},{9,13},{10,... | collective-permute-start | bytes 258056 | tf_op jit(solution)/shard_map/ppermute | solution.py:22
  9.0 13.0 %copy-start = (bf16[24,1920]{1,0:T(8,128)(2,1)S(1)}, bf16[24,1920]{1,0:T(8,128)(2,1)}, u32[]{:S(2)}) copy-start(bf16[24,1920]{1,0:T(8,128)(2,1)} %shard_map.64) | copy-start | bytes 276484
  9.0 12.4 %collective-permute-start.2 = (bf16[24,1920]{1,0:T(8,128)(2,1)}, bf16[24,1920]{1,0:T(8,128)(2,1)S(1)}, u32[]{:S(2)}, u32[]{:S(2)}) collective-permute-start(bf16[24,1920]{1,0:T(8,128)(2,1)} %shard_map.64), channel_id=1, source_target_pairs={{0,12},{1,13},{2,14},{3,15},{4,8},{5,9},{6,10},{7,11},{8,4},{9,5},... | collective-permute-start | bytes 276488 | tf_op jit(solution)/shard_map/ppermute | solution.py:22
  12.8 9.2 %collective-permute-start.1 = (bf16[24,1920]{1,0:T(8,128)(2,1)}, bf16[24,1920]{1,0:T(8,128)(2,1)S(1)}, u32[]{:S(2)}, u32[]{:S(2)}) collective-permute-start(bf16[24,1920]{1,0:T(8,128)(2,1)} %shard_map.64), channel_id=1, source_target_pairs={{0,8},{1,9},{2,10},{3,11},{4,12},{5,13},{6,14},{7,15},{8,0},{9,1},... | collective-permute-start | bytes 276488 | tf_op jit(solution)/shard_map/ppermute | solution.py:22
  15.3 6.7 %collective-permute-start = (bf16[24,1920]{1,0:T(8,128)(2,1)}, bf16[24,1920]{1,0:T(8,128)(2,1)S(1)}, u32[]{:S(2)}, u32[]{:S(2)}) collective-permute-start(bf16[24,1920]{1,0:T(8,128)(2,1)} %shard_map.64), channel_id=1, source_target_pairs={{0,4},{1,5},{2,6},{3,7},{4,0},{5,1},{6,2},{7,3},{8,12},{9,13},{10,... | collective-permute-start | bytes 276488 | tf_op jit(solution)/shard_map/ppermute | solution.py:22
  19.8 10.7 %collective-permute-start.8 = (bf16[96,1792]{1,0:T(8,128)(2,1)S(1)}, bf16[96,1792]{1,0:T(8,128)(2,1)S(1)}, u32[]{:S(2)}, u32[]{:S(2)}) collective-permute-start(bf16[96,1792]{1,0:T(8,128)(2,1)S(1)} %pad_maximum_fusion.1.refs_0_), channel_id=1, source_target_pairs={{0,2},{1,3},{2,0},{3,1},{4,6},{5,7},{6,4},{7,5},{8,10},{9,11},{10,... | collective-permute-start | bytes 1032200 | tf_op jit(solution)/shard_map/ppermute | solution.py:22
  22.0 13.0 %collective-permute-start.3 = (bf16[96,1920]{1,0:T(8,128)(2,1)S(1)}, bf16[96,1920]{1,0:T(8,128)(2,1)S(1)}, u32[]{:S(2)}, u32[]{:S(2)}) collective-permute-start(bf16[96,1920]{1,0:T(8,128)(2,1)S(1)} %pad_maximum_fusion.refs_0_), channel_id=1, source_target_pairs={{0,2},{1,3},{2,0},{3,1},{4,6},{5,7},{6,4},{7,5},{8,10},{9,11},{10,... | collective-permute-start | bytes 1105928 | tf_op jit(solution)/shard_map/ppermute | solution.py:22
  30.5 5.3 %collective-permute-start.9 = (bf16[192,1792]{1,0:T(8,128)(2,1)S(1)}, bf16[192,1792]{1,0:T(8,128)(2,1)S(1)}, u32[]{:S(2)}, u32[]{:S(2)}) collective-permute-start(bf16[192,1792]{1,0:T(8,128)(2,1)S(1)} %constant_dynamic-update-slice_fusion.5), channel_id=1, source_target_pairs={{0,1},{1,0},{2,3},{3,2},{4,5},{5,4},{6,7},{7,6},{8,9},{9,8},{10,11... | collective-permute-start | bytes 2064392 | tf_op jit(solution)/shard_map/ppermute | solution.py:22
  35.8 6.2 %collective-permute-start.4 = (bf16[192,1920]{1,0:T(8,128)(2,1)}, bf16[192,1920]{1,0:T(8,128)(2,1)S(1)}, u32[]{:S(2)}, u32[]{:S(2)}) collective-permute-start(bf16[192,1920]{1,0:T(8,128)(2,1)} %constant_dynamic-update-slice_fusion), channel_id=1, source_target_pairs={{0,1},{1,0},{2,3},{3,2},{4,5},{5,4},{6,7},{7,6},{8,9},{9,8},{10,11... | collective-permute-start | bytes 2211848 | tf_op jit(solution)/shard_map/ppermute | solution.py:22
  51.0 5.4 %collective-permute-start.10 = (bf16[192,1792]{1,0:T(8,128)(2,1)S(1)}, bf16[192,1792]{1,0:T(8,128)(2,1)S(1)}, u32[]{:S(2)}, u32[]{:S(2)}) collective-permute-start(bf16[192,1792]{1,0:T(8,128)(2,1)S(1)} %get-tuple-element.11), channel_id=1, source_target_pairs={{0,1},{1,0},{2,3},{3,2},{4,5},{5,4},{6,7},{7,6},{8,9},{9,8},{10,11... | collective-permute-start | bytes 2064392 | tf_op jit(solution)/shard_map/ppermute | solution.py:22
  56.3 2.2 %collective-permute-start.15 = (bf16[192,1792]{1,0:T(8,128)(2,1)S(1)}, bf16[192,1792]{1,0:T(8,128)(2,1)S(1)}, u32[]{:S(2)}, u32[]{:S(2)}) collective-permute-start(bf16[192,1792]{1,0:T(8,128)(2,1)S(1)} %get-tuple-element.14), channel_id=1, source_target_pairs={{0,1},{1,0},{2,3},{3,2},{4,5},{5,4},{6,7},{7,6},{8,9},{9,8},{10,11... | collective-permute-start | bytes 2064392 | tf_op jit(solution)/shard_map/ppermute | solution.py:22
  56.6 10.9 %collective-permute-start.11 = (bf16[96,1792]{1,0:T(8,128)(2,1)S(1)}, bf16[96,1792]{1,0:T(8,128)(2,1)S(1)}, u32[]{:S(2)}, u32[]{:S(2)}) collective-permute-start(bf16[96,1792]{1,0:T(8,128)(2,1)S(1)} %slice.49), channel_id=1, source_target_pairs={{0,2},{1,3},{2,0},{3,1},{4,6},{5,7},{6,4},{7,5},{8,10},{9,11},{10,... | collective-permute-start | bytes 1032200 | tf_op jit(solution)/shard_map/ppermute | solution.py:22
  58.7 15.8 %collective-permute-start.16 = (bf16[96,1792]{1,0:T(8,128)(2,1)S(1)}, bf16[96,1792]{1,0:T(8,128)(2,1)S(1)}, u32[]{:S(2)}, u32[]{:S(2)}) collective-permute-start(bf16[96,1792]{1,0:T(8,128)(2,1)S(1)} %slice.55), channel_id=1, source_target_pairs={{0,2},{1,3},{2,0},{3,1},{4,6},{5,7},{6,4},{7,5},{8,10},{9,11},{10,... | collective-permute-start | bytes 1032200 | tf_op jit(solution)/shard_map/ppermute | solution.py:22
  68.3 9.1 %collective-permute-start.14 = (bf16[24,1792]{1,0:T(8,128)(2,1)S(1)}, bf16[24,1792]{1,0:T(8,128)(2,1)S(1)}, u32[]{:S(2)}, u32[]{:S(2)}) collective-permute-start(bf16[24,1792]{1,0:T(8,128)(2,1)S(1)} %get-tuple-element.19), channel_id=1, source_target_pairs={{0,12},{1,13},{2,14},{3,15},{4,8},{5,9},{6,10},{7,11},{8,4},{9,5},... | collective-permute-start | bytes 258056 | tf_op jit(solution)/shard_map/ppermute | solution.py:22
  70.4 9.2 %collective-permute-start.13 = (bf16[24,1792]{1,0:T(8,128)(2,1)S(1)}, bf16[24,1792]{1,0:T(8,128)(2,1)S(1)}, u32[]{:S(2)}, u32[]{:S(2)}) collective-permute-start(bf16[24,1792]{1,0:T(8,128)(2,1)S(1)} %get-tuple-element.20), channel_id=1, source_target_pairs={{0,8},{1,9},{2,10},{3,11},{4,12},{5,13},{6,14},{7,15},{8,0},{9,1},... | collective-permute-start | bytes 258056 | tf_op jit(solution)/shard_map/ppermute | solution.py:22
  70.4 9.2 %collective-permute-start.12 = (bf16[24,1792]{1,0:T(8,128)(2,1)S(1)}, bf16[24,1792]{1,0:T(8,128)(2,1)S(1)}, u32[]{:S(2)}, u32[]{:S(2)}) collective-permute-start(bf16[24,1792]{1,0:T(8,128)(2,1)S(1)} %get-tuple-element.21), channel_id=1, source_target_pairs={{0,4},{1,5},{2,6},{3,7},{4,0},{5,1},{6,2},{7,3},{8,12},{9,13},{10,... | collective-permute-start | bytes 258056 | tf_op jit(solution)/shard_map/ppermute | solution.py:22
  75.2 7.3 %collective-permute-start.19 = (bf16[24,1792]{1,0:T(8,128)(2,1)S(1)}, bf16[24,1792]{1,0:T(8,128)(2,1)S(1)}, u32[]{:S(2)}, u32[]{:S(2)}) collective-permute-start(bf16[24,1792]{1,0:T(8,128)(2,1)S(1)} %get-tuple-element.15), channel_id=1, source_target_pairs={{0,12},{1,13},{2,14},{3,15},{4,8},{5,9},{6,10},{7,11},{8,4},{9,5},... | collective-permute-start | bytes 258056 | tf_op jit(solution)/shard_map/ppermute | solution.py:22
  77.3 7.5 %collective-permute-start.18 = (bf16[24,1792]{1,0:T(8,128)(2,1)S(1)}, bf16[24,1792]{1,0:T(8,128)(2,1)S(1)}, u32[]{:S(2)}, u32[]{:S(2)}) collective-permute-start(bf16[24,1792]{1,0:T(8,128)(2,1)S(1)} %get-tuple-element.16), channel_id=1, source_target_pairs={{0,8},{1,9},{2,10},{3,11},{4,12},{5,13},{6,14},{7,15},{8,0},{9,1},... | collective-permute-start | bytes 258056 | tf_op jit(solution)/shard_map/ppermute | solution.py:22
  77.3 7.5 %copy-start.1 = (bf16[24,1792]{1,0:T(8,128)(2,1)}, bf16[24,1792]{1,0:T(8,128)(2,1)S(1)}, u32[]{:S(2)}) copy-start(bf16[24,1792]{1,0:T(8,128)(2,1)S(1)} %collective-permute-done.14.refs_3_) | copy-start | bytes 258052
  77.3 7.5 %collective-permute-start.17 = (bf16[24,1792]{1,0:T(8,128)(2,1)S(1)}, bf16[24,1792]{1,0:T(8,128)(2,1)S(1)}, u32[]{:S(2)}, u32[]{:S(2)}) collective-permute-start(bf16[24,1792]{1,0:T(8,128)(2,1)S(1)} %get-tuple-element.17), channel_id=1, source_target_pairs={{0,4},{1,5},{2,6},{3,7},{4,0},{5,1},{6,2},{7,3},{8,12},{9,13},{10,... | collective-permute-start | bytes 258056 | tf_op jit(solution)/shard_map/ppermute | solution.py:22
  79.6 5.2 %copy-start.2 = (bf16[24,1792]{1,0:T(8,128)(2,1)}, bf16[24,1792]{1,0:T(8,128)(2,1)S(1)}, u32[]{:S(2)}) copy-start(bf16[24,1792]{1,0:T(8,128)(2,1)S(1)} %collective-permute-done.13.refs_2_) | copy-start | bytes 258052
  79.6 5.3 %copy-start.3 = (bf16[24,1792]{1,0:T(8,128)(2,1)}, bf16[24,1792]{1,0:T(8,128)(2,1)S(1)}, u32[]{:S(2)}) copy-start(bf16[24,1792]{1,0:T(8,128)(2,1)S(1)} %collective-permute-done.12.refs_1_) | copy-start | bytes 258052
  82.5 2.4 %copy-start.4 = (bf16[24,1792]{1,0:T(8,128)(2,1)}, bf16[24,1792]{1,0:T(8,128)(2,1)S(1)}, u32[]{:S(2)}) copy-start(bf16[24,1792]{1,0:T(8,128)(2,1)S(1)} %collective-permute-done.19.refs_7_) | copy-start | bytes 258052
  84.9 0.6 copy-start.5
  84.9 0.7 copy-start.6

commit v3 on v0

v3 whole, which is shorter than its diff:
```python
import functools

import jax
import jax.numpy as jnp
from jax import lax
from jax.experimental import pallas as pl
from jax.experimental.pallas import tpu as pltpu
from jax.sharding import PartitionSpec as P

GROUPS = 8
EXP_G = 2
LANES = 128
TILE = 8
MIB = 1 << 20
VMEM_LIMIT = 48 * MIB
RING = 4
DOWN_RING = 4
DOWN_CHUNKS = 2
SMALL_COST = pl.CostEstimate(flops=1, bytes_accessed=1, transcendentals=0)
STEP_COST = pl.CostEstimate(flops=1 << 29, bytes_accessed=1, transcendentals=0)
bf16 = jnp.bfloat16
f32 = jnp.float32


def swap(block, bits, count):
    return lax.ppermute(block, "wide", [(i, i ^ bits) for i in range(count)])


def half_roll(block):
    return pltpu.roll(block, TILE // 2, 0)


def low_half(shape):
    return lax.broadcasted_iota(jnp.int32, shape, 0) < TILE // 2


def unpack_pair(u, v):
    full = (u.shape[0] - TILE) // 2
    u_rest, v_rest = u[2 * full :], v[2 * full :]
    low = low_half(u_rest.shape)
    a = [u[:full], v[:full], jnp.where(low, u_rest, half_roll(v_rest))]
    b = [u[full : 2 * full], v[full : 2 * full], jnp.where(low, half_roll(u_rest), v_rest)]
    return a, b


def pack_pair(a, b):
    full = (a.shape[0] - TILE) // 2
    a_rest, b_rest = a[2 * full :], b[2 * full :]
    low = low_half(a_rest.shape)
    u = [a[:full], b[:full], jnp.where(low, a_rest, half_roll(b_rest))]
    v = [a[full : 2 * full], b[full : 2 * full], jnp.where(low, half_roll(a_rest), b_rest)]
    return u, v


def pack_columns(rows_ref, a, b):
    full = rows_ref.shape[0] - TILE
    a_rest, b_rest = rows_ref[full:, a], rows_ref[full:, b]
    rest = jnp.where(low_half(a_rest.shape), a_rest, half_roll(b_rest))
    return jnp.concatenate([rows_ref[:full, a], rows_ref[:full, b], rest], 0).astype(bf16)


def prepare_kernel(tokens_ref, ids_ref, gates_ref, whole_ref, first_ref, second_ref, rows_ref):
    rows, width = tokens_ref.shape
    half, cut = width // 2, first_ref.shape[1]
    rows_ref[0:rows, :width] = tokens_ref[...].astype(f32)
    experts = GROUPS * EXP_G
    catalog = lax.broadcasted_iota(jnp.int32, (experts, rows), 0)
    weight = jnp.zeros((experts, rows), f32)
    for k in range(ids_ref.shape[0]):
        weight = weight + jnp.where(ids_ref[k : k + 1, :] == catalog, gates_ref[k : k + 1, :], 0.0)
    row = lax.broadcasted_iota(jnp.int32, (experts, LANES), 0)
    eye = (row == lax.broadcasted_iota(jnp.int32, (experts, LANES), 1)).astype(bf16)
    rows_ref[0:rows, width : width + LANES] = lax.dot_general(
        weight.astype(bf16), eye, (((0,), (0,)), ((), ())), preferred_element_type=f32
    )
    rows_ref[:, width + LANES :] = jnp.zeros((rows_ref.shape[0], LANES), f32)
    first = pack_columns(rows_ref, slice(0, cut), slice(half, half + cut))
    second = pack_columns(rows_ref, slice(cut, half), slice(half + cut, width))
    route = pack_columns(rows_ref, slice(width, width + LANES), slice(width + LANES, width + 2 * LANES))
    first_ref[...] = first
    second_ref[:, : half - cut] = second
    second_ref[:, half - cut :] = route
    whole_ref[:, :cut] = first
    whole_ref[:, cut:half] = second
    whole_ref[:, half:] = route


def prepare(tokens, expert_ids, gates, cut):
    rows, width = tokens.shape
    half = width // 2
    padded = -(-rows // TILE) * TILE
    return pl.pallas_call(
        prepare_kernel,
        out_shape=[
            jax.ShapeDtypeStruct((2 * rows, half + LANES), bf16),
            jax.ShapeDtypeStruct((2 * rows, cut), bf16),
            jax.ShapeDtypeStruct((2 * rows, half - cut + LANES), bf16),
        ],
        scratch_shapes=[pltpu.VMEM((padded, width + 2 * LANES), f32)],
    )(tokens, expert_ids.T, gates.T)


def unpack_kernel(unit, places, size, refs, out_ref):
    def read(place, at, width):
        ref, number = refs[place[0]], place[1]
        return ref[number * unit : (number + 1) * unit, at : at + width].astype(f32)

    at = 0
    for first in range(0, len(places), 4):
        pieces_a, pieces_b, pieces_r = [], [], []
        for i in (first, first + 2):
            pair = places[i : i + 2]
            a, b = unpack_pair(*(read(p, p[2], size) for p in pair))
            pieces_a += a
            pieces_b += b
            if pair[0][3] is not None:
                pieces_r += unpack_pair(*(read(p, p[3], LANES) for p in pair))[0]
        rows_a = jnp.concatenate(pieces_a, 0)
        rows = slice(at, at + rows_a.shape[0])
        out_ref[rows, :size] = rows_a.astype(bf16)
        out_ref[rows, size : 2 * size] = jnp.concatenate(pieces_b, 0).astype(bf16)
        if pieces_r:
            out_ref[rows, 2 * size :] = jnp.concatenate(pieces_r, 0).astype(bf16)
        at = rows.stop


def unpack(arrays, unit, places, size):
    width = 2 * size + (0 if places[0][3] is None else LANES)

    def kernel(*refs):
        unpack_kernel(unit, places, size, refs[:-1], refs[-1])

    return call_small(kernel, jax.ShapeDtypeStruct((len(places) * unit // 2, width), bf16), arrays)


def stack(arrays):
    def kernel(*refs):
        at = 0
        for ref in refs[:-1]:
            refs[-1][at : at + ref.shape[0], :] = ref[...]
            at += ref.shape[0]

    rows = sum(a.shape[0] for a in arrays)
    return call_small(kernel, jax.ShapeDtypeStruct((rows, arrays[0].shape[1]), bf16), arrays)


def expert_kernel(unit, far, start, size, first, last, *refs):
    refs = list(refs)
    mine_ref, other_ref = refs[:2]
    refs = refs[2:]
    group_ref = refs.pop(0) if last else None
    prior_ref = None if first else refs.pop(0)
    gate_ref, up_ref = refs[:2]
    refs = refs[2:]
    if last:
        down_ref, keep_far_ref, send_far_ref, keep_ref, send_ref = refs[:5]
        refs = refs[5:]
    else:
        acc_ref = refs.pop(0)
    lhs_ref, ring_ref, sems = refs[:3]
    half = gate_ref.shape[1] // 2
    steps = [(expert, which) for expert in range(EXP_G) for which in range(2)]
    slots = ring_ref.shape[0]

    def fetch(step):
        expert, which = steps[step]
        source = (gate_ref, up_ref)[which]
        return [
            pltpu.make_async_copy(
                source.at[expert, pl.ds(side * half + start, size), :],
                ring_ref.at[step % slots, pl.ds(side * size, size), :],
                sems.at[step % slots, side],
            )
            for side in range(2)
        ]

    for step in range(slots):
        for copy in fetch(step):
            copy.start()
    if last:
        hidden_ref, down_ring_ref, down_sems = refs[3:6]
        down_slots, column = down_ring_ref.shape[0], down_ring_ref.shape[2] // 2
        down_steps = [(chunk, expert) for chunk in range(half // column) for expert in range(EXP_G)]

        def fetch_down(step):
            chunk, expert = down_steps[step]
            return [
                pltpu.make_async_copy(
                    down_ref.at[expert, :, pl.ds(side * half + chunk * column, column)],
                    down_ring_ref.at[step % down_slots, :, pl.ds(side * column, column)],
                    down_sems.at[step % down_slots, side],
                )
                for side in range(2)
            ]

        for step in range(down_slots):
            for copy in fetch_down(step):
                copy.start()
    rows = mine_ref.shape[0]
    lhs_ref[:rows, :] = mine_ref[:, : 2 * size]
    lhs_ref[rows:, :] = other_ref[:, : 2 * size]
    depth = gate_ref.shape[2]
    parts = []
    for step, (expert, which) in enumerate(steps):
        for copy in fetch(step):
            copy.wait()
        value = jnp.dot(lhs_ref[...], ring_ref[step % slots], preferred_element_type=f32)
        if step + slots < len(steps):
            for copy in fetch(step + slots):
                copy.start()
        if not first:
            value = value + prior_ref[expert, which]
        if not last:
            acc_ref[expert, which] = value
            continue
        parts.append(value)
        if which == 1:
            gate_value, lifted = parts[-2:]
            value = gate_value / (1.0 + jnp.exp(-gate_value)) * lifted
            for at, ref in ((0, mine_ref), (rows, other_ref)):
                route = ref[:, 2 * size :].astype(f32)
                lane = lax.broadcasted_iota(jnp.int32, route.shape, 1)
                scale = jnp.sum(jnp.where(lane == group_ref[0] * EXP_G + expert, route, 0.0), 1, keepdims=True)
                hidden_ref[expert, at : at + rows, :] = (value[at : at + rows] * scale).astype(bf16)
    if not last:
        return
    places = []
    for far_ref, ref in ((keep_far_ref, keep_ref), (send_far_ref, send_ref)):
        for near in range(2):
            places += [(ref, near * (far - 1) + far - 2 - f) for f in range(far - 1)] + [(far_ref, near)]
    total = None
    for step, (chunk, expert) in enumerate(down_steps):
        for copy in fetch_down(step):
            copy.wait()
        part = jnp.dot(hidden_ref[expert], down_ring_ref[step % down_slots], preferred_element_type=f32)
        if step + down_slots < len(down_steps):
            for copy in fetch_down(step + down_slots):
                copy.start()
        if expert == 0:
            total = part
            continue
        total = total + part
        if expert < EXP_G - 1:
            continue
        columns = slice(chunk * column, (chunk + 1) * column)
        for pair in range(len(places) // 2):
            block = total[pair * unit : (pair + 1) * unit]
            packed = pack_pair(block[:, :column], block[:, column:])
            for (ref, place), pieces in zip(places[2 * pair : 2 * pair + 2], packed, strict=True):
                ref[place * unit : (place + 1) * unit, columns] = jnp.concatenate(pieces, 0).astype(bf16)


def expert_step(mine, other, unit, start, size, group, prior, w_gate, w_up, w_down):
    first, last = prior is None, group is not None
    rows = 2 * mine.shape[0]
    far = rows // unit // 2
    depth = w_gate.shape[2]
    vmem = pl.BlockSpec(memory_space=pltpu.VMEM)
    hbm = pl.BlockSpec(memory_space=pl.ANY)
    smem = pl.BlockSpec(memory_space=pltpu.SMEM)
    scratch = [
        pltpu.VMEM((rows, 2 * size), bf16),
        pltpu.VMEM((RING, 2 * size, depth), bf16),
        pltpu.SemaphoreType.DMA((RING, 2)),
    ]
    args = [mine, other, *([group] if last else []), *([] if first else [prior]), w_gate, w_up]
    specs = [vmem] * 2 + [smem] * last + [vmem] * (not first) + [hbm, hbm]
    if last:
        args.append(w_down)
        specs.append(hbm)
        half = w_down.shape[2] // 2
        column = half // DOWN_CHUNKS
        few, many = (2 * unit, half), (2 * (far - 1) * unit, half)
        shapes = [jax.ShapeDtypeStruct(shape, bf16) for shape in (few, few, many, many)]
        scratch += [
            pltpu.VMEM((EXP_G, rows, depth), bf16),
            pltpu.VMEM((DOWN_RING, depth, 2 * column), bf16),
            pltpu.SemaphoreType.DMA((DOWN_RING, 2)),
        ]
    else:
        shapes = [jax.ShapeDtypeStruct((EXP_G, 2, rows, depth), f32)]
    return pl.pallas_call(
        functools.partial(expert_kernel, unit, far, start, size, first, last),
        out_shape=shapes,
        in_specs=specs,
        out_specs=[vmem] * len(shapes),
        scratch_shapes=scratch,
        compiler_params=pltpu.CompilerParams(vmem_limit_bytes=VMEM_LIMIT),
        cost_estimate=STEP_COST,
    )(*args)


def call_small(kernel, shapes, args, scratch=(), after=()):
    vmem = pl.BlockSpec(memory_space=pltpu.VMEM)

    def body(*refs):
        kernel(*refs[: len(args)], *refs[len(args) + len(after) :])

    return pl.pallas_call(
        body,
        out_shape=shapes,
        in_specs=[vmem] * len(args) + [pl.BlockSpec(memory_space=pl.ANY)] * len(after),
        out_specs=jax.tree.map(lambda _: vmem, shapes),
        scratch_shapes=list(scratch),
        compiler_params=pltpu.CompilerParams(vmem_limit_bytes=VMEM_LIMIT),
        cost_estimate=SMALL_COST,
    )(*args, *after)


def add_far(keep, got, cut):
    def kernel(keep_ref, got_ref, mine_ref, first_ref, second_ref):
        unit = mine_ref.shape[0]
        total = keep_ref[...].astype(f32) + got_ref[...].astype(f32)
        mine_ref[...] = total[:unit].astype(bf16)
        first_ref[...] = total[unit:, :cut].astype(bf16)
        second_ref[...] = total[unit:, cut:].astype(bf16)

    unit, half = keep.shape[0] // 2, keep.shape[1]
    shapes = [jax.ShapeDtypeStruct((unit, size), bf16) for size in (half, cut, half - cut)]
    return call_small(kernel, shapes, (keep, got))


def add_rest(keep, got, unit, after):
    few = keep.shape[0] // (2 * unit)

    def kernel(keep_ref, got_ref, mine_ref, *near_refs):
        total = keep_ref[...].astype(f32) + got_ref[...].astype(f32)
        mine_ref[...] = total[: few * unit].astype(bf16)
        for i, ref in enumerate(near_refs):
            ref[...] = total[(few + i) * unit : (few + i + 1) * unit].astype(bf16)

    shapes = [jax.ShapeDtypeStruct((rows, keep.shape[1]), bf16) for rows in [few * unit] + [unit] * few]
    mine, *nears = call_small(kernel, shapes, (keep, got), after=after)
    return mine, nears


def add_one(keep, number, columns, got):
    unit = got.shape[0]

    def kernel(keep_ref, got_ref, out_ref):
        kept = keep_ref[number * unit : (number + 1) * unit, columns]
        out_ref[...] = (kept.astype(f32) + got_ref[...].astype(f32)).astype(bf16)

    return call_small(kernel, jax.ShapeDtypeStruct(got.shape, bf16), (keep, got))


def finish(keep, got, wholes, first, second, rows):
    unit, half = got.shape
    cut = first.shape[1]
    padded = -(-rows // TILE) * TILE
    full = rows // TILE * TILE

    def kernel(keep_ref, *refs):
        first_ref, second_ref, out_ref, rows_ref = refs[-4:]
        for columns, part_ref in ((slice(0, cut), first_ref), (slice(cut, half), second_ref)):
            total = keep_ref[keep_ref.shape[0] - unit :, columns].astype(f32) + part_ref[...].astype(f32)
            for ref in refs[:-4]:
                total = total + ref[:, columns].astype(f32)
            a, b = columns, slice(half + columns.start, half + columns.stop)
            rest = total[2 * full :]
            rows_ref[:full, a] = total[:full]
            rows_ref[:full, b] = total[full : 2 * full]
            rows_ref[full:, a] = rest
            rows_ref[full:, b] = half_roll(rest)
        out_ref[...] = rows_ref[0:rows, :].astype(bf16)

    return call_small(
        kernel,
        jax.ShapeDtypeStruct((rows, 2 * half), bf16),
        (keep, got, *wholes, first, second),
        [pltpu.VMEM((padded, 2 * half), f32)],
    )


def local(tokens, expert_ids, gates, w_gate, w_up, w_down):
    count = lax.axis_size("wide")
    group_size = count // GROUPS
    far = count // 4
    rows, width = tokens.shape
    unit, half = 2 * rows, width // 2
    cut = half // 2 // (2 * LANES) * (2 * LANES)
    group = (lax.axis_index("wide") // group_size).astype(jnp.int32).reshape(1)

    whole, first, second = prepare(tokens, expert_ids, gates, cut)
    wholes = [whole] + [swap(whole, 4 * f, count) for f in range(1, far - 1)]
    first = swap(first, 4 * (far - 1), count)
    second = swap(second, 4 * (far - 1), count)
    nexts = [swap(stack(wholes[:2]), 2, count)] + [swap(block, 2, count) for block in wholes[2:]]
    first_next = swap(first, 2, count)
    second_next = swap(second, 2, count)

    def rows_of(last, last_next, start, size, routes):
        arrays = [*wholes, last, *nexts, last_next]
        places = [(i, 0) for i in range(far)] + [(far, 0), (far, 1)] + [(i, 0) for i in range(far + 1, len(arrays))]
        places = [(*p, *((0, size) if arrays[p[0]].shape[1] < half else (start, half))) for p in places]
        return unpack(arrays, unit, [(*p[:3], p[3] if routes else None) for p in places], size)

    mine = rows_of(first, first_next, 0, cut, False)
    other = swap(mine, 1, count)
    state = expert_step(mine, other, unit, 0, cut, None, None, w_gate, w_up, None)[0]
    mine = rows_of(second, second_next, cut, half - cut, True)
    other = swap(mine, 1, count)
    keep_far, send_far, keep, send = expert_step(
        mine, other, unit, cut, half - cut, group, state, w_gate, w_up, w_down
    )

    mine, *nears = add_far(keep_far, swap(send_far, 1, count), cut)
    last_far = []
    for near, columns in zip(nears, (slice(0, cut), slice(cut, half)), strict=True):
        got = swap(near, 2, count)
        last_far.append(swap(add_one(mine, 0, columns, got), 4 * (far - 1), count))
        if len(last_far) == 1:
            after = got
    mine, nears = add_rest(keep, swap(send, 1, count), unit, [after])
    parts = []
    for i, near in enumerate(nears):
        got = swap(near, 2, count)
        if i < far - 2:
            parts.append(swap(add_one(mine, i, slice(0, half), got), 4 * (far - 2 - i), count))
    return finish(mine, got, parts, *last_far, rows)


def solution(mesh):
    return jax.shard_map(
        local,
        mesh=mesh,
        in_specs=(
            P(("parts", "wide"), None),
            P(("parts", "wide"), None),
            P(("parts", "wide"), None),
            P(None, None, "wide"),
            P(None, None, "wide"),
            P(None, "wide", None),
        ),
        out_specs=P(("parts", "wide"), None),
        check_vma=False,
    )
```

time: 192 us -> 80.9 us (0.42)
  the two profiles are of different devices: /device:TPU:13 before, /device:TPU:0 now
where the time goes in v3:
time: 80.9 us; the launch traced here: 80.7 us
  waiting for transfers between devices  31.3 us (39%)
  starting transfers between devices  26.7 us (33%)
  Pallas kernels  21.6 us (27%)
  local copies, waits for them, and re-layouts  0.92 us (1%)
    ppermute x21, waiting for transfers between devices, swap(): return lax.ppermute(block, 'wide', [(i, i ^ bits) for i in range(count)])  31.3 us
    ppermute x21, starting transfers between devices, swap(): return lax.ppermute(block, 'wide', [(i, i ^ bits) for i in range(count)])  26.7 us
    pallas_call x2, Pallas kernels, expert_step(): pl.pallas_call(functools.partial(expert_kernel, unit, far, start, size, f...  18.3 us
    pallas_call x1, Pallas kernels, prepare(): pl.pallas_call(prepare_kernel, out_shape=[jax.ShapeDtypeStruct((2 * rows,...  1.84 us
  transfers between devices with their start and end apart: 21, of which 13 were waited for; matrix products, arithmetic and copies ran while one was open for 0% of the time, Pallas kernels for 8%

profile of v3, /device:TPU:0, one launch (start us, length us, event | category | flops | bytes accessed | tf_op | source)
XLA Modules:
  0.0 80.7 jit_solution(203526565548270032)
XLA Ops:
  0.0 1.8 %shard_map.64 = (bf16[24,3712]{1,0:T(8,128)(2,1)}, bf16[24,1792]{1,0:T(8,128)(2,1)}, bf16[24,1920]{1,0:T(8,128)(2,1)}) custom-call(bf16[12,7168]{1,0:T(8,128)(2,1)} %tokens_ref.1, s32[8,12]{1,0:T(8,128)} %bitcast.3, f32[8,12]{1,0:T(8,128)} %bitcast.4), custom_call_target="tpu_custom_call" | custom-call | tf_op jit(solution)/shard_map/pallas_call | solution.py:92
  1.8 3.0 %collective-permute-start = (bf16[24,3712]{1,0:T(8,128)(2,1)}, bf16[24,3712]{1,0:T(8,128)(2,1)S(1)}, u32[]{:S(2)}, u32[]{:S(2)}) collective-permute-start(bf16[24,3712]{1,0:T(8,128)(2,1)} %get-tuple-element.19.refs_0_), channel_id=1, source_target_pairs={{0,4},{1,5},{2,6},{3,7},{4,0},{5,1},{6,2},{7,3},{8,12},{9,13},{10,... | collective-permute-start | bytes 534536 | tf_op jit(solution)/shard_map/ppermute | solution.py:26
  4.9 2.6 %collective-permute-start.1 = (bf16[24,3712]{1,0:T(8,128)(2,1)}, bf16[24,3712]{1,0:T(8,128)(2,1)S(1)}, u32[]{:S(2)}, u32[]{:S(2)}) collective-permute-start(bf16[24,3712]{1,0:T(8,128)(2,1)} %get-tuple-element.19.refs_0_), channel_id=1, source_target_pairs={{0,8},{1,9},{2,10},{3,11},{4,12},{5,13},{6,14},{7,15},{8,0},{9,1},... | collective-permute-start | bytes 534536 | tf_op jit(solution)/shard_map/ppermute | solution.py:26
  7.5 5.8 %collective-permute-done.refs_1_ = bf16[24,3712]{1,0:T(8,128)(2,1)S(1)} collective-permute-done((bf16[24,3712]{1,0:T(8,128)(2,1)}, bf16[24,3712]{1,0:T(8,128)(2,1)S(1)}, u32[]{:S(2)}, u32[]{:S(2)}) %collective-permute-start) | collective-permute-done | bytes 178208 | tf_op jit(solution)/shard_map/ppermute | solution.py:26
  13.3 0.0 copy-start
  13.3 0.9 %copy-done = bf16[24,3712]{1,0:T(8,128)(2,1)S(1)} copy-done((bf16[24,3712]{1,0:T(8,128)(2,1)S(1)}, bf16[24,3712]{1,0:T(8,128)(2,1)}, u32[]{:S(2)}) %copy-start) | copy-done | bytes 178200
  14.2 1.8 %collective-permute-start.3 = (bf16[48,3712]{1,0:T(8,128)(2,1)S(1)}, bf16[48,3712]{1,0:T(8,128)(2,1)S(1)}, u32[]{:S(2)}, u32[]{:S(2)}) collective-permute-start(bf16[48,3712]{1,0:T(8,128)(2,1)S(1)} %shard_map.65), channel_id=1, source_target_pairs={{0,2},{1,3},{2,0},{3,1},{4,6},{5,7},{6,4},{7,5},{8,10},{9,11},{10,... | collective-permute-start | bytes 1069064 | tf_op jit(solution)/shard_map/ppermute | solution.py:26
  16.0 0.0 collective-permute-done.1.refs_2_
  16.0 1.4 %collective-permute-start.4 = (bf16[24,3712]{1,0:T(8,128)(2,1)S(1)}, bf16[24,3712]{1,0:T(8,128)(2,1)S(1)}, u32[]{:S(2)}, u32[]{:S(2)}) collective-permute-start(bf16[24,3712]{1,0:T(8,128)(2,1)S(1)} %collective-permute-done.1.refs_2_), channel_id=1, source_target_pairs={{0,2},{1,3},{2,0},{3,1},{4,6},{5,7},{6,4},{7,5},{8,10},{9,11},{10,... | collective-permute-start | bytes 534536 | tf_op jit(solution)/shard_map/ppermute | solution.py:26
  17.3 2.5 %collective-permute-start.7 = (bf16[24,1792]{1,0:T(8,128)(2,1)}, bf16[24,1792]{1,0:T(8,128)(2,1)S(1)}, u32[]{:S(2)}, u32[]{:S(2)}) collective-permute-start(bf16[24,1792]{1,0:T(8,128)(2,1)} %get-tuple-element.21), channel_id=1, source_target_pairs={{0,12},{1,13},{2,14},{3,15},{4,8},{5,9},{6,10},{7,11},{8,4},{9,5},... | collective-permute-start | bytes 258056 | tf_op jit(solution)/shard_map/ppermute | solution.py:26
  19.8 1.4 %collective-permute-start.2 = (bf16[24,1920]{1,0:T(8,128)(2,1)}, bf16[24,1920]{1,0:T(8,128)(2,1)S(1)}, u32[]{:S(2)}, u32[]{:S(2)}) collective-permute-start(bf16[24,1920]{1,0:T(8,128)(2,1)} %get-tuple-element.20), channel_id=1, source_target_pairs={{0,12},{1,13},{2,14},{3,15},{4,8},{5,9},{6,10},{7,11},{8,4},{9,5},... | collective-permute-start | bytes 276488 | tf_op jit(solution)/shard_map/ppermute | solution.py:26
  21.2 2.7 %collective-permute-done.7.refs_3_ = bf16[24,1792]{1,0:T(8,128)(2,1)S(1)} collective-permute-done((bf16[24,1792]{1,0:T(8,128)(2,1)}, bf16[24,1792]{1,0:T(8,128)(2,1)S(1)}, u32[]{:S(2)}, u32[]{:S(2)}) %collective-permute-start.7) | collective-permute-done | bytes 86048 | tf_op jit(solution)/shard_map/ppermute | solution.py:26
  23.9 1.3 %collective-permute-start.8 = (bf16[24,1792]{1,0:T(8,128)(2,1)S(1)}, bf16[24,1792]{1,0:T(8,128)(2,1)S(1)}, u32[]{:S(2)}, u32[]{:S(2)}) collective-permute-start(bf16[24,1792]{1,0:T(8,128)(2,1)S(1)} %collective-permute-done.7.refs_3_), channel_id=1, source_target_pairs={{0,2},{1,3},{2,0},{3,1},{4,6},{5,7},{6,4},{7,5},{8,10},{9,11},{10,... | collective-permute-start | bytes 258056 | tf_op jit(solution)/shard_map/ppermute | solution.py:26
  25.2 1.1 %collective-permute-done.2.refs_3_ = bf16[24,1920]{1,0:T(8,128)(2,1)S(1)} collective-permute-done((bf16[24,1920]{1,0:T(8,128)(2,1)}, bf16[24,1920]{1,0:T(8,128)(2,1)S(1)}, u32[]{:S(2)}, u32[]{:S(2)}) %collective-permute-start.2) | collective-permute-done | bytes 92192 | tf_op jit(solution)/shard_map/ppermute | solution.py:26
  26.4 0.7 collective-permute-start.5
  27.1 2.7 %collective-permute-done.8.refs_6_ = bf16[24,1792]{1,0:T(8,128)(2,1)S(1)} collective-permute-done((bf16[24,1792]{1,0:T(8,128)(2,1)S(1)}, bf16[24,1792]{1,0:T(8,128)(2,1)S(1)}, u32[]{:S(2)}, u32[]{:S(2)}) %collective-permute-start.8) | collective-permute-done | bytes 86048 | tf_op jit(solution)/shard_map/ppermute | solution.py:26
  29.7 0.0 collective-permute-done.4.refs_5_
  29.8 0.0 collective-permute-done.3.refs_4_
  29.8 0.1 shard_map.67.refs_0_
  29.8 0.1 collective-permute-start.9
  29.9 1.0 %collective-permute-done.5.refs_6_ = bf16[24,1920]{1,0:T(8,128)(2,1)S(1)} collective-permute-done((bf16[24,1920]{1,0:T(8,128)(2,1)S(1)}, bf16[24,1920]{1,0:T(8,128)(2,1)S(1)}, u32[]{:S(2)}, u32[]{:S(2)}) %collective-permute-start.5) | collective-permute-done | bytes 92192 | tf_op jit(solution)/shard_map/ppermute | solution.py:26
  30.9 0.1 shard_map.66.refs_0_
  31.0 0.1 collective-permute-start.6
  31.1 1.0 %collective-permute-done.9.refs_1_ = bf16[96,3584]{1,0:T(8,128)(2,1)S(1)} collective-permute-done((bf16[96,3584]{1,0:T(8,128)(2,1)S(1)}, bf16[96,3584]{1,0:T(8,128)(2,1)S(1)}, u32[]{:S(2)}, u32[]{:S(2)}) %collective-permute-start.9) | collective-permute-done | bytes 688160 | tf_op jit(solution)/shard_map/ppermute | solution.py:26
  32.0 6.2 %shard_map.68.refs_3_ = f32[2,2,192,512]{3,2,1,0:T(8,128)S(1)} custom-call(bf16[96,3584]{1,0:T(8,128)(2,1)S(1)} %shard_map.67.refs_0_, bf16[96,3584]{1,0:T(8,128)(2,1)S(1)} %collective-permute-done.9.refs_1_, bf16[2,7168,512]{2,1,0:T(8,128)(2,1)} %refs_4_.1, bf16[2,7168,512]{2,1,0:T(8,128)(2,1)} %refs_5_.1), custom_call_target="tpu_custom_call" | custom-call | flops 536870912 | bytes 1 | tf_op jit(solution)/shard_map/pallas_call | solution.py:282
  38.2 0.0 collective-permute-done.6.refs_1_
  38.3 12.1 %shard_map.69 = (bf16[48,3584]{1,0:T(8,128)(2,1)S(1)}, bf16[48,3584]{1,0:T(8,128)(2,1)S(1)}, bf16[144,3584]{1,0:T(8,128)(2,1)S(1)}, bf16[144,3584]{1,0:T(8,128)(2,1)S(1)}) custom-call(bf16[96,3712]{1,0:T(8,128)(2,1)S(1)} %shard_map.66.refs_0_, bf16[96,3712]{1,0:T(8,128)(2,1)S(1)} %collective-permute-done.6.refs_1_, s32[1]{0:T(128)} %bitcast.2.refs_2_, ...), custom_call_target="tpu_custom_call" | custom-call | flops 536870912 | bytes 1 | tf_op jit(solution)/shard_map/pallas_call | solution.py:282
  50.4 0.2 collective-permute-start.10
  50.6 0.4 collective-permute-start.11
  51.0 2.6 %collective-permute-done.11.refs_1_ = bf16[48,3584]{1,0:T(8,128)(2,1)S(1)} collective-permute-done((bf16[48,3584]{1,0:T(8,128)(2,1)S(1)}, bf16[48,3584]{1,0:T(8,128)(2,1)S(1)}, u32[]{:S(2)}, u32[]{:S(2)}) %collective-permute-start.11) | collective-permute-done | bytes 344096 | tf_op jit(solution)/shard_map/ppermute | solution.py:26
  53.6 0.1 shard_map.70
  53.7 1.3 %collective-permute-start.12 = (bf16[24,1792]{1,0:T(8,128)(2,1)S(1)}, bf16[24,1792]{1,0:T(8,128)(2,1)S(1)}, u32[]{:S(2)}, u32[]{:S(2)}) collective-permute-start(bf16[24,1792]{1,0:T(8,128)(2,1)S(1)} %get-tuple-element.26), channel_id=1, source_target_pairs={{0,2},{1,3},{2,0},{3,1},{4,6},{5,7},{6,4},{7,5},{8,10},{9,11},{10,... | collective-permute-start | bytes 258056 | tf_op jit(solution)/shard_map/ppermute | solution.py:26
  55.0 3.4 %collective-permute-done.12.refs_2_.refs_1_ = bf16[24,1792]{1,0:T(8,128)(2,1)S(1)} collective-permute-done((bf16[24,1792]{1,0:T(8,128)(2,1)S(1)}, bf16[24,1792]{1,0:T(8,128)(2,1)S(1)}, u32[]{:S(2)}, u32[]{:S(2)}) %collective-permute-start.12) | collective-permute-done | bytes 86048 | tf_op jit(solution)/shard_map/ppermute | solution.py:26
  58.3 0.0 collective-permute-done.10.refs_1_
  58.3 0.2 shard_map.71
  58.6 1.3 %collective-permute-start.14 = (bf16[24,3584]{1,0:T(8,128)(2,1)S(1)}, bf16[24,3584]{1,0:T(8,128)(2,1)S(1)}, u32[]{:S(2)}, u32[]{:S(2)}) collective-permute-start(bf16[24,3584]{1,0:T(8,128)(2,1)S(1)} %get-tuple-element.29), channel_id=1, source_target_pairs={{0,2},{1,3},{2,0},{3,1},{4,6},{5,7},{6,4},{7,5},{8,10},{9,11},{10,... | collective-permute-start | bytes 516104 | tf_op jit(solution)/shard_map/ppermute | solution.py:26
  59.9 0.8 %collective-permute-start.16 = (bf16[24,3584]{1,0:T(8,128)(2,1)S(1)}, bf16[24,3584]{1,0:T(8,128)(2,1)S(1)}, u32[]{:S(2)}, u32[]{:S(2)}) collective-permute-start(bf16[24,3584]{1,0:T(8,128)(2,1)S(1)} %get-tuple-element.30), channel_id=1, source_target_pairs={{0,2},{1,3},{2,0},{3,1},{4,6},{5,7},{6,4},{7,5},{8,10},{9,11},{10,... | collective-permute-start | bytes 516104 | tf_op jit(solution)/shard_map/ppermute | solution.py:26
  60.7 1.2 %collective-permute-start.19 = (bf16[24,1792]{1,0:T(8,128)(2,1)S(1)}, bf16[24,1792]{1,0:T(8,128)(2,1)S(1)}, u32[]{:S(2)}, u32[]{:S(2)}) collective-permute-start(bf16[24,1792]{1,0:T(8,128)(2,1)S(1)} %get-tuple-element.32), channel_id=1, source_target_pairs={{0,2},{1,3},{2,0},{3,1},{4,6},{5,7},{6,4},{7,5},{8,10},{9,11},{10,... | collective-permute-start | bytes 258056 | tf_op jit(solution)/shard_map/ppermute | solution.py:26
  61.9 0.8 %collective-permute-start.13 = (bf16[24,3584]{1,0:T(8,128)(2,1)S(1)}, bf16[24,3584]{1,0:T(8,128)(2,1)S(1)}, u32[]{:S(2)}, u32[]{:S(2)}) collective-permute-start(bf16[24,3584]{1,0:T(8,128)(2,1)S(1)} %get-tuple-element.28), channel_id=1, source_target_pairs={{0,2},{1,3},{2,0},{3,1},{4,6},{5,7},{6,4},{7,5},{8,10},{9,11},{10,... | collective-permute-start | bytes 516104 | tf_op jit(solution)/shard_map/ppermute | solution.py:26
  62.7 3.3 %collective-permute-done.14.refs_1_ = bf16[24,3584]{1,0:T(8,128)(2,1)S(1)} collective-permute-done((bf16[24,3584]{1,0:T(8,128)(2,1)S(1)}, bf16[24,3584]{1,0:T(8,128)(2,1)S(1)}, u32[]{:S(2)}, u32[]{:S(2)}) %collective-permute-start.14) | collective-permute-done | bytes 172064 | tf_op jit(solution)/shard_map/ppermute | solution.py:26
  66.0 1.1 %collective-permute-start.15 = (bf16[24,3584]{1,0:T(8,128)(2,1)S(1)}, bf16[24,3584]{1,0:T(8,128)(2,1)S(1)}, u32[]{:S(2)}, u32[]{:S(2)}) collective-permute-start(bf16[24,3584]{1,0:T(8,128)(2,1)S(1)} %shard_map.72), channel_id=1, source_target_pairs={{0,8},{1,9},{2,10},{3,11},{4,12},{5,13},{6,14},{7,15},{8,0},{9,1},... | collective-permute-start | bytes 516104 | tf_op jit(solution)/shard_map/ppermute | solution.py:26
  67.2 2.5 %collective-permute-done.16.refs_1_ = bf16[24,3584]{1,0:T(8,128)(2,1)S(1)} collective-permute-done((bf16[24,3584]{1,0:T(8,128)(2,1)S(1)}, bf16[24,3584]{1,0:T(8,128)(2,1)S(1)}, u32[]{:S(2)}, u32[]{:S(2)}) %collective-permute-start.16) | collective-permute-done | bytes 172064 | tf_op jit(solution)/shard_map/ppermute | solution.py:26
  69.7 0.1 collective-permute-start.17
  69.8 3.1 %collective-permute-start.18 = (bf16[24,1792]{1,0:T(8,128)(2,1)S(1)}, bf16[24,1792]{1,0:T(8,128)(2,1)S(1)}, u32[]{:S(2)}, u32[]{:S(2)}) collective-permute-start(bf16[24,1792]{1,0:T(8,128)(2,1)S(1)} %shard_map.74), channel_id=1, source_target_pairs={{0,12},{1,13},{2,14},{3,15},{4,8},{5,9},{6,10},{7,11},{8,4},{9,5},... | collective-permute-start | bytes 258056 | tf_op jit(solution)/shard_map/ppermute | solution.py:26
  72.9 0.0 collective-permute-done.19.refs_1_
  72.9 1.7 %collective-permute-start.20 = (bf16[24,1792]{1,0:T(8,128)(2,1)S(1)}, bf16[24,1792]{1,0:T(8,128)(2,1)S(1)}, u32[]{:S(2)}, u32[]{:S(2)}) collective-permute-start(bf16[24,1792]{1,0:T(8,128)(2,1)S(1)} %shard_map.75), channel_id=1, source_target_pairs={{0,12},{1,13},{2,14},{3,15},{4,8},{5,9},{6,10},{7,11},{8,4},{9,5},... | collective-permute-start | bytes 258056 | tf_op jit(solution)/shard_map/ppermute | solution.py:26
  74.6 4.0 %collective-permute-done.18.refs_4_ = bf16[24,1792]{1,0:T(8,128)(2,1)S(1)} collective-permute-done((bf16[24,1792]{1,0:T(8,128)(2,1)S(1)}, bf16[24,1792]{1,0:T(8,128)(2,1)S(1)}, u32[]{:S(2)}, u32[]{:S(2)}) %collective-permute-start.18) | collective-permute-done | bytes 86048 | tf_op jit(solution)/shard_map/ppermute | solution.py:26
  78.7 0.9 %collective-permute-done.20.refs_5_ = bf16[24,1792]{1,0:T(8,128)(2,1)S(1)} collective-permute-done((bf16[24,1792]{1,0:T(8,128)(2,1)S(1)}, bf16[24,1792]{1,0:T(8,128)(2,1)S(1)}, u32[]{:S(2)}, u32[]{:S(2)}) %collective-permute-start.20) | collective-permute-done | bytes 86048 | tf_op jit(solution)/shard_map/ppermute | solution.py:26
  79.6 0.0 collective-permute-done.13.refs_1_
  79.6 0.0 collective-permute-done.15.refs_2_
  79.6 0.3 collective-permute-done.17.refs_3_
  79.9 0.8 %shard_map.76 = bf16[12,7168]{1,0:T(8,128)(2,1)} custom-call(bf16[72,3584]{1,0:T(8,128)(2,1)S(1)} %get-tuple-element.27.refs_0_, bf16[24,3584]{1,0:T(8,128)(2,1)S(1)} %collective-permute-done.13.refs_1_, bf16[24,3584]{1,0:T(8,128)(2,1)S(1)} %collective-permute-done.15.refs_2_, bf16[24,3584]{1,0:T(8,128)(2,1)S(1)} %collective-permute-done.17.refs_3_, ...), custom_call_target="tpu_custom_call" | custom-call | flops 1 | bytes 1 | tf_op jit(solution)/shard_map/pallas_call | solution.py:299
  (5 shorter events, 0.2 us)
Async XLA Ops:
  1.8 11.4 %collective-permute-start = (bf16[24,3712]{1,0:T(8,128)(2,1)}, bf16[24,3712]{1,0:T(8,128)(2,1)S(1)}, u32[]{:S(2)}, u32[]{:S(2)}) collective-permute-start(bf16[24,3712]{1,0:T(8,128)(2,1)} %get-tuple-element.19.refs_0_), channel_id=1, source_target_pairs={{0,4},{1,5},{2,6},{3,7},{4,0},{5,1},{6,2},{7,3},{8,12},{9,13},{10,... | collective-permute-start | bytes 534536 | tf_op jit(solution)/shard_map/ppermute | solution.py:26
  4.9 11.1 %collective-permute-start.1 = (bf16[24,3712]{1,0:T(8,128)(2,1)}, bf16[24,3712]{1,0:T(8,128)(2,1)S(1)}, u32[]{:S(2)}, u32[]{:S(2)}) collective-permute-start(bf16[24,3712]{1,0:T(8,128)(2,1)} %get-tuple-element.19.refs_0_), channel_id=1, source_target_pairs={{0,8},{1,9},{2,10},{3,11},{4,12},{5,13},{6,14},{7,15},{8,0},{9,1},... | collective-permute-start | bytes 534536 | tf_op jit(solution)/shard_map/ppermute | solution.py:26
  13.3 0.9 %copy-start = (bf16[24,3712]{1,0:T(8,128)(2,1)S(1)}, bf16[24,3712]{1,0:T(8,128)(2,1)}, u32[]{:S(2)}) copy-start(bf16[24,3712]{1,0:T(8,128)(2,1)} %get-tuple-element.19.refs_0_) | copy-start | bytes 534532
  14.2 15.5 %collective-permute-start.3 = (bf16[48,3712]{1,0:T(8,128)(2,1)S(1)}, bf16[48,3712]{1,0:T(8,128)(2,1)S(1)}, u32[]{:S(2)}, u32[]{:S(2)}) collective-permute-start(bf16[48,3712]{1,0:T(8,128)(2,1)S(1)} %shard_map.65), channel_id=1, source_target_pairs={{0,2},{1,3},{2,0},{3,1},{4,6},{5,7},{6,4},{7,5},{8,10},{9,11},{10,... | collective-permute-start | bytes 1069064 | tf_op jit(solution)/shard_map/ppermute | solution.py:26
  16.0 13.8 %collective-permute-start.4 = (bf16[24,3712]{1,0:T(8,128)(2,1)S(1)}, bf16[24,3712]{1,0:T(8,128)(2,1)S(1)}, u32[]{:S(2)}, u32[]{:S(2)}) collective-permute-start(bf16[24,3712]{1,0:T(8,128)(2,1)S(1)} %collective-permute-done.1.refs_2_), channel_id=1, source_target_pairs={{0,2},{1,3},{2,0},{3,1},{4,6},{5,7},{6,4},{7,5},{8,10},{9,11},{10,... | collective-permute-start | bytes 534536 | tf_op jit(solution)/shard_map/ppermute | solution.py:26
  17.3 6.5 %collective-permute-start.7 = (bf16[24,1792]{1,0:T(8,128)(2,1)}, bf16[24,1792]{1,0:T(8,128)(2,1)S(1)}, u32[]{:S(2)}, u32[]{:S(2)}) collective-permute-start(bf16[24,1792]{1,0:T(8,128)(2,1)} %get-tuple-element.21), channel_id=1, source_target_pairs={{0,12},{1,13},{2,14},{3,15},{4,8},{5,9},{6,10},{7,11},{8,4},{9,5},... | collective-permute-start | bytes 258056 | tf_op jit(solution)/shard_map/ppermute | solution.py:26
  19.8 6.6 %collective-permute-start.2 = (bf16[24,1920]{1,0:T(8,128)(2,1)}, bf16[24,1920]{1,0:T(8,128)(2,1)S(1)}, u32[]{:S(2)}, u32[]{:S(2)}) collective-permute-start(bf16[24,1920]{1,0:T(8,128)(2,1)} %get-tuple-element.20), channel_id=1, source_target_pairs={{0,12},{1,13},{2,14},{3,15},{4,8},{5,9},{6,10},{7,11},{8,4},{9,5},... | collective-permute-start | bytes 276488 | tf_op jit(solution)/shard_map/ppermute | solution.py:26
  23.9 5.9 %collective-permute-start.8 = (bf16[24,1792]{1,0:T(8,128)(2,1)S(1)}, bf16[24,1792]{1,0:T(8,128)(2,1)S(1)}, u32[]{:S(2)}, u32[]{:S(2)}) collective-permute-start(bf16[24,1792]{1,0:T(8,128)(2,1)S(1)} %collective-permute-done.7.refs_3_), channel_id=1, source_target_pairs={{0,2},{1,3},{2,0},{3,1},{4,6},{5,7},{6,4},{7,5},{8,10},{9,11},{10,... | collective-permute-start | bytes 258056 | tf_op jit(solution)/shard_map/ppermute | solution.py:26
  26.4 4.6 %collective-permute-start.5 = (bf16[24,1920]{1,0:T(8,128)(2,1)S(1)}, bf16[24,1920]{1,0:T(8,128)(2,1)S(1)}, u32[]{:S(2)}, u32[]{:S(2)}) collective-permute-start(bf16[24,1920]{1,0:T(8,128)(2,1)S(1)} %collective-permute-done.2.refs_3_), channel_id=1, source_target_pairs={{0,2},{1,3},{2,0},{3,1},{4,6},{5,7},{6,4},{7,5},{8,10},{9,11},{10,... | collective-permute-start | bytes 276488 | tf_op jit(solution)/shard_map/ppermute | solution.py:26
  29.8 2.2 %collective-permute-start.9 = (bf16[96,3584]{1,0:T(8,128)(2,1)S(1)}, bf16[96,3584]{1,0:T(8,128)(2,1)S(1)}, u32[]{:S(2)}, u32[]{:S(2)}) collective-permute-start(bf16[96,3584]{1,0:T(8,128)(2,1)S(1)} %shard_map.67.refs_0_), channel_id=1, source_target_pairs={{0,1},{1,0},{2,3},{3,2},{4,5},{5,4},{6,7},{7,6},{8,9},{9,8},{10,11... | collective-permute-start | bytes 2064392 | tf_op jit(solution)/shard_map/ppermute | solution.py:26
  31.0 7.3 %collective-permute-start.6 = (bf16[96,3712]{1,0:T(8,128)(2,1)S(1)}, bf16[96,3712]{1,0:T(8,128)(2,1)S(1)}, u32[]{:S(2)}, u32[]{:S(2)}) collective-permute-start(bf16[96,3712]{1,0:T(8,128)(2,1)S(1)} %shard_map.66.refs_0_), channel_id=1, source_target_pairs={{0,1},{1,0},{2,3},{3,2},{4,5},{5,4},{6,7},{7,6},{8,9},{9,8},{10,11... | collective-permute-start | bytes 2138120 | tf_op jit(solution)/shard_map/ppermute | solution.py:26
  50.4 7.9 %collective-permute-start.10 = (bf16[144,3584]{1,0:T(8,128)(2,1)S(1)}, bf16[144,3584]{1,0:T(8,128)(2,1)S(1)}, u32[]{:S(2)}, u32[]{:S(2)}) collective-permute-start(bf16[144,3584]{1,0:T(8,128)(2,1)S(1)} %get-tuple-element.23), channel_id=1, source_target_pairs={{0,1},{1,0},{2,3},{3,2},{4,5},{5,4},{6,7},{7,6},{8,9},{9,8},{10,11... | collective-permute-start | bytes 3096584 | tf_op jit(solution)/shard_map/ppermute | solution.py:26
  50.6 3.0 %collective-permute-start.11 = (bf16[48,3584]{1,0:T(8,128)(2,1)S(1)}, bf16[48,3584]{1,0:T(8,128)(2,1)S(1)}, u32[]{:S(2)}, u32[]{:S(2)}) collective-permute-start(bf16[48,3584]{1,0:T(8,128)(2,1)S(1)} %get-tuple-element.25), channel_id=1, source_target_pairs={{0,1},{1,0},{2,3},{3,2},{4,5},{5,4},{6,7},{7,6},{8,9},{9,8},{10,11... | collective-permute-start | bytes 1032200 | tf_op jit(solution)/shard_map/ppermute | solution.py:26
  53.7 4.7 %collective-permute-start.12 = (bf16[24,1792]{1,0:T(8,128)(2,1)S(1)}, bf16[24,1792]{1,0:T(8,128)(2,1)S(1)}, u32[]{:S(2)}, u32[]{:S(2)}) collective-permute-start(bf16[24,1792]{1,0:T(8,128)(2,1)S(1)} %get-tuple-element.26), channel_id=1, source_target_pairs={{0,2},{1,3},{2,0},{3,1},{4,6},{5,7},{6,4},{7,5},{8,10},{9,11},{10,... | collective-permute-start | bytes 258056 | tf_op jit(solution)/shard_map/ppermute | solution.py:26
  58.6 7.4 %collective-permute-start.14 = (bf16[24,3584]{1,0:T(8,128)(2,1)S(1)}, bf16[24,3584]{1,0:T(8,128)(2,1)S(1)}, u32[]{:S(2)}, u32[]{:S(2)}) collective-permute-start(bf16[24,3584]{1,0:T(8,128)(2,1)S(1)} %get-tuple-element.29), channel_id=1, source_target_pairs={{0,2},{1,3},{2,0},{3,1},{4,6},{5,7},{6,4},{7,5},{8,10},{9,11},{10,... | collective-permute-start | bytes 516104 | tf_op jit(solution)/shard_map/ppermute | solution.py:26
  59.9 9.8 %collective-permute-start.16 = (bf16[24,3584]{1,0:T(8,128)(2,1)S(1)}, bf16[24,3584]{1,0:T(8,128)(2,1)S(1)}, u32[]{:S(2)}, u32[]{:S(2)}) collective-permute-start(bf16[24,3584]{1,0:T(8,128)(2,1)S(1)} %get-tuple-element.30), channel_id=1, source_target_pairs={{0,2},{1,3},{2,0},{3,1},{4,6},{5,7},{6,4},{7,5},{8,10},{9,11},{10,... | collective-permute-start | bytes 516104 | tf_op jit(solution)/shard_map/ppermute | solution.py:26
  60.7 12.2 %collective-permute-start.19 = (bf16[24,1792]{1,0:T(8,128)(2,1)S(1)}, bf16[24,1792]{1,0:T(8,128)(2,1)S(1)}, u32[]{:S(2)}, u32[]{:S(2)}) collective-permute-start(bf16[24,1792]{1,0:T(8,128)(2,1)S(1)} %get-tuple-element.32), channel_id=1, source_target_pairs={{0,2},{1,3},{2,0},{3,1},{4,6},{5,7},{6,4},{7,5},{8,10},{9,11},{10,... | collective-permute-start | bytes 258056 | tf_op jit(solution)/shard_map/ppermute | solution.py:26
  61.9 17.7 %collective-permute-start.13 = (bf16[24,3584]{1,0:T(8,128)(2,1)S(1)}, bf16[24,3584]{1,0:T(8,128)(2,1)S(1)}, u32[]{:S(2)}, u32[]{:S(2)}) collective-permute-start(bf16[24,3584]{1,0:T(8,128)(2,1)S(1)} %get-tuple-element.28), channel_id=1, source_target_pairs={{0,2},{1,3},{2,0},{3,1},{4,6},{5,7},{6,4},{7,5},{8,10},{9,11},{10,... | collective-permute-start | bytes 516104 | tf_op jit(solution)/shard_map/ppermute | solution.py:26
  66.0 13.6 %collective-permute-start.15 = (bf16[24,3584]{1,0:T(8,128)(2,1)S(1)}, bf16[24,3584]{1,0:T(8,128)(2,1)S(1)}, u32[]{:S(2)}, u32[]{:S(2)}) collective-permute-start(bf16[24,3584]{1,0:T(8,128)(2,1)S(1)} %shard_map.72), channel_id=1, source_target_pairs={{0,8},{1,9},{2,10},{3,11},{4,12},{5,13},{6,14},{7,15},{8,0},{9,1},... | collective-permute-start | bytes 516104 | tf_op jit(solution)/shard_map/ppermute | solution.py:26
  69.7 10.2 %collective-permute-start.17 = (bf16[24,3584]{1,0:T(8,128)(2,1)S(1)}, bf16[24,3584]{1,0:T(8,128)(2,1)S(1)}, u32[]{:S(2)}, u32[]{:S(2)}) collective-permute-start(bf16[24,3584]{1,0:T(8,128)(2,1)S(1)} %shard_map.73), channel_id=1, source_target_pairs={{0,4},{1,5},{2,6},{3,7},{4,0},{5,1},{6,2},{7,3},{8,12},{9,13},{10,... | collective-permute-start | bytes 516104 | tf_op jit(solution)/shard_map/ppermute | solution.py:26
  69.8 8.8 %collective-permute-start.18 = (bf16[24,1792]{1,0:T(8,128)(2,1)S(1)}, bf16[24,1792]{1,0:T(8,128)(2,1)S(1)}, u32[]{:S(2)}, u32[]{:S(2)}) collective-permute-start(bf16[24,1792]{1,0:T(8,128)(2,1)S(1)} %shard_map.74), channel_id=1, source_target_pairs={{0,12},{1,13},{2,14},{3,15},{4,8},{5,9},{6,10},{7,11},{8,4},{9,5},... | collective-permute-start | bytes 258056 | tf_op jit(solution)/shard_map/ppermute | solution.py:26
  72.9 6.6 %collective-permute-start.20 = (bf16[24,1792]{1,0:T(8,128)(2,1)S(1)}, bf16[24,1792]{1,0:T(8,128)(2,1)S(1)}, u32[]{:S(2)}, u32[]{:S(2)}) collective-permute-start(bf16[24,1792]{1,0:T(8,128)(2,1)S(1)} %shard_map.75), channel_id=1, source_target_pairs={{0,12},{1,13},{2,14},{3,15},{4,8},{5,9},{6,10},{7,11},{8,4},{9,5},... | collective-permute-start | bytes 258056 | tf_op jit(solution)/shard_map/ppermute | solution.py:26

commit v4 on v3

v4 whole, which is shorter than its diff:
```python
import functools

import jax
import jax.numpy as jnp
from jax import lax
from jax.experimental import pallas as pl
from jax.experimental.pallas import tpu as pltpu
from jax.sharding import PartitionSpec as P

GROUPS = 8
EXP_G = 2
LANES = 128
TILE = 8
MIB = 1 << 20
DOWN_CHUNKS = 4
SMALL_VMEM = 8 * MIB
PREPARE_VMEM = 58 * MIB
FIRST_VMEM = 36 * MIB
STEP_VMEM = 14 * MIB
DOWN_RING = 4
SMALL_COST = pl.CostEstimate(flops=1, bytes_accessed=1, transcendentals=0)
LOAD_COST = pl.CostEstimate(flops=1, bytes_accessed=1 << 24, transcendentals=0)
STEP_COST = pl.CostEstimate(flops=1 << 29, bytes_accessed=1, transcendentals=0)
bf16 = jnp.bfloat16
f32 = jnp.float32


def swap(block, bits, count):
    return lax.ppermute(block, "wide", [(i, i ^ bits) for i in range(count)])


def half_roll(block):
    return pltpu.roll(block, TILE // 2, 0)


def low_half(shape):
    return lax.broadcasted_iota(jnp.int32, shape, 0) < TILE // 2


def unpack_pair(u, v):
    full = (u.shape[0] - TILE) // 2
    u_rest, v_rest = u[2 * full :], v[2 * full :]
    low = low_half(u_rest.shape)
    a = [u[:full], v[:full], jnp.where(low, u_rest, half_roll(v_rest))]
    b = [u[full : 2 * full], v[full : 2 * full], jnp.where(low, half_roll(u_rest), v_rest)]
    return a, b


def pack_pair(a, b):
    full = (a.shape[0] - TILE) // 2
    a_rest, b_rest = a[2 * full :], b[2 * full :]
    low = low_half(a_rest.shape)
    u = [a[:full], b[:full], jnp.where(low, a_rest, half_roll(b_rest))]
    v = [a[full : 2 * full], b[full : 2 * full], jnp.where(low, half_roll(a_rest), b_rest)]
    return u, v


def pack_columns(rows_ref, a, b):
    full = rows_ref.shape[0] - TILE
    a_rest, b_rest = rows_ref[full:, a], rows_ref[full:, b]
    rest = jnp.where(low_half(a_rest.shape), a_rest, half_roll(b_rest))
    return jnp.concatenate([rows_ref[:full, a], rows_ref[:full, b], rest], 0).astype(bf16)


def prepare_kernel(tokens_hbm, ids_hbm, gates_hbm, out_ref, rows_ref, tokens_ref, ids_ref, gates_ref, sems):
    copies = [
        pltpu.make_async_copy(source, target, sems.at[i])
        for i, (source, target) in enumerate(
            ((tokens_hbm, tokens_ref), (ids_hbm, ids_ref), (gates_hbm, gates_ref))
        )
    ]
    for copy in copies:
        copy.start()
    for copy in copies:
        copy.wait()
    rows, width = tokens_ref.shape
    half = width // 2
    rows_ref[0:rows, :width] = tokens_ref[...].astype(f32)
    experts = GROUPS * EXP_G
    catalog = lax.broadcasted_iota(jnp.int32, (experts, rows), 0)
    weight = jnp.zeros((experts, rows), f32)
    for k in range(ids_ref.shape[0]):
        weight = weight + jnp.where(ids_ref[k : k + 1, :] == catalog, gates_ref[k : k + 1, :], 0.0)
    row = lax.broadcasted_iota(jnp.int32, (experts, LANES), 0)
    eye = (row == lax.broadcasted_iota(jnp.int32, (experts, LANES), 1)).astype(bf16)
    rows_ref[0:rows, width : width + LANES] = lax.dot_general(
        weight.astype(bf16), eye, (((0,), (0,)), ((), ())), preferred_element_type=f32
    )
    rows_ref[:, width + LANES :] = jnp.zeros((rows_ref.shape[0], LANES), f32)
    out_ref[:, :half] = pack_columns(rows_ref, slice(0, half), slice(half, width))
    out_ref[:, half:] = pack_columns(rows_ref, slice(width, width + LANES), slice(width + LANES, width + 2 * LANES))


def prepare(tokens, expert_ids, gates):
    rows, width = tokens.shape
    padded = -(-rows // TILE) * TILE
    args = (tokens, expert_ids.T, gates.T)
    return call_small(
        prepare_kernel,
        jax.ShapeDtypeStruct((2 * rows, width // 2 + LANES), bf16),
        (),
        [pltpu.VMEM((padded, width + 2 * LANES), f32)]
        + [pltpu.VMEM(a.shape, a.dtype) for a in args]
        + [pltpu.SemaphoreType.DMA((len(args),))],
        hbm=args,
        vmem_limit=PREPARE_VMEM,
    )


def preload(weights, vmem_limit):
    pieces = 4

    def kernel(source_ref, out_ref, sems):
        rows = weights.shape[1] // pieces
        copies = [
            pltpu.make_async_copy(
                source_ref.at[e, pl.ds(i * rows, rows), :], out_ref.at[e, pl.ds(i * rows, rows), :], sems.at[e, i]
            )
            for e in range(EXP_G)
            for i in range(pieces)
        ]
        for copy in copies:
            copy.start()
        for copy in copies:
            copy.wait()

    return call_small(
        kernel,
        jax.ShapeDtypeStruct(weights.shape, weights.dtype),
        (),
        [pltpu.SemaphoreType.DMA((EXP_G, pieces))],
        hbm=(weights,),
        cost=LOAD_COST,
        vmem_limit=vmem_limit,
    )


def unpack(blocks, unit):
    arrays = [array for array, _ in blocks]
    half = arrays[0].shape[1] - LANES

    def kernel(*refs):
        out_ref = refs[-1]
        values = [
            ref[number * unit : (number + 1) * unit, :].astype(f32)
            for ref, (_, number) in zip(refs[:-1], blocks, strict=True)
        ]
        pieces = []
        for i in (0, 2):
            a, b = unpack_pair(*values[i : i + 2])
            pieces.append((jnp.concatenate(a, 0), jnp.concatenate(b, 0)))
        rows_a, rows_b = (jnp.concatenate(part, 0) for part in zip(*pieces, strict=True))
        out_ref[:, :half] = rows_a[:, :half].astype(bf16)
        out_ref[:, half : 2 * half] = rows_b[:, :half].astype(bf16)
        out_ref[:, 2 * half :] = rows_a[:, half:].astype(bf16)

    shape = jax.ShapeDtypeStruct((len(blocks) * unit // 2, 2 * half + LANES), bf16)
    return call_small(kernel, shape, arrays)


def stack(arrays, *after):
    def kernel(*refs):
        at = 0
        for ref in refs[:-1]:
            refs[-1][at : at + ref.shape[0], :] = ref[...]
            at += ref.shape[0]

    rows = sum(a.shape[0] for a in arrays)
    return call_small(kernel, jax.ShapeDtypeStruct((rows, arrays[0].shape[1]), bf16), arrays, after=after)


def hold(block, *after, cost=None):
    return call_small(
        lambda block_ref, out_ref: out_ref.__setitem__(..., block_ref[...]),
        jax.ShapeDtypeStruct(block.shape, block.dtype),
        (block,),
        after=after,
        cost=cost or SMALL_COST,
    )


def expert_kernel(unit, far, count, *refs):
    blocks, refs = refs[:count], refs[count:]
    gate_ref, up_ref, down_ref, keep_far_ref, send_far_ref, keep_ref, send_ref = refs[:7]
    lhs_ref, hidden_ref, ring_ref, sems = refs[7:]
    width, depth = gate_ref.shape[1:]
    half = width // 2
    slots, column = ring_ref.shape[0], ring_ref.shape[2] // 2
    steps = [(chunk, expert) for chunk in range(half // column) for expert in range(EXP_G)]

    def fetch(step):
        chunk, expert = steps[step]
        return [
            pltpu.make_async_copy(
                down_ref.at[expert, :, pl.ds(side * half + chunk * column, column)],
                ring_ref.at[step % slots, :, pl.ds(side * column, column)],
                sems.at[step % slots, side],
            )
            for side in range(2)
        ]

    for step in range(slots):
        for copy in fetch(step):
            copy.start()
    at = 0
    scales = []
    group = lax.axis_index("wide") // (lax.axis_size("wide") // GROUPS)
    for ref in blocks:
        rows = slice(at, at + ref.shape[0])
        lhs_ref[rows, :] = ref[:, :width]
        route = ref[:, width:].astype(f32)
        lane = lax.broadcasted_iota(jnp.int32, route.shape, 1)
        scales.append(
            [
                jnp.sum(jnp.where(lane == group * EXP_G + expert, route, 0.0), 1, keepdims=True)
                for expert in range(EXP_G)
            ]
        )
        at = rows.stop
    for expert in range(EXP_G):
        gate_value = jnp.dot(lhs_ref[...], gate_ref[expert], preferred_element_type=f32)
        lifted = jnp.dot(lhs_ref[...], up_ref[expert], preferred_element_type=f32)
        value = gate_value / (1.0 + jnp.exp(-gate_value)) * lifted
        scale = jnp.concatenate([pair[expert] for pair in scales], 0)
        hidden_ref[expert] = (value * scale).astype(bf16)
    places = []
    for far_ref, ref in ((keep_far_ref, keep_ref), (send_far_ref, send_ref)):
        for first in range(0, far, 2):
            for near in range(2):
                for f in (first, first + 1):
                    places.append((far_ref, near) if f == far - 1 else (ref, near * (far - 1) + far - 2 - f))
    total = None
    for step, (chunk, expert) in enumerate(steps):
        for copy in fetch(step):
            copy.wait()
        part = jnp.dot(hidden_ref[expert], ring_ref[step % slots], preferred_element_type=f32)
        if step + slots < len(steps):
            for copy in fetch(step + slots):
                copy.start()
        if expert == 0:
            total = part
            continue
        total = total + part
        if expert < EXP_G - 1:
            continue
        columns = slice(chunk * column, (chunk + 1) * column)
        for pair in range(len(places) // 2):
            block = total[pair * unit : (pair + 1) * unit]
            packed = pack_pair(block[:, :column], block[:, column:])
            for (ref, place), parts in zip(places[2 * pair : 2 * pair + 2], packed, strict=True):
                ref[place * unit : (place + 1) * unit, columns] = jnp.concatenate(parts, 0).astype(bf16)


def expert_step(blocks, unit, w_gate, w_up, w_down):
    rows = sum(b.shape[0] for b in blocks)
    far = rows // unit // 2
    _, width, depth = w_up.shape
    half = width // 2
    column = half // DOWN_CHUNKS
    vmem = pl.BlockSpec(memory_space=pltpu.VMEM)
    few, many = (2 * unit, half), (2 * (far - 1) * unit, half)
    return pl.pallas_call(
        functools.partial(expert_kernel, unit, far, len(blocks)),
        out_shape=[jax.ShapeDtypeStruct(shape, bf16) for shape in (few, few, many, many)],
        in_specs=[vmem] * (len(blocks) + 2) + [pl.BlockSpec(memory_space=pl.ANY)],
        out_specs=[vmem] * 4,
        scratch_shapes=[
            pltpu.VMEM((rows, width), bf16),
            pltpu.VMEM((EXP_G, rows, depth), bf16),
            pltpu.VMEM((DOWN_RING, depth, 2 * column), bf16),
            pltpu.SemaphoreType.DMA((DOWN_RING, 2)),
        ],
        compiler_params=pltpu.CompilerParams(vmem_limit_bytes=STEP_VMEM),
        cost_estimate=STEP_COST,
    )(*blocks, w_gate, w_up, w_down)


def call_small(kernel, shapes, args, scratch=(), after=(), hbm=(), cost=SMALL_COST, vmem_limit=SMALL_VMEM):
    vmem = pl.BlockSpec(memory_space=pltpu.VMEM)
    count = len(args) + len(hbm)

    def body(*refs):
        kernel(*refs[:count], *refs[count + len(after) :])

    return pl.pallas_call(
        body,
        out_shape=shapes,
        in_specs=[vmem] * len(args) + [pl.BlockSpec(memory_space=pl.ANY)] * (len(hbm) + len(after)),
        out_specs=jax.tree.map(lambda _: vmem, shapes),
        scratch_shapes=list(scratch),
        compiler_params=pltpu.CompilerParams(vmem_limit_bytes=vmem_limit),
        cost_estimate=cost,
    )(*args, *hbm, *after)


def add_far(keep, got):
    unit = keep.shape[0] // 2

    def kernel(keep_ref, got_ref, mine_ref, near_ref):
        total = keep_ref[...].astype(f32) + got_ref[...].astype(f32)
        mine_ref[...] = total[:unit].astype(bf16)
        near_ref[...] = total[unit:].astype(bf16)

    return call_small(kernel, [jax.ShapeDtypeStruct((unit, keep.shape[1]), bf16)] * 2, (keep, got))


def add_rest(keep, got, unit, after):
    few = keep.shape[0] // (2 * unit)

    def kernel(keep_ref, got_ref, mine_ref, *near_refs):
        total = keep_ref[...].astype(f32) + got_ref[...].astype(f32)
        mine_ref[...] = total[: few * unit].astype(bf16)
        for i, ref in enumerate(near_refs):
            ref[...] = total[(few + i) * unit : (few + i + 1) * unit].astype(bf16)

    shapes = [jax.ShapeDtypeStruct((rows, keep.shape[1]), bf16) for rows in [few * unit] + [unit] * few]
    mine, *nears = call_small(kernel, shapes, (keep, got), after=after)
    return mine, nears


def add_one(keep, number, got, after=()):
    unit = got.shape[0]

    def kernel(keep_ref, got_ref, out_ref):
        kept = keep_ref[number * unit : (number + 1) * unit, :]
        out_ref[...] = (kept.astype(f32) + got_ref[...].astype(f32)).astype(bf16)

    return call_small(kernel, jax.ShapeDtypeStruct(got.shape, bf16), (keep, got), after=after)


def finish(keep, got, parts, rows):
    unit, half = got.shape
    padded = -(-rows // TILE) * TILE
    full = rows // TILE * TILE

    def kernel(keep_ref, *refs):
        out_ref, rows_ref = refs[-2:]
        total = keep_ref[keep_ref.shape[0] - unit :, :].astype(f32)
        for ref in refs[:-2]:
            total = total + ref[...].astype(f32)
        rest = total[2 * full :]
        rows_ref[:full, :half] = total[:full]
        rows_ref[:full, half:] = total[full : 2 * full]
        rows_ref[full:, :half] = rest
        rows_ref[full:, half:] = half_roll(rest)
        out_ref[...] = rows_ref[0:rows, :].astype(bf16)

    return call_small(
        kernel,
        jax.ShapeDtypeStruct((rows, 2 * half), bf16),
        (keep, got, *parts),
        [pltpu.VMEM((padded, 2 * half), f32)],
    )


def local(tokens, expert_ids, gates, w_gate, w_up, w_down):
    count = lax.axis_size("wide")
    far = count // 4
    rows, width = tokens.shape
    unit, half = 2 * rows, width // 2

    whole = prepare(tokens, expert_ids, gates)
    blocks = [whole] + [swap(whole, 4 * f, count) for f in range(1, far)]
    gate, up = w_gate, preload(w_up, FIRST_VMEM)
    pair = swap(stack(blocks[:2], up), 2, count)
    nexts = [(pair, 0), (pair, 1)] + [(swap(block, 2, count), 0) for block in blocks[2:]]
    blocks = [(block, 0) for block in blocks]
    mine = [unpack(blocks[f : f + 2] + nexts[f : f + 2], unit) for f in range(0, far, 2)]
    other = [swap(rows_of, 1, count) for rows_of in mine]
    keep_far, send_far, keep, send = expert_step(mine + other, unit, gate, up, w_down)

    got = swap(send_far, 1, count)
    mine, near = add_far(keep_far, got)
    send = hold(send, got)
    got = swap(near, 2, count)
    last_far = hold(swap(add_one(mine, 0, got), 4 * (far - 1), count), cost=LOAD_COST)
    mine, nears = add_rest(keep, swap(send, 1, count), unit, [got])
    parts = [last_far]
    for i, near in enumerate(nears):
        got = swap(near, 2, count)
        if i < far - 2:
            parts.append(swap(add_one(mine, i, got), 4 * (far - 2 - i), count))
    return finish(mine, got, parts, rows)


def solution(mesh):
    return jax.shard_map(
        local,
        mesh=mesh,
        in_specs=(
            P(("parts", "wide"), None),
            P(("parts", "wide"), None),
            P(("parts", "wide"), None),
            P(None, None, "wide"),
            P(None, None, "wide"),
            P(None, "wide", None),
        ),
        out_specs=P(("parts", "wide"), None),
        check_vma=False,
    )
```

time: 80.9 us -> 75.9 us (0.938)
  starting transfers between devices: 26.7 us -> 23.4 us
  local copies, waits for them, and re-layouts: 0.92 us -> 0.01 us
    pallas_call x3 -> x1, Pallas kernels: 20.2 us -> 12.5 us  [expert_step(): pl.pallas_call(functools.partial(expert_kernel, unit, far, len(blocks)),...]
    pallas_call x10 -> x13, Pallas kernels: 1.47 us -> 8.74 us  [call_small(): pl.pallas_call(body, out_shape=shapes, in_specs=[vmem] * len(args) + [pl....]
    ppermute x21 -> x17, starting transfers between devices: 26.7 us -> 23.4 us  [swap(): return lax.ppermute(block, 'wide', [(i, i ^ bits) for i in range(count)])]
    unnamed x2 -> x4, local copies, waits for them, and re-layouts: 0.92 us -> 0.01 us
    ppermute x21 -> x17, waiting for transfers between devices: 31.3 us -> 30.9 us  [swap(): return lax.ppermute(block, 'wide', [(i, i ^ bits) for i in range(count)])]
  transfers between devices with their start and end apart: 21 -> 17, of which waited for: 13 -> 13; matrix products, arithmetic and copies ran while one was open for 0% -> 0% of each run, Pallas kernels for 8% -> 8%
where the time goes in v4:
time: 75.9 us; the launch traced here: 75.7 us
  waiting for transfers between devices  30.9 us (41%)
  starting transfers between devices  23.4 us (31%)
  Pallas kernels  21.3 us (28%)
    ppermute x17, waiting for transfers between devices, swap(): return lax.ppermute(block, 'wide', [(i, i ^ bits) for i in range(count)])  30.9 us
    ppermute x17, starting transfers between devices, swap(): return lax.ppermute(block, 'wide', [(i, i ^ bits) for i in range(count)])  23.4 us
    pallas_call x1, Pallas kernels, expert_step(): pl.pallas_call(functools.partial(expert_kernel, unit, far, len(blocks)),...  12.5 us
    pallas_call x13, Pallas kernels, call_small(): pl.pallas_call(body, out_shape=shapes, in_specs=[vmem] * len(args) + [pl....  8.74 us
  transfers between devices with their start and end apart: 17, of which 13 were waited for; matrix products, arithmetic and copies ran while one was open for 0% of the time, Pallas kernels for 8%

profile of v4, /device:TPU:0, one launch (start us, length us, event | category | flops | bytes accessed | tf_op | source)
XLA Modules:
  0.0 75.7 jit_solution(9121271311549753840)
XLA Ops:
  0.0 1.8 %shard_map.64.refs_0_ = bf16[24,3712]{1,0:T(8,128)(2,1)} custom-call(bf16[12,7168]{1,0:T(8,128)(2,1)} %refs_0_.2, s32[8,12]{1,0:T(8,128)} %bitcast.2, f32[8,12]{1,0:T(8,128)} %bitcast.3), custom_call_target="tpu_custom_call" | custom-call | flops 1 | bytes 1 | tf_op jit(solution)/shard_map/pallas_call | solution.py:285
  1.8 0.0 copy-start.1
  1.8 3.1 %collective-permute-start = (bf16[24,3712]{1,0:T(8,128)(2,1)}, bf16[24,3712]{1,0:T(8,128)(2,1)S(1)}, u32[]{:S(2)}, u32[]{:S(2)}) collective-permute-start(bf16[24,3712]{1,0:T(8,128)(2,1)} %shard_map.64.refs_0_), channel_id=1, source_target_pairs={{0,4},{1,5},{2,6},{3,7},{4,0},{5,1},{6,2},{7,3},{8,12},{9,13},{10,... | collective-permute-start | bytes 534536 | tf_op jit(solution)/shard_map/ppermute | solution.py:29
  4.9 2.5 %collective-permute-start.3 = (bf16[24,3712]{1,0:T(8,128)(2,1)}, bf16[24,3712]{1,0:T(8,128)(2,1)S(1)}, u32[]{:S(2)}, u32[]{:S(2)}) collective-permute-start(bf16[24,3712]{1,0:T(8,128)(2,1)} %shard_map.64.refs_0_), channel_id=1, source_target_pairs={{0,12},{1,13},{2,14},{3,15},{4,8},{5,9},{6,10},{7,11},{8,4},{9,5},... | collective-permute-start | bytes 534536 | tf_op jit(solution)/shard_map/ppermute | solution.py:29
  7.4 0.1 collective-permute-start.2
  7.5 5.3 %shard_map.65.refs_2_.refs_5_ = bf16[2,7168,512]{2,1,0:T(8,128)(2,1)S(1)} custom-call(bf16[2,7168,512]{2,1,0:T(8,128)(2,1)} %refs_0_.3), custom_call_target="tpu_custom_call" | custom-call | flops 1 | bytes 16777216 | tf_op jit(solution)/shard_map/pallas_call | solution.py:285
  12.8 0.0 copy-start
  12.9 0.0 collective-permute-done.refs_1_
  12.9 0.0 copy-done.1
  12.9 1.6 %collective-permute-start.1 = (bf16[48,3712]{1,0:T(8,128)(2,1)S(1)}, bf16[48,3712]{1,0:T(8,128)(2,1)S(1)}, u32[]{:S(2)}, u32[]{:S(2)}) collective-permute-start(bf16[48,3712]{1,0:T(8,128)(2,1)S(1)} %shard_map.66), channel_id=1, source_target_pairs={{0,2},{1,3},{2,0},{3,1},{4,6},{5,7},{6,4},{7,5},{8,10},{9,11},{10,... | collective-permute-start | bytes 1069064 | tf_op jit(solution)/shard_map/ppermute | solution.py:29
  14.5 2.4 %collective-permute-done.3.refs_1_ = bf16[24,3712]{1,0:T(8,128)(2,1)S(1)} collective-permute-done((bf16[24,3712]{1,0:T(8,128)(2,1)}, bf16[24,3712]{1,0:T(8,128)(2,1)S(1)}, u32[]{:S(2)}, u32[]{:S(2)}) %collective-permute-start.3) | collective-permute-done | bytes 178208 | tf_op jit(solution)/shard_map/ppermute | solution.py:29
  16.9 1.5 %collective-permute-start.5 = (bf16[24,3712]{1,0:T(8,128)(2,1)S(1)}, bf16[24,3712]{1,0:T(8,128)(2,1)S(1)}, u32[]{:S(2)}, u32[]{:S(2)}) collective-permute-start(bf16[24,3712]{1,0:T(8,128)(2,1)S(1)} %collective-permute-done.3.refs_1_), channel_id=1, source_target_pairs={{0,2},{1,3},{2,0},{3,1},{4,6},{5,7},{6,4},{7,5},{8,10},{9,11},{10,... | collective-permute-start | bytes 534536 | tf_op jit(solution)/shard_map/ppermute | solution.py:29
  18.4 5.0 %collective-permute-done.2.refs_0_ = bf16[24,3712]{1,0:T(8,128)(2,1)S(1)} collective-permute-done((bf16[24,3712]{1,0:T(8,128)(2,1)}, bf16[24,3712]{1,0:T(8,128)(2,1)S(1)}, u32[]{:S(2)}, u32[]{:S(2)}) %collective-permute-start.2) | collective-permute-done | bytes 178208 | tf_op jit(solution)/shard_map/ppermute | solution.py:29
  23.4 1.5 %collective-permute-start.4 = (bf16[24,3712]{1,0:T(8,128)(2,1)S(1)}, bf16[24,3712]{1,0:T(8,128)(2,1)S(1)}, u32[]{:S(2)}, u32[]{:S(2)}) collective-permute-start(bf16[24,3712]{1,0:T(8,128)(2,1)S(1)} %collective-permute-done.2.refs_0_), channel_id=1, source_target_pairs={{0,2},{1,3},{2,0},{3,1},{4,6},{5,7},{6,4},{7,5},{8,10},{9,11},{10,... | collective-permute-start | bytes 534536 | tf_op jit(solution)/shard_map/ppermute | solution.py:29
  25.0 2.6 %collective-permute-done.5.refs_3_ = bf16[24,3712]{1,0:T(8,128)(2,1)S(1)} collective-permute-done((bf16[24,3712]{1,0:T(8,128)(2,1)S(1)}, bf16[24,3712]{1,0:T(8,128)(2,1)S(1)}, u32[]{:S(2)}, u32[]{:S(2)}) %collective-permute-start.5) | collective-permute-done | bytes 178208 | tf_op jit(solution)/shard_map/ppermute | solution.py:29
  27.5 2.6 %collective-permute-done.4.refs_2_ = bf16[24,3712]{1,0:T(8,128)(2,1)S(1)} collective-permute-done((bf16[24,3712]{1,0:T(8,128)(2,1)S(1)}, bf16[24,3712]{1,0:T(8,128)(2,1)S(1)}, u32[]{:S(2)}, u32[]{:S(2)}) %collective-permute-start.4) | collective-permute-done | bytes 178208 | tf_op jit(solution)/shard_map/ppermute | solution.py:29
  30.1 0.1 shard_map.68.refs_1_
  30.2 0.1 collective-permute-start.7
  30.3 0.0 collective-permute-done.1.refs_2_.refs_3_
  30.3 0.1 shard_map.67.refs_0_
  30.4 0.5 collective-permute-start.6
  30.9 1.5 %collective-permute-done.7.refs_3_ = bf16[48,7296]{1,0:T(8,128)(2,1)S(1)} collective-permute-done((bf16[48,7296]{1,0:T(8,128)(2,1)S(1)}, bf16[48,7296]{1,0:T(8,128)(2,1)S(1)}, u32[]{:S(2)}, u32[]{:S(2)}) %collective-permute-start.7) | collective-permute-done | bytes 700448 | tf_op jit(solution)/shard_map/ppermute | solution.py:29
  32.4 1.0 %collective-permute-done.6.refs_2_ = bf16[48,7296]{1,0:T(8,128)(2,1)S(1)} collective-permute-done((bf16[48,7296]{1,0:T(8,128)(2,1)S(1)}, bf16[48,7296]{1,0:T(8,128)(2,1)S(1)}, u32[]{:S(2)}, u32[]{:S(2)}) %collective-permute-start.6) | collective-permute-done | bytes 700448 | tf_op jit(solution)/shard_map/ppermute | solution.py:29
  33.4 0.0 copy-done
  33.4 12.5 %shard_map.69 = (bf16[48,3584]{1,0:T(8,128)(2,1)S(1)}, bf16[48,3584]{1,0:T(8,128)(2,1)S(1)}, bf16[144,3584]{1,0:T(8,128)(2,1)S(1)}, bf16[144,3584]{1,0:T(8,128)(2,1)S(1)}) custom-call(bf16[48,7296]{1,0:T(8,128)(2,1)S(1)} %shard_map.67.refs_0_, bf16[48,7296]{1,0:T(8,128)(2,1)S(1)} %shard_map.68.refs_1_, bf16[48,7296]{1,0:T(8,128)(2,1)S(1)} %collective-permute-done.6.refs_2_, ...), custom_call_target="tpu_custom_call" | custom-call | flops 536870912 | bytes 1 | tf_op jit(solution)/shard_map/pallas_call | solution.py:262
  46.0 0.2 collective-permute-start.8
  46.2 1.5 %collective-permute-done.8.refs_1_ = bf16[48,3584]{1,0:T(8,128)(2,1)S(1)} collective-permute-done((bf16[48,3584]{1,0:T(8,128)(2,1)S(1)}, bf16[48,3584]{1,0:T(8,128)(2,1)S(1)}, u32[]{:S(2)}, u32[]{:S(2)}) %collective-permute-start.8) | collective-permute-done | bytes 344096 | tf_op jit(solution)/shard_map/ppermute | solution.py:29
  47.7 0.1 shard_map.70
  47.8 0.2 collective-permute-start.9
  48.0 0.1 shard_map.71
  48.1 1.6 %collective-permute-start.10 = (bf16[24,3584]{1,0:T(8,128)(2,1)S(1)}, bf16[24,3584]{1,0:T(8,128)(2,1)S(1)}, u32[]{:S(2)}, u32[]{:S(2)}) collective-permute-start(bf16[24,3584]{1,0:T(8,128)(2,1)S(1)} %get-tuple-element.19), channel_id=1, source_target_pairs={{0,2},{1,3},{2,0},{3,1},{4,6},{5,7},{6,4},{7,5},{8,10},{9,11},{10,... | collective-permute-start | bytes 516104 | tf_op jit(solution)/shard_map/ppermute | solution.py:29
  49.7 5.1 %collective-permute-done.10.refs_2_.refs_1_ = bf16[24,3584]{1,0:T(8,128)(2,1)S(1)} collective-permute-done((bf16[24,3584]{1,0:T(8,128)(2,1)S(1)}, bf16[24,3584]{1,0:T(8,128)(2,1)S(1)}, u32[]{:S(2)}, u32[]{:S(2)}) %collective-permute-start.10) | collective-permute-done | bytes 172064 | tf_op jit(solution)/shard_map/ppermute | solution.py:29
  54.8 0.0 collective-permute-done.9.refs_1_
  54.8 0.2 shard_map.72
  55.0 1.6 %collective-permute-start.13 = (bf16[24,3584]{1,0:T(8,128)(2,1)S(1)}, bf16[24,3584]{1,0:T(8,128)(2,1)S(1)}, u32[]{:S(2)}, u32[]{:S(2)}) collective-permute-start(bf16[24,3584]{1,0:T(8,128)(2,1)S(1)} %get-tuple-element.23), channel_id=1, source_target_pairs={{0,2},{1,3},{2,0},{3,1},{4,6},{5,7},{6,4},{7,5},{8,10},{9,11},{10,... | collective-permute-start | bytes 516104 | tf_op jit(solution)/shard_map/ppermute | solution.py:29
  56.6 0.5 collective-permute-start.15
  57.2 2.7 %collective-permute-start.12 = (bf16[24,3584]{1,0:T(8,128)(2,1)S(1)}, bf16[24,3584]{1,0:T(8,128)(2,1)S(1)}, u32[]{:S(2)}, u32[]{:S(2)}) collective-permute-start(bf16[24,3584]{1,0:T(8,128)(2,1)S(1)} %shard_map.73), channel_id=1, source_target_pairs={{0,12},{1,13},{2,14},{3,15},{4,8},{5,9},{6,10},{7,11},{8,4},{9,5},... | collective-permute-start | bytes 516104 | tf_op jit(solution)/shard_map/ppermute | solution.py:29
  59.9 1.5 %collective-permute-start.11 = (bf16[24,3584]{1,0:T(8,128)(2,1)S(1)}, bf16[24,3584]{1,0:T(8,128)(2,1)S(1)}, u32[]{:S(2)}, u32[]{:S(2)}) collective-permute-start(bf16[24,3584]{1,0:T(8,128)(2,1)S(1)} %get-tuple-element.21), channel_id=1, source_target_pairs={{0,2},{1,3},{2,0},{3,1},{4,6},{5,7},{6,4},{7,5},{8,10},{9,11},{10,... | collective-permute-start | bytes 516104 | tf_op jit(solution)/shard_map/ppermute | solution.py:29
  61.4 1.0 %collective-permute-done.13.refs_1_ = bf16[24,3584]{1,0:T(8,128)(2,1)S(1)} collective-permute-done((bf16[24,3584]{1,0:T(8,128)(2,1)S(1)}, bf16[24,3584]{1,0:T(8,128)(2,1)S(1)}, u32[]{:S(2)}, u32[]{:S(2)}) %collective-permute-start.13) | collective-permute-done | bytes 172064 | tf_op jit(solution)/shard_map/ppermute | solution.py:29
  62.4 2.6 %collective-permute-start.14 = (bf16[24,3584]{1,0:T(8,128)(2,1)S(1)}, bf16[24,3584]{1,0:T(8,128)(2,1)S(1)}, u32[]{:S(2)}, u32[]{:S(2)}) collective-permute-start(bf16[24,3584]{1,0:T(8,128)(2,1)S(1)} %shard_map.75), channel_id=1, source_target_pairs={{0,8},{1,9},{2,10},{3,11},{4,12},{5,13},{6,14},{7,15},{8,0},{9,1},... | collective-permute-start | bytes 516104 | tf_op jit(solution)/shard_map/ppermute | solution.py:29
  65.0 1.0 %collective-permute-done.15.refs_1_ = bf16[24,3584]{1,0:T(8,128)(2,1)S(1)} collective-permute-done((bf16[24,3584]{1,0:T(8,128)(2,1)S(1)}, bf16[24,3584]{1,0:T(8,128)(2,1)S(1)}, u32[]{:S(2)}, u32[]{:S(2)}) %collective-permute-start.15) | collective-permute-done | bytes 172064 | tf_op jit(solution)/shard_map/ppermute | solution.py:29
  66.1 0.1 shard_map.76
  66.1 1.6 %collective-permute-start.16 = (bf16[24,3584]{1,0:T(8,128)(2,1)S(1)}, bf16[24,3584]{1,0:T(8,128)(2,1)S(1)}, u32[]{:S(2)}, u32[]{:S(2)}) collective-permute-start(bf16[24,3584]{1,0:T(8,128)(2,1)S(1)} %shard_map.76), channel_id=1, source_target_pairs={{0,4},{1,5},{2,6},{3,7},{4,0},{5,1},{6,2},{7,3},{8,12},{9,13},{10,... | collective-permute-start | bytes 516104 | tf_op jit(solution)/shard_map/ppermute | solution.py:29
  67.7 0.0 collective-permute-done.12.refs_0_
  67.7 0.6 collective-permute-done.11.refs_1_
  68.3 6.3 %collective-permute-done.14.refs_3_ = bf16[24,3584]{1,0:T(8,128)(2,1)S(1)} collective-permute-done((bf16[24,3584]{1,0:T(8,128)(2,1)S(1)}, bf16[24,3584]{1,0:T(8,128)(2,1)S(1)}, u32[]{:S(2)}, u32[]{:S(2)}) %collective-permute-start.14) | collective-permute-done | bytes 172064 | tf_op jit(solution)/shard_map/ppermute | solution.py:29
  74.6 0.2 collective-permute-done.16.refs_4_
  74.9 0.9 %shard_map.77 = bf16[12,7168]{1,0:T(8,128)(2,1)} custom-call(bf16[72,3584]{1,0:T(8,128)(2,1)S(1)} %get-tuple-element.20.refs_0_, bf16[24,3584]{1,0:T(8,128)(2,1)S(1)} %collective-permute-done.11.refs_1_, bf16[24,3584]{1,0:T(8,128)(2,1)S(1)} %shard_map.74.refs_2_, bf16[24,3584]{1,0:T(8,128)(2,1)S(1)} %collective-permute-done.14.refs_3_, ...), custom_call_target="tpu_custom_call" | custom-call | flops 1 | bytes 1 | tf_op jit(solution)/shard_map/pallas_call | solution.py:285
  (4 shorter events, 0.1 us)
Async XLA Ops:
  1.8 11.0 %copy-start.1 = (bf16[24,3712]{1,0:T(8,128)(2,1)S(1)}, bf16[24,3712]{1,0:T(8,128)(2,1)}, u32[]{:S(2)}) copy-start(bf16[24,3712]{1,0:T(8,128)(2,1)} %shard_map.64.refs_0_) | copy-start | bytes 534532
  1.8 11.0 %collective-permute-start = (bf16[24,3712]{1,0:T(8,128)(2,1)}, bf16[24,3712]{1,0:T(8,128)(2,1)S(1)}, u32[]{:S(2)}, u32[]{:S(2)}) collective-permute-start(bf16[24,3712]{1,0:T(8,128)(2,1)} %shard_map.64.refs_0_), channel_id=1, source_target_pairs={{0,4},{1,5},{2,6},{3,7},{4,0},{5,1},{6,2},{7,3},{8,12},{9,13},{10,... | collective-permute-start | bytes 534536 | tf_op jit(solution)/shard_map/ppermute | solution.py:29
  4.9 12.0 %collective-permute-start.3 = (bf16[24,3712]{1,0:T(8,128)(2,1)}, bf16[24,3712]{1,0:T(8,128)(2,1)S(1)}, u32[]{:S(2)}, u32[]{:S(2)}) collective-permute-start(bf16[24,3712]{1,0:T(8,128)(2,1)} %shard_map.64.refs_0_), channel_id=1, source_target_pairs={{0,12},{1,13},{2,14},{3,15},{4,8},{5,9},{6,10},{7,11},{8,4},{9,5},... | collective-permute-start | bytes 534536 | tf_op jit(solution)/shard_map/ppermute | solution.py:29
  7.4 16.0 %collective-permute-start.2 = (bf16[24,3712]{1,0:T(8,128)(2,1)}, bf16[24,3712]{1,0:T(8,128)(2,1)S(1)}, u32[]{:S(2)}, u32[]{:S(2)}) collective-permute-start(bf16[24,3712]{1,0:T(8,128)(2,1)} %shard_map.64.refs_0_), channel_id=1, source_target_pairs={{0,8},{1,9},{2,10},{3,11},{4,12},{5,13},{6,14},{7,15},{8,0},{9,1},... | collective-permute-start | bytes 534536 | tf_op jit(solution)/shard_map/ppermute | solution.py:29
  12.8 20.6 %copy-start = (bf16[2,7168,512]{2,1,0:T(8,128)(2,1)S(1)}, bf16[2,7168,512]{2,1,0:T(8,128)(2,1)}, u32[]{:S(2)}) copy-start(bf16[2,7168,512]{2,1,0:T(8,128)(2,1)} %refs_4_.1) | copy-start | bytes 44040196
  12.9 17.4 %collective-permute-start.1 = (bf16[48,3712]{1,0:T(8,128)(2,1)S(1)}, bf16[48,3712]{1,0:T(8,128)(2,1)S(1)}, u32[]{:S(2)}, u32[]{:S(2)}) collective-permute-start(bf16[48,3712]{1,0:T(8,128)(2,1)S(1)} %shard_map.66), channel_id=1, source_target_pairs={{0,2},{1,3},{2,0},{3,1},{4,6},{5,7},{6,4},{7,5},{8,10},{9,11},{10,... | collective-permute-start | bytes 1069064 | tf_op jit(solution)/shard_map/ppermute | solution.py:29
  16.9 10.6 %collective-permute-start.5 = (bf16[24,3712]{1,0:T(8,128)(2,1)S(1)}, bf16[24,3712]{1,0:T(8,128)(2,1)S(1)}, u32[]{:S(2)}, u32[]{:S(2)}) collective-permute-start(bf16[24,3712]{1,0:T(8,128)(2,1)S(1)} %collective-permute-done.3.refs_1_), channel_id=1, source_target_pairs={{0,2},{1,3},{2,0},{3,1},{4,6},{5,7},{6,4},{7,5},{8,10},{9,11},{10,... | collective-permute-start | bytes 534536 | tf_op jit(solution)/shard_map/ppermute | solution.py:29
  23.4 6.7 %collective-permute-start.4 = (bf16[24,3712]{1,0:T(8,128)(2,1)S(1)}, bf16[24,3712]{1,0:T(8,128)(2,1)S(1)}, u32[]{:S(2)}, u32[]{:S(2)}) collective-permute-start(bf16[24,3712]{1,0:T(8,128)(2,1)S(1)} %collective-permute-done.2.refs_0_), channel_id=1, source_target_pairs={{0,2},{1,3},{2,0},{3,1},{4,6},{5,7},{6,4},{7,5},{8,10},{9,11},{10,... | collective-permute-start | bytes 534536 | tf_op jit(solution)/shard_map/ppermute | solution.py:29
  30.2 2.2 %collective-permute-start.7 = (bf16[48,7296]{1,0:T(8,128)(2,1)S(1)}, bf16[48,7296]{1,0:T(8,128)(2,1)S(1)}, u32[]{:S(2)}, u32[]{:S(2)}) collective-permute-start(bf16[48,7296]{1,0:T(8,128)(2,1)S(1)} %shard_map.68.refs_1_), channel_id=1, source_target_pairs={{0,1},{1,0},{2,3},{3,2},{4,5},{5,4},{6,7},{7,6},{8,9},{9,8},{10,11... | collective-permute-start | bytes 2101256 | tf_op jit(solution)/shard_map/ppermute | solution.py:29
  30.4 3.0 %collective-permute-start.6 = (bf16[48,7296]{1,0:T(8,128)(2,1)S(1)}, bf16[48,7296]{1,0:T(8,128)(2,1)S(1)}, u32[]{:S(2)}, u32[]{:S(2)}) collective-permute-start(bf16[48,7296]{1,0:T(8,128)(2,1)S(1)} %shard_map.67.refs_0_), channel_id=1, source_target_pairs={{0,1},{1,0},{2,3},{3,2},{4,5},{5,4},{6,7},{7,6},{8,9},{9,8},{10,11... | collective-permute-start | bytes 2101256 | tf_op jit(solution)/shard_map/ppermute | solution.py:29
  46.0 1.7 %collective-permute-start.8 = (bf16[48,3584]{1,0:T(8,128)(2,1)S(1)}, bf16[48,3584]{1,0:T(8,128)(2,1)S(1)}, u32[]{:S(2)}, u32[]{:S(2)}) collective-permute-start(bf16[48,3584]{1,0:T(8,128)(2,1)S(1)} %get-tuple-element.17), channel_id=1, source_target_pairs={{0,1},{1,0},{2,3},{3,2},{4,5},{5,4},{6,7},{7,6},{8,9},{9,8},{10,11... | collective-permute-start | bytes 1032200 | tf_op jit(solution)/shard_map/ppermute | solution.py:29
  47.8 7.0 %collective-permute-start.9 = (bf16[144,3584]{1,0:T(8,128)(2,1)S(1)}, bf16[144,3584]{1,0:T(8,128)(2,1)S(1)}, u32[]{:S(2)}, u32[]{:S(2)}) collective-permute-start(bf16[144,3584]{1,0:T(8,128)(2,1)S(1)} %shard_map.70), channel_id=1, source_target_pairs={{0,1},{1,0},{2,3},{3,2},{4,5},{5,4},{6,7},{7,6},{8,9},{9,8},{10,11... | collective-permute-start | bytes 3096584 | tf_op jit(solution)/shard_map/ppermute | solution.py:29
  48.1 6.7 %collective-permute-start.10 = (bf16[24,3584]{1,0:T(8,128)(2,1)S(1)}, bf16[24,3584]{1,0:T(8,128)(2,1)S(1)}, u32[]{:S(2)}, u32[]{:S(2)}) collective-permute-start(bf16[24,3584]{1,0:T(8,128)(2,1)S(1)} %get-tuple-element.19), channel_id=1, source_target_pairs={{0,2},{1,3},{2,0},{3,1},{4,6},{5,7},{6,4},{7,5},{8,10},{9,11},{10,... | collective-permute-start | bytes 516104 | tf_op jit(solution)/shard_map/ppermute | solution.py:29
  55.0 7.4 %collective-permute-start.13 = (bf16[24,3584]{1,0:T(8,128)(2,1)S(1)}, bf16[24,3584]{1,0:T(8,128)(2,1)S(1)}, u32[]{:S(2)}, u32[]{:S(2)}) collective-permute-start(bf16[24,3584]{1,0:T(8,128)(2,1)S(1)} %get-tuple-element.23), channel_id=1, source_target_pairs={{0,2},{1,3},{2,0},{3,1},{4,6},{5,7},{6,4},{7,5},{8,10},{9,11},{10,... | collective-permute-start | bytes 516104 | tf_op jit(solution)/shard_map/ppermute | solution.py:29
  56.6 9.5 %collective-permute-start.15 = (bf16[24,3584]{1,0:T(8,128)(2,1)S(1)}, bf16[24,3584]{1,0:T(8,128)(2,1)S(1)}, u32[]{:S(2)}, u32[]{:S(2)}) collective-permute-start(bf16[24,3584]{1,0:T(8,128)(2,1)S(1)} %get-tuple-element.24), channel_id=1, source_target_pairs={{0,2},{1,3},{2,0},{3,1},{4,6},{5,7},{6,4},{7,5},{8,10},{9,11},{10,... | collective-permute-start | bytes 516104 | tf_op jit(solution)/shard_map/ppermute | solution.py:29
  57.2 10.6 %collective-permute-start.12 = (bf16[24,3584]{1,0:T(8,128)(2,1)S(1)}, bf16[24,3584]{1,0:T(8,128)(2,1)S(1)}, u32[]{:S(2)}, u32[]{:S(2)}) collective-permute-start(bf16[24,3584]{1,0:T(8,128)(2,1)S(1)} %shard_map.73), channel_id=1, source_target_pairs={{0,12},{1,13},{2,14},{3,15},{4,8},{5,9},{6,10},{7,11},{8,4},{9,5},... | collective-permute-start | bytes 516104 | tf_op jit(solution)/shard_map/ppermute | solution.py:29
  59.9 8.4 %collective-permute-start.11 = (bf16[24,3584]{1,0:T(8,128)(2,1)S(1)}, bf16[24,3584]{1,0:T(8,128)(2,1)S(1)}, u32[]{:S(2)}, u32[]{:S(2)}) collective-permute-start(bf16[24,3584]{1,0:T(8,128)(2,1)S(1)} %get-tuple-element.21), channel_id=1, source_target_pairs={{0,2},{1,3},{2,0},{3,1},{4,6},{5,7},{6,4},{7,5},{8,10},{9,11},{10,... | collective-permute-start | bytes 516104 | tf_op jit(solution)/shard_map/ppermute | solution.py:29
  62.4 12.2 %collective-permute-start.14 = (bf16[24,3584]{1,0:T(8,128)(2,1)S(1)}, bf16[24,3584]{1,0:T(8,128)(2,1)S(1)}, u32[]{:S(2)}, u32[]{:S(2)}) collective-permute-start(bf16[24,3584]{1,0:T(8,128)(2,1)S(1)} %shard_map.75), channel_id=1, source_target_pairs={{0,8},{1,9},{2,10},{3,11},{4,12},{5,13},{6,14},{7,15},{8,0},{9,1},... | collective-permute-start | bytes 516104 | tf_op jit(solution)/shard_map/ppermute | solution.py:29
  66.1 8.7 %collective-permute-start.16 = (bf16[24,3584]{1,0:T(8,128)(2,1)S(1)}, bf16[24,3584]{1,0:T(8,128)(2,1)S(1)}, u32[]{:S(2)}, u32[]{:S(2)}) collective-permute-start(bf16[24,3584]{1,0:T(8,128)(2,1)S(1)} %shard_map.76), channel_id=1, source_target_pairs={{0,4},{1,5},{2,6},{3,7},{4,0},{5,1},{6,2},{7,3},{8,12},{9,13},{10,... | collective-permute-start | bytes 516104 | tf_op jit(solution)/shard_map/ppermute | solution.py:29

commit v5 on v4

--- a/solution.py
+++ b/solution.py
@@ -374,7 +374,7 @@
     send = hold(send, got)
     got = swap(near, 2, count)
     last_far = hold(swap(add_one(mine, 0, got), 4 * (far - 1), count), cost=LOAD_COST)
-    mine, nears = add_rest(keep, swap(send, 1, count), unit, [got])
+    mine, nears = add_rest(keep, swap(send, 1, count), unit, [])
     parts = [last_far]
     for i, near in enumerate(nears):
         got = swap(near, 2, count)

time: 75.9 us -> 73.8 us (0.972)
  waiting for transfers between devices: 30.9 us -> 29.4 us
    ppermute x17, waiting for transfers between devices: 30.9 us -> 29.4 us  [swap(): return lax.ppermute(block, 'wide', [(i, i ^ bits) for i in range(count)])]
  transfers between devices with their start and end apart: 17 -> 17, of which waited for: 13 -> 12; matrix products, arithmetic and copies ran while one was open for 0% -> 0% of each run, Pallas kernels for 8% -> 8%
where the time goes in v5:
time: 73.8 us; the launch traced here: 73.6 us
  waiting for transfers between devices  29.4 us (40%)
  starting transfers between devices  22.8 us (31%)
  Pallas kernels  21.3 us (29%)
    ppermute x17, waiting for transfers between devices, swap(): return lax.ppermute(block, 'wide', [(i, i ^ bits) for i in range(count)])  29.4 us
    ppermute x17, starting transfers between devices, swap(): return lax.ppermute(block, 'wide', [(i, i ^ bits) for i in range(count)])  22.8 us
    pallas_call x1, Pallas kernels, expert_step(): pl.pallas_call(functools.partial(expert_kernel, unit, far, len(blocks)),...  12.5 us
    pallas_call x13, Pallas kernels, call_small(): pl.pallas_call(body, out_shape=shapes, in_specs=[vmem] * len(args) + [pl....  8.73 us
  transfers between devices with their start and end apart: 17, of which 12 were waited for; matrix products, arithmetic and copies ran while one was open for 0% of the time, Pallas kernels for 8%

profile of v5, /device:TPU:0, one launch (start us, length us, event | category | flops | bytes accessed | tf_op | source)
XLA Modules:
  0.0 73.6 jit_solution(8944527434568485068)
XLA Ops:
  0.0 1.8 %shard_map.64.refs_0_ = bf16[24,3712]{1,0:T(8,128)(2,1)} custom-call(bf16[12,7168]{1,0:T(8,128)(2,1)} %refs_0_.2, s32[8,12]{1,0:T(8,128)} %bitcast.2, f32[8,12]{1,0:T(8,128)} %bitcast.3), custom_call_target="tpu_custom_call" | custom-call | flops 1 | bytes 1 | tf_op jit(solution)/shard_map/pallas_call | solution.py:285
  1.8 0.0 copy-start.1
  1.8 3.1 %collective-permute-start = (bf16[24,3712]{1,0:T(8,128)(2,1)}, bf16[24,3712]{1,0:T(8,128)(2,1)S(1)}, u32[]{:S(2)}, u32[]{:S(2)}) collective-permute-start(bf16[24,3712]{1,0:T(8,128)(2,1)} %shard_map.64.refs_0_), channel_id=1, source_target_pairs={{0,4},{1,5},{2,6},{3,7},{4,0},{5,1},{6,2},{7,3},{8,12},{9,13},{10,... | collective-permute-start | bytes 534536 | tf_op jit(solution)/shard_map/ppermute | solution.py:29
  4.9 2.5 %collective-permute-start.3 = (bf16[24,3712]{1,0:T(8,128)(2,1)}, bf16[24,3712]{1,0:T(8,128)(2,1)S(1)}, u32[]{:S(2)}, u32[]{:S(2)}) collective-permute-start(bf16[24,3712]{1,0:T(8,128)(2,1)} %shard_map.64.refs_0_), channel_id=1, source_target_pairs={{0,12},{1,13},{2,14},{3,15},{4,8},{5,9},{6,10},{7,11},{8,4},{9,5},... | collective-permute-start | bytes 534536 | tf_op jit(solution)/shard_map/ppermute | solution.py:29
  7.4 0.1 collective-permute-start.2
  7.5 5.3 %shard_map.65.refs_2_.refs_5_ = bf16[2,7168,512]{2,1,0:T(8,128)(2,1)S(1)} custom-call(bf16[2,7168,512]{2,1,0:T(8,128)(2,1)} %refs_0_.3), custom_call_target="tpu_custom_call" | custom-call | flops 1 | bytes 16777216 | tf_op jit(solution)/shard_map/pallas_call | solution.py:285
  12.8 0.0 copy-start
  12.9 0.0 collective-permute-done.refs_1_
  12.9 0.0 copy-done.1
  12.9 1.6 %collective-permute-start.1 = (bf16[48,3712]{1,0:T(8,128)(2,1)S(1)}, bf16[48,3712]{1,0:T(8,128)(2,1)S(1)}, u32[]{:S(2)}, u32[]{:S(2)}) collective-permute-start(bf16[48,3712]{1,0:T(8,128)(2,1)S(1)} %shard_map.66), channel_id=1, source_target_pairs={{0,2},{1,3},{2,0},{3,1},{4,6},{5,7},{6,4},{7,5},{8,10},{9,11},{10,... | collective-permute-start | bytes 1069064 | tf_op jit(solution)/shard_map/ppermute | solution.py:29
  14.5 2.4 %collective-permute-done.3.refs_1_ = bf16[24,3712]{1,0:T(8,128)(2,1)S(1)} collective-permute-done((bf16[24,3712]{1,0:T(8,128)(2,1)}, bf16[24,3712]{1,0:T(8,128)(2,1)S(1)}, u32[]{:S(2)}, u32[]{:S(2)}) %collective-permute-start.3) | collective-permute-done | bytes 178208 | tf_op jit(solution)/shard_map/ppermute | solution.py:29
  16.9 1.5 %collective-permute-start.5 = (bf16[24,3712]{1,0:T(8,128)(2,1)S(1)}, bf16[24,3712]{1,0:T(8,128)(2,1)S(1)}, u32[]{:S(2)}, u32[]{:S(2)}) collective-permute-start(bf16[24,3712]{1,0:T(8,128)(2,1)S(1)} %collective-permute-done.3.refs_1_), channel_id=1, source_target_pairs={{0,2},{1,3},{2,0},{3,1},{4,6},{5,7},{6,4},{7,5},{8,10},{9,11},{10,... | collective-permute-start | bytes 534536 | tf_op jit(solution)/shard_map/ppermute | solution.py:29
  18.4 5.0 %collective-permute-done.2.refs_0_ = bf16[24,3712]{1,0:T(8,128)(2,1)S(1)} collective-permute-done((bf16[24,3712]{1,0:T(8,128)(2,1)}, bf16[24,3712]{1,0:T(8,128)(2,1)S(1)}, u32[]{:S(2)}, u32[]{:S(2)}) %collective-permute-start.2) | collective-permute-done | bytes 178208 | tf_op jit(solution)/shard_map/ppermute | solution.py:29
  23.4 1.5 %collective-permute-start.4 = (bf16[24,3712]{1,0:T(8,128)(2,1)S(1)}, bf16[24,3712]{1,0:T(8,128)(2,1)S(1)}, u32[]{:S(2)}, u32[]{:S(2)}) collective-permute-start(bf16[24,3712]{1,0:T(8,128)(2,1)S(1)} %collective-permute-done.2.refs_0_), channel_id=1, source_target_pairs={{0,2},{1,3},{2,0},{3,1},{4,6},{5,7},{6,4},{7,5},{8,10},{9,11},{10,... | collective-permute-start | bytes 534536 | tf_op jit(solution)/shard_map/ppermute | solution.py:29
  25.0 2.6 %collective-permute-done.5.refs_3_ = bf16[24,3712]{1,0:T(8,128)(2,1)S(1)} collective-permute-done((bf16[24,3712]{1,0:T(8,128)(2,1)S(1)}, bf16[24,3712]{1,0:T(8,128)(2,1)S(1)}, u32[]{:S(2)}, u32[]{:S(2)}) %collective-permute-start.5) | collective-permute-done | bytes 178208 | tf_op jit(solution)/shard_map/ppermute | solution.py:29
  27.5 2.6 %collective-permute-done.4.refs_2_ = bf16[24,3712]{1,0:T(8,128)(2,1)S(1)} collective-permute-done((bf16[24,3712]{1,0:T(8,128)(2,1)S(1)}, bf16[24,3712]{1,0:T(8,128)(2,1)S(1)}, u32[]{:S(2)}, u32[]{:S(2)}) %collective-permute-start.4) | collective-permute-done | bytes 178208 | tf_op jit(solution)/shard_map/ppermute | solution.py:29
  30.1 0.1 shard_map.68.refs_1_
  30.2 0.1 collective-permute-start.7
  30.3 0.0 collective-permute-done.1.refs_2_.refs_3_
  30.3 0.1 shard_map.67.refs_0_
  30.4 0.5 collective-permute-start.6
  30.9 1.5 %collective-permute-done.7.refs_3_ = bf16[48,7296]{1,0:T(8,128)(2,1)S(1)} collective-permute-done((bf16[48,7296]{1,0:T(8,128)(2,1)S(1)}, bf16[48,7296]{1,0:T(8,128)(2,1)S(1)}, u32[]{:S(2)}, u32[]{:S(2)}) %collective-permute-start.7) | collective-permute-done | bytes 700448 | tf_op jit(solution)/shard_map/ppermute | solution.py:29
  32.4 1.0 %collective-permute-done.6.refs_2_ = bf16[48,7296]{1,0:T(8,128)(2,1)S(1)} collective-permute-done((bf16[48,7296]{1,0:T(8,128)(2,1)S(1)}, bf16[48,7296]{1,0:T(8,128)(2,1)S(1)}, u32[]{:S(2)}, u32[]{:S(2)}) %collective-permute-start.6) | collective-permute-done | bytes 700448 | tf_op jit(solution)/shard_map/ppermute | solution.py:29
  33.4 0.0 copy-done
  33.4 12.5 %shard_map.69 = (bf16[48,3584]{1,0:T(8,128)(2,1)S(1)}, bf16[48,3584]{1,0:T(8,128)(2,1)S(1)}, bf16[144,3584]{1,0:T(8,128)(2,1)S(1)}, bf16[144,3584]{1,0:T(8,128)(2,1)S(1)}) custom-call(bf16[48,7296]{1,0:T(8,128)(2,1)S(1)} %shard_map.67.refs_0_, bf16[48,7296]{1,0:T(8,128)(2,1)S(1)} %shard_map.68.refs_1_, bf16[48,7296]{1,0:T(8,128)(2,1)S(1)} %collective-permute-done.6.refs_2_, ...), custom_call_target="tpu_custom_call" | custom-call | flops 536870912 | bytes 1 | tf_op jit(solution)/shard_map/pallas_call | solution.py:262
  46.0 0.2 collective-permute-start.8
  46.2 1.5 %collective-permute-done.8.refs_1_ = bf16[48,3584]{1,0:T(8,128)(2,1)S(1)} collective-permute-done((bf16[48,3584]{1,0:T(8,128)(2,1)S(1)}, bf16[48,3584]{1,0:T(8,128)(2,1)S(1)}, u32[]{:S(2)}, u32[]{:S(2)}) %collective-permute-start.8) | collective-permute-done | bytes 344096 | tf_op jit(solution)/shard_map/ppermute | solution.py:29
  47.7 0.1 shard_map.70
  47.8 0.2 collective-permute-start.9
  48.0 0.1 shard_map.72
  48.1 1.6 %collective-permute-start.11 = (bf16[24,3584]{1,0:T(8,128)(2,1)S(1)}, bf16[24,3584]{1,0:T(8,128)(2,1)S(1)}, u32[]{:S(2)}, u32[]{:S(2)}) collective-permute-start(bf16[24,3584]{1,0:T(8,128)(2,1)S(1)} %get-tuple-element.22), channel_id=1, source_target_pairs={{0,2},{1,3},{2,0},{3,1},{4,6},{5,7},{6,4},{7,5},{8,10},{9,11},{10,... | collective-permute-start | bytes 516104 | tf_op jit(solution)/shard_map/ppermute | solution.py:29
  49.7 0.8 %collective-permute-done.9.refs_1_ = bf16[144,3584]{1,0:T(8,128)(2,1)S(1)} collective-permute-done((bf16[144,3584]{1,0:T(8,128)(2,1)S(1)}, bf16[144,3584]{1,0:T(8,128)(2,1)S(1)}, u32[]{:S(2)}, u32[]{:S(2)}) %collective-permute-start.9) | collective-permute-done | bytes 1032224 | tf_op jit(solution)/shard_map/ppermute | solution.py:29
  50.5 0.2 shard_map.71
  50.7 1.6 %collective-permute-start.13 = (bf16[24,3584]{1,0:T(8,128)(2,1)S(1)}, bf16[24,3584]{1,0:T(8,128)(2,1)S(1)}, u32[]{:S(2)}, u32[]{:S(2)}) collective-permute-start(bf16[24,3584]{1,0:T(8,128)(2,1)S(1)} %get-tuple-element.23), channel_id=1, source_target_pairs={{0,2},{1,3},{2,0},{3,1},{4,6},{5,7},{6,4},{7,5},{8,10},{9,11},{10,... | collective-permute-start | bytes 516104 | tf_op jit(solution)/shard_map/ppermute | solution.py:29
  52.3 0.5 collective-permute-start.15
  52.8 2.5 %collective-permute-done.11.refs_1_ = bf16[24,3584]{1,0:T(8,128)(2,1)S(1)} collective-permute-done((bf16[24,3584]{1,0:T(8,128)(2,1)S(1)}, bf16[24,3584]{1,0:T(8,128)(2,1)S(1)}, u32[]{:S(2)}, u32[]{:S(2)}) %collective-permute-start.11) | collective-permute-done | bytes 172064 | tf_op jit(solution)/shard_map/ppermute | solution.py:29
  55.4 2.7 %collective-permute-start.12 = (bf16[24,3584]{1,0:T(8,128)(2,1)S(1)}, bf16[24,3584]{1,0:T(8,128)(2,1)S(1)}, u32[]{:S(2)}, u32[]{:S(2)}) collective-permute-start(bf16[24,3584]{1,0:T(8,128)(2,1)S(1)} %shard_map.73), channel_id=1, source_target_pairs={{0,12},{1,13},{2,14},{3,15},{4,8},{5,9},{6,10},{7,11},{8,4},{9,5},... | collective-permute-start | bytes 516104 | tf_op jit(solution)/shard_map/ppermute | solution.py:29
  58.1 1.5 %collective-permute-start.10 = (bf16[24,3584]{1,0:T(8,128)(2,1)S(1)}, bf16[24,3584]{1,0:T(8,128)(2,1)S(1)}, u32[]{:S(2)}, u32[]{:S(2)}) collective-permute-start(bf16[24,3584]{1,0:T(8,128)(2,1)S(1)} %get-tuple-element.19), channel_id=1, source_target_pairs={{0,2},{1,3},{2,0},{3,1},{4,6},{5,7},{6,4},{7,5},{8,10},{9,11},{10,... | collective-permute-start | bytes 516104 | tf_op jit(solution)/shard_map/ppermute | solution.py:29
  59.6 0.0 collective-permute-done.13.refs_1_
  59.7 2.0 %collective-permute-start.14 = (bf16[24,3584]{1,0:T(8,128)(2,1)S(1)}, bf16[24,3584]{1,0:T(8,128)(2,1)S(1)}, u32[]{:S(2)}, u32[]{:S(2)}) collective-permute-start(bf16[24,3584]{1,0:T(8,128)(2,1)S(1)} %shard_map.75), channel_id=1, source_target_pairs={{0,8},{1,9},{2,10},{3,11},{4,12},{5,13},{6,14},{7,15},{8,0},{9,1},... | collective-permute-start | bytes 516104 | tf_op jit(solution)/shard_map/ppermute | solution.py:29
  61.7 1.0 %collective-permute-done.15.refs_1_ = bf16[24,3584]{1,0:T(8,128)(2,1)S(1)} collective-permute-done((bf16[24,3584]{1,0:T(8,128)(2,1)S(1)}, bf16[24,3584]{1,0:T(8,128)(2,1)S(1)}, u32[]{:S(2)}, u32[]{:S(2)}) %collective-permute-start.15) | collective-permute-done | bytes 172064 | tf_op jit(solution)/shard_map/ppermute | solution.py:29
  62.8 1.6 %collective-permute-start.16 = (bf16[24,3584]{1,0:T(8,128)(2,1)S(1)}, bf16[24,3584]{1,0:T(8,128)(2,1)S(1)}, u32[]{:S(2)}, u32[]{:S(2)}) collective-permute-start(bf16[24,3584]{1,0:T(8,128)(2,1)S(1)} %shard_map.76), channel_id=1, source_target_pairs={{0,4},{1,5},{2,6},{3,7},{4,0},{5,1},{6,2},{7,3},{8,12},{9,13},{10,... | collective-permute-start | bytes 516104 | tf_op jit(solution)/shard_map/ppermute | solution.py:29
  64.3 0.0 collective-permute-done.12.refs_0_
  64.4 1.5 %collective-permute-done.10.refs_1_ = bf16[24,3584]{1,0:T(8,128)(2,1)S(1)} collective-permute-done((bf16[24,3584]{1,0:T(8,128)(2,1)S(1)}, bf16[24,3584]{1,0:T(8,128)(2,1)S(1)}, u32[]{:S(2)}, u32[]{:S(2)}) %collective-permute-start.10) | collective-permute-done | bytes 172064 | tf_op jit(solution)/shard_map/ppermute | solution.py:29
  65.8 6.9 %collective-permute-done.14.refs_3_ = bf16[24,3584]{1,0:T(8,128)(2,1)S(1)} collective-permute-done((bf16[24,3584]{1,0:T(8,128)(2,1)S(1)}, bf16[24,3584]{1,0:T(8,128)(2,1)S(1)}, u32[]{:S(2)}, u32[]{:S(2)}) %collective-permute-start.14) | collective-permute-done | bytes 172064 | tf_op jit(solution)/shard_map/ppermute | solution.py:29
  72.7 0.0 collective-permute-done.16.refs_4_
  72.7 0.9 %shard_map.77 = bf16[12,7168]{1,0:T(8,128)(2,1)} custom-call(bf16[72,3584]{1,0:T(8,128)(2,1)S(1)} %get-tuple-element.18.refs_0_, bf16[24,3584]{1,0:T(8,128)(2,1)S(1)} %collective-permute-done.10.refs_1_, bf16[24,3584]{1,0:T(8,128)(2,1)S(1)} %shard_map.74.refs_2_, bf16[24,3584]{1,0:T(8,128)(2,1)S(1)} %collective-permute-done.14.refs_3_, ...), custom_call_target="tpu_custom_call" | custom-call | flops 1 | bytes 1 | tf_op jit(solution)/shard_map/pallas_call | solution.py:285
  (5 shorter events, 0.2 us)
Async XLA Ops:
  1.8 11.0 %copy-start.1 = (bf16[24,3712]{1,0:T(8,128)(2,1)S(1)}, bf16[24,3712]{1,0:T(8,128)(2,1)}, u32[]{:S(2)}) copy-start(bf16[24,3712]{1,0:T(8,128)(2,1)} %shard_map.64.refs_0_) | copy-start | bytes 534532
  1.8 11.0 %collective-permute-start = (bf16[24,3712]{1,0:T(8,128)(2,1)}, bf16[24,3712]{1,0:T(8,128)(2,1)S(1)}, u32[]{:S(2)}, u32[]{:S(2)}) collective-permute-start(bf16[24,3712]{1,0:T(8,128)(2,1)} %shard_map.64.refs_0_), channel_id=1, source_target_pairs={{0,4},{1,5},{2,6},{3,7},{4,0},{5,1},{6,2},{7,3},{8,12},{9,13},{10,... | collective-permute-start | bytes 534536 | tf_op jit(solution)/shard_map/ppermute | solution.py:29
  4.9 12.0 %collective-permute-start.3 = (bf16[24,3712]{1,0:T(8,128)(2,1)}, bf16[24,3712]{1,0:T(8,128)(2,1)S(1)}, u32[]{:S(2)}, u32[]{:S(2)}) collective-permute-start(bf16[24,3712]{1,0:T(8,128)(2,1)} %shard_map.64.refs_0_), channel_id=1, source_target_pairs={{0,12},{1,13},{2,14},{3,15},{4,8},{5,9},{6,10},{7,11},{8,4},{9,5},... | collective-permute-start | bytes 534536 | tf_op jit(solution)/shard_map/ppermute | solution.py:29
  7.4 16.0 %collective-permute-start.2 = (bf16[24,3712]{1,0:T(8,128)(2,1)}, bf16[24,3712]{1,0:T(8,128)(2,1)S(1)}, u32[]{:S(2)}, u32[]{:S(2)}) collective-permute-start(bf16[24,3712]{1,0:T(8,128)(2,1)} %shard_map.64.refs_0_), channel_id=1, source_target_pairs={{0,8},{1,9},{2,10},{3,11},{4,12},{5,13},{6,14},{7,15},{8,0},{9,1},... | collective-permute-start | bytes 534536 | tf_op jit(solution)/shard_map/ppermute | solution.py:29
  12.8 20.6 %copy-start = (bf16[2,7168,512]{2,1,0:T(8,128)(2,1)S(1)}, bf16[2,7168,512]{2,1,0:T(8,128)(2,1)}, u32[]{:S(2)}) copy-start(bf16[2,7168,512]{2,1,0:T(8,128)(2,1)} %refs_4_.1) | copy-start | bytes 44040196
  12.9 17.4 %collective-permute-start.1 = (bf16[48,3712]{1,0:T(8,128)(2,1)S(1)}, bf16[48,3712]{1,0:T(8,128)(2,1)S(1)}, u32[]{:S(2)}, u32[]{:S(2)}) collective-permute-start(bf16[48,3712]{1,0:T(8,128)(2,1)S(1)} %shard_map.66), channel_id=1, source_target_pairs={{0,2},{1,3},{2,0},{3,1},{4,6},{5,7},{6,4},{7,5},{8,10},{9,11},{10,... | collective-permute-start | bytes 1069064 | tf_op jit(solution)/shard_map/ppermute | solution.py:29
  16.9 10.6 %collective-permute-start.5 = (bf16[24,3712]{1,0:T(8,128)(2,1)S(1)}, bf16[24,3712]{1,0:T(8,128)(2,1)S(1)}, u32[]{:S(2)}, u32[]{:S(2)}) collective-permute-start(bf16[24,3712]{1,0:T(8,128)(2,1)S(1)} %collective-permute-done.3.refs_1_), channel_id=1, source_target_pairs={{0,2},{1,3},{2,0},{3,1},{4,6},{5,7},{6,4},{7,5},{8,10},{9,11},{10,... | collective-permute-start | bytes 534536 | tf_op jit(solution)/shard_map/ppermute | solution.py:29
  23.4 6.7 %collective-permute-start.4 = (bf16[24,3712]{1,0:T(8,128)(2,1)S(1)}, bf16[24,3712]{1,0:T(8,128)(2,1)S(1)}, u32[]{:S(2)}, u32[]{:S(2)}) collective-permute-start(bf16[24,3712]{1,0:T(8,128)(2,1)S(1)} %collective-permute-done.2.refs_0_), channel_id=1, source_target_pairs={{0,2},{1,3},{2,0},{3,1},{4,6},{5,7},{6,4},{7,5},{8,10},{9,11},{10,... | collective-permute-start | bytes 534536 | tf_op jit(solution)/shard_map/ppermute | solution.py:29
  30.2 2.2 %collective-permute-start.7 = (bf16[48,7296]{1,0:T(8,128)(2,1)S(1)}, bf16[48,7296]{1,0:T(8,128)(2,1)S(1)}, u32[]{:S(2)}, u32[]{:S(2)}) collective-permute-start(bf16[48,7296]{1,0:T(8,128)(2,1)S(1)} %shard_map.68.refs_1_), channel_id=1, source_target_pairs={{0,1},{1,0},{2,3},{3,2},{4,5},{5,4},{6,7},{7,6},{8,9},{9,8},{10,11... | collective-permute-start | bytes 2101256 | tf_op jit(solution)/shard_map/ppermute | solution.py:29
  30.4 3.0 %collective-permute-start.6 = (bf16[48,7296]{1,0:T(8,128)(2,1)S(1)}, bf16[48,7296]{1,0:T(8,128)(2,1)S(1)}, u32[]{:S(2)}, u32[]{:S(2)}) collective-permute-start(bf16[48,7296]{1,0:T(8,128)(2,1)S(1)} %shard_map.67.refs_0_), channel_id=1, source_target_pairs={{0,1},{1,0},{2,3},{3,2},{4,5},{5,4},{6,7},{7,6},{8,9},{9,8},{10,11... | collective-permute-start | bytes 2101256 | tf_op jit(solution)/shard_map/ppermute | solution.py:29
  46.0 1.7 %collective-permute-start.8 = (bf16[48,3584]{1,0:T(8,128)(2,1)S(1)}, bf16[48,3584]{1,0:T(8,128)(2,1)S(1)}, u32[]{:S(2)}, u32[]{:S(2)}) collective-permute-start(bf16[48,3584]{1,0:T(8,128)(2,1)S(1)} %get-tuple-element.17), channel_id=1, source_target_pairs={{0,1},{1,0},{2,3},{3,2},{4,5},{5,4},{6,7},{7,6},{8,9},{9,8},{10,11... | collective-permute-start | bytes 1032200 | tf_op jit(solution)/shard_map/ppermute | solution.py:29
  47.8 2.7 %collective-permute-start.9 = (bf16[144,3584]{1,0:T(8,128)(2,1)S(1)}, bf16[144,3584]{1,0:T(8,128)(2,1)S(1)}, u32[]{:S(2)}, u32[]{:S(2)}) collective-permute-start(bf16[144,3584]{1,0:T(8,128)(2,1)S(1)} %shard_map.70), channel_id=1, source_target_pairs={{0,1},{1,0},{2,3},{3,2},{4,5},{5,4},{6,7},{7,6},{8,9},{9,8},{10,11... | collective-permute-start | bytes 3096584 | tf_op jit(solution)/shard_map/ppermute | solution.py:29
  48.1 7.3 %collective-permute-start.11 = (bf16[24,3584]{1,0:T(8,128)(2,1)S(1)}, bf16[24,3584]{1,0:T(8,128)(2,1)S(1)}, u32[]{:S(2)}, u32[]{:S(2)}) collective-permute-start(bf16[24,3584]{1,0:T(8,128)(2,1)S(1)} %get-tuple-element.22), channel_id=1, source_target_pairs={{0,2},{1,3},{2,0},{3,1},{4,6},{5,7},{6,4},{7,5},{8,10},{9,11},{10,... | collective-permute-start | bytes 516104 | tf_op jit(solution)/shard_map/ppermute | solution.py:29
  50.7 8.9 %collective-permute-start.13 = (bf16[24,3584]{1,0:T(8,128)(2,1)S(1)}, bf16[24,3584]{1,0:T(8,128)(2,1)S(1)}, u32[]{:S(2)}, u32[]{:S(2)}) collective-permute-start(bf16[24,3584]{1,0:T(8,128)(2,1)S(1)} %get-tuple-element.23), channel_id=1, source_target_pairs={{0,2},{1,3},{2,0},{3,1},{4,6},{5,7},{6,4},{7,5},{8,10},{9,11},{10,... | collective-permute-start | bytes 516104 | tf_op jit(solution)/shard_map/ppermute | solution.py:29
  52.3 10.4 %collective-permute-start.15 = (bf16[24,3584]{1,0:T(8,128)(2,1)S(1)}, bf16[24,3584]{1,0:T(8,128)(2,1)S(1)}, u32[]{:S(2)}, u32[]{:S(2)}) collective-permute-start(bf16[24,3584]{1,0:T(8,128)(2,1)S(1)} %get-tuple-element.24), channel_id=1, source_target_pairs={{0,2},{1,3},{2,0},{3,1},{4,6},{5,7},{6,4},{7,5},{8,10},{9,11},{10,... | collective-permute-start | bytes 516104 | tf_op jit(solution)/shard_map/ppermute | solution.py:29
  55.4 9.0 %collective-permute-start.12 = (bf16[24,3584]{1,0:T(8,128)(2,1)S(1)}, bf16[24,3584]{1,0:T(8,128)(2,1)S(1)}, u32[]{:S(2)}, u32[]{:S(2)}) collective-permute-start(bf16[24,3584]{1,0:T(8,128)(2,1)S(1)} %shard_map.73), channel_id=1, source_target_pairs={{0,12},{1,13},{2,14},{3,15},{4,8},{5,9},{6,10},{7,11},{8,4},{9,5},... | collective-permute-start | bytes 516104 | tf_op jit(solution)/shard_map/ppermute | solution.py:29
  58.1 7.8 %collective-permute-start.10 = (bf16[24,3584]{1,0:T(8,128)(2,1)S(1)}, bf16[24,3584]{1,0:T(8,128)(2,1)S(1)}, u32[]{:S(2)}, u32[]{:S(2)}) collective-permute-start(bf16[24,3584]{1,0:T(8,128)(2,1)S(1)} %get-tuple-element.19), channel_id=1, source_target_pairs={{0,2},{1,3},{2,0},{3,1},{4,6},{5,7},{6,4},{7,5},{8,10},{9,11},{10,... | collective-permute-start | bytes 516104 | tf_op jit(solution)/shard_map/ppermute | solution.py:29
  59.7 13.1 %collective-permute-start.14 = (bf16[24,3584]{1,0:T(8,128)(2,1)S(1)}, bf16[24,3584]{1,0:T(8,128)(2,1)S(1)}, u32[]{:S(2)}, u32[]{:S(2)}) collective-permute-start(bf16[24,3584]{1,0:T(8,128)(2,1)S(1)} %shard_map.75), channel_id=1, source_target_pairs={{0,8},{1,9},{2,10},{3,11},{4,12},{5,13},{6,14},{7,15},{8,0},{9,1},... | collective-permute-start | bytes 516104 | tf_op jit(solution)/shard_map/ppermute | solution.py:29
  62.8 10.0 %collective-permute-start.16 = (bf16[24,3584]{1,0:T(8,128)(2,1)S(1)}, bf16[24,3584]{1,0:T(8,128)(2,1)S(1)}, u32[]{:S(2)}, u32[]{:S(2)}) collective-permute-start(bf16[24,3584]{1,0:T(8,128)(2,1)S(1)} %shard_map.76), channel_id=1, source_target_pairs={{0,4},{1,5},{2,6},{3,7},{4,0},{5,1},{6,2},{7,3},{8,12},{9,13},{10,... | collective-permute-start | bytes 516104 | tf_op jit(solution)/shard_map/ppermute | solution.py:29

commit v6 on v5

--- a/solution.py
+++ b/solution.py
@@ -12,11 +12,12 @@
 LANES = 128
 TILE = 8
 MIB = 1 << 20
+GATE_CHUNKS = 2
 DOWN_CHUNKS = 4
 SMALL_VMEM = 8 * MIB
 PREPARE_VMEM = 58 * MIB
 FIRST_VMEM = 36 * MIB
-STEP_VMEM = 14 * MIB
+STEP_VMEM = 15 * MIB
 DOWN_RING = 4
 SMALL_COST = pl.CostEstimate(flops=1, bytes_accessed=1, transcendentals=0)
 LOAD_COST = pl.CostEstimate(flops=1, bytes_accessed=1 << 24, transcendentals=0)
@@ -202,27 +203,28 @@
     for step in range(slots):
         for copy in fetch(step):
             copy.start()
+    group = lax.axis_index("wide") // (lax.axis_size("wide") // GROUPS)
     at = 0
-    scales = []
-    group = lax.axis_index("wide") // (lax.axis_size("wide") // GROUPS)
     for ref in blocks:
-        rows = slice(at, at + ref.shape[0])
-        lhs_ref[rows, :] = ref[:, :width]
-        route = ref[:, width:].astype(f32)
-        lane = lax.broadcasted_iota(jnp.int32, route.shape, 1)
-        scales.append(
-            [
-                jnp.sum(jnp.where(lane == group * EXP_G + expert, route, 0.0), 1, keepdims=True)
-                for expert in range(EXP_G)
-            ]
-        )
-        at = rows.stop
-    for expert in range(EXP_G):
-        gate_value = jnp.dot(lhs_ref[...], gate_ref[expert], preferred_element_type=f32)
-        lifted = jnp.dot(lhs_ref[...], up_ref[expert], preferred_element_type=f32)
-        value = gate_value / (1.0 + jnp.exp(-gate_value)) * lifted
-        scale = jnp.concatenate([pair[expert] for pair in scales], 0)
-        hidden_ref[expert] = (value * scale).astype(bf16)
+        lhs_ref[at : at + ref.shape[0], :] = ref[:, :width]
+        at += ref.shape[0]
+    part = depth // GATE_CHUNKS
+
+    def hidden_part(i, carry):
+        expert = i // GATE_CHUNKS
+        columns = pl.ds(pl.multiple_of(i % GATE_CHUNKS * part, part), part)
+        gate_value = jnp.dot(lhs_ref[...], gate_ref[expert, :, columns], preferred_element_type=f32)
+        lifted = jnp.dot(lhs_ref[...], up_ref[expert, :, columns], preferred_element_type=f32)
+        scales = []
+        for ref in blocks:
+            route = ref[:, width:].astype(f32)
+            lane = lax.broadcasted_iota(jnp.int32, route.shape, 1)
+            scales.append(jnp.sum(jnp.where(lane == group * EXP_G + expert, route, 0.0), 1, keepdims=True))
+        value = gate_value / (1.0 + jnp.exp(-gate_value)) * lifted * jnp.concatenate(scales, 0)
+        hidden_ref[expert, :, columns] = value.astype(bf16)
+        return carry
+
+    lax.fori_loop(0, EXP_G * GATE_CHUNKS, hidden_part, 0)
     places = []
     for far_ref, ref in ((keep_far_ref, keep_ref), (send_far_ref, send_ref)):
         for first in range(0, far, 2):

time: 73.8 us -> 72.6 us (0.984)
  Pallas kernels: 21.3 us -> 20.1 us
    pallas_call x1, Pallas kernels: 12.5 us -> 11.4 us  [expert_step(): pl.pallas_call(functools.partial(expert_kernel, unit, far, len(blocks)),...]
where the time goes in v6:
time: 72.6 us; the launch traced here: 72.4 us
  waiting for transfers between devices  29.4 us (40%)
  starting transfers between devices  22.8 us (31%)
  Pallas kernels  20.1 us (28%)
    ppermute x17, waiting for transfers between devices, swap(): return lax.ppermute(block, 'wide', [(i, i ^ bits) for i in range(count)])  29.4 us
    ppermute x17, starting transfers between devices, swap(): return lax.ppermute(block, 'wide', [(i, i ^ bits) for i in range(count)])  22.8 us
    pallas_call x1, Pallas kernels, expert_step(): pl.pallas_call(functools.partial(expert_kernel, unit, far, len(blocks)),...  11.4 us
    pallas_call x13, Pallas kernels, call_small(): pl.pallas_call(body, out_shape=shapes, in_specs=[vmem] * len(args) + [pl....  8.74 us
  transfers between devices with their start and end apart: 17, of which 12 were waited for; matrix products, arithmetic and copies ran while one was open for 0% of the time, Pallas kernels for 8%

profile of v6, /device:TPU:0, one launch (start us, length us, event | category | flops | bytes accessed | tf_op | source)
XLA Modules:
  0.0 72.4 jit_solution(6670770372717010832)
XLA Ops:
  0.0 1.8 %shard_map.64.refs_0_ = bf16[24,3712]{1,0:T(8,128)(2,1)} custom-call(bf16[12,7168]{1,0:T(8,128)(2,1)} %refs_0_.2, s32[8,12]{1,0:T(8,128)} %bitcast.2, f32[8,12]{1,0:T(8,128)} %bitcast.3), custom_call_target="tpu_custom_call" | custom-call | flops 1 | bytes 1 | tf_op jit(solution)/shard_map/pallas_call | solution.py:287
  1.8 0.0 copy-start.1
  1.8 3.1 %collective-permute-start = (bf16[24,3712]{1,0:T(8,128)(2,1)}, bf16[24,3712]{1,0:T(8,128)(2,1)S(1)}, u32[]{:S(2)}, u32[]{:S(2)}) collective-permute-start(bf16[24,3712]{1,0:T(8,128)(2,1)} %shard_map.64.refs_0_), channel_id=1, source_target_pairs={{0,4},{1,5},{2,6},{3,7},{4,0},{5,1},{6,2},{7,3},{8,12},{9,13},{10,... | collective-permute-start | bytes 534536 | tf_op jit(solution)/shard_map/ppermute | solution.py:30
  4.9 2.5 %collective-permute-start.3 = (bf16[24,3712]{1,0:T(8,128)(2,1)}, bf16[24,3712]{1,0:T(8,128)(2,1)S(1)}, u32[]{:S(2)}, u32[]{:S(2)}) collective-permute-start(bf16[24,3712]{1,0:T(8,128)(2,1)} %shard_map.64.refs_0_), channel_id=1, source_target_pairs={{0,12},{1,13},{2,14},{3,15},{4,8},{5,9},{6,10},{7,11},{8,4},{9,5},... | collective-permute-start | bytes 534536 | tf_op jit(solution)/shard_map/ppermute | solution.py:30
  7.4 0.1 collective-permute-start.2
  7.5 5.3 %shard_map.65.refs_2_.refs_5_ = bf16[2,7168,512]{2,1,0:T(8,128)(2,1)S(1)} custom-call(bf16[2,7168,512]{2,1,0:T(8,128)(2,1)} %refs_0_.3), custom_call_target="tpu_custom_call" | custom-call | flops 1 | bytes 16777216 | tf_op jit(solution)/shard_map/pallas_call | solution.py:287
  12.8 0.0 copy-start
  12.9 0.0 collective-permute-done.refs_1_
  12.9 0.0 copy-done.1
  12.9 1.6 %collective-permute-start.1 = (bf16[48,3712]{1,0:T(8,128)(2,1)S(1)}, bf16[48,3712]{1,0:T(8,128)(2,1)S(1)}, u32[]{:S(2)}, u32[]{:S(2)}) collective-permute-start(bf16[48,3712]{1,0:T(8,128)(2,1)S(1)} %shard_map.66), channel_id=1, source_target_pairs={{0,2},{1,3},{2,0},{3,1},{4,6},{5,7},{6,4},{7,5},{8,10},{9,11},{10,... | collective-permute-start | bytes 1069064 | tf_op jit(solution)/shard_map/ppermute | solution.py:30
  14.5 2.4 %collective-permute-done.3.refs_1_ = bf16[24,3712]{1,0:T(8,128)(2,1)S(1)} collective-permute-done((bf16[24,3712]{1,0:T(8,128)(2,1)}, bf16[24,3712]{1,0:T(8,128)(2,1)S(1)}, u32[]{:S(2)}, u32[]{:S(2)}) %collective-permute-start.3) | collective-permute-done | bytes 178208 | tf_op jit(solution)/shard_map/ppermute | solution.py:30
  16.9 1.5 %collective-permute-start.5 = (bf16[24,3712]{1,0:T(8,128)(2,1)S(1)}, bf16[24,3712]{1,0:T(8,128)(2,1)S(1)}, u32[]{:S(2)}, u32[]{:S(2)}) collective-permute-start(bf16[24,3712]{1,0:T(8,128)(2,1)S(1)} %collective-permute-done.3.refs_1_), channel_id=1, source_target_pairs={{0,2},{1,3},{2,0},{3,1},{4,6},{5,7},{6,4},{7,5},{8,10},{9,11},{10,... | collective-permute-start | bytes 534536 | tf_op jit(solution)/shard_map/ppermute | solution.py:30
  18.4 5.0 %collective-permute-done.2.refs_0_ = bf16[24,3712]{1,0:T(8,128)(2,1)S(1)} collective-permute-done((bf16[24,3712]{1,0:T(8,128)(2,1)}, bf16[24,3712]{1,0:T(8,128)(2,1)S(1)}, u32[]{:S(2)}, u32[]{:S(2)}) %collective-permute-start.2) | collective-permute-done | bytes 178208 | tf_op jit(solution)/shard_map/ppermute | solution.py:30
  23.4 1.5 %collective-permute-start.4 = (bf16[24,3712]{1,0:T(8,128)(2,1)S(1)}, bf16[24,3712]{1,0:T(8,128)(2,1)S(1)}, u32[]{:S(2)}, u32[]{:S(2)}) collective-permute-start(bf16[24,3712]{1,0:T(8,128)(2,1)S(1)} %collective-permute-done.2.refs_0_), channel_id=1, source_target_pairs={{0,2},{1,3},{2,0},{3,1},{4,6},{5,7},{6,4},{7,5},{8,10},{9,11},{10,... | collective-permute-start | bytes 534536 | tf_op jit(solution)/shard_map/ppermute | solution.py:30
  25.0 2.6 %collective-permute-done.5.refs_3_ = bf16[24,3712]{1,0:T(8,128)(2,1)S(1)} collective-permute-done((bf16[24,3712]{1,0:T(8,128)(2,1)S(1)}, bf16[24,3712]{1,0:T(8,128)(2,1)S(1)}, u32[]{:S(2)}, u32[]{:S(2)}) %collective-permute-start.5) | collective-permute-done | bytes 178208 | tf_op jit(solution)/shard_map/ppermute | solution.py:30
  27.5 2.6 %collective-permute-done.4.refs_2_ = bf16[24,3712]{1,0:T(8,128)(2,1)S(1)} collective-permute-done((bf16[24,3712]{1,0:T(8,128)(2,1)S(1)}, bf16[24,3712]{1,0:T(8,128)(2,1)S(1)}, u32[]{:S(2)}, u32[]{:S(2)}) %collective-permute-start.4) | collective-permute-done | bytes 178208 | tf_op jit(solution)/shard_map/ppermute | solution.py:30
  30.1 0.1 shard_map.68.refs_1_
  30.2 0.1 collective-permute-start.7
  30.3 0.0 collective-permute-done.1.refs_2_.refs_3_
  30.3 0.1 shard_map.67.refs_0_
  30.4 0.6 collective-permute-start.6
  31.0 1.5 %collective-permute-done.7.refs_3_ = bf16[48,7296]{1,0:T(8,128)(2,1)S(1)} collective-permute-done((bf16[48,7296]{1,0:T(8,128)(2,1)S(1)}, bf16[48,7296]{1,0:T(8,128)(2,1)S(1)}, u32[]{:S(2)}, u32[]{:S(2)}) %collective-permute-start.7) | collective-permute-done | bytes 700448 | tf_op jit(solution)/shard_map/ppermute | solution.py:30
  32.4 1.0 %collective-permute-done.6.refs_2_ = bf16[48,7296]{1,0:T(8,128)(2,1)S(1)} collective-permute-done((bf16[48,7296]{1,0:T(8,128)(2,1)S(1)}, bf16[48,7296]{1,0:T(8,128)(2,1)S(1)}, u32[]{:S(2)}, u32[]{:S(2)}) %collective-permute-start.6) | collective-permute-done | bytes 700448 | tf_op jit(solution)/shard_map/ppermute | solution.py:30
  33.4 0.0 copy-done
  33.4 11.4 %shard_map.69 = (bf16[48,3584]{1,0:T(8,128)(2,1)S(1)}, bf16[48,3584]{1,0:T(8,128)(2,1)S(1)}, bf16[144,3584]{1,0:T(8,128)(2,1)S(1)}, bf16[144,3584]{1,0:T(8,128)(2,1)S(1)}) custom-call(bf16[48,7296]{1,0:T(8,128)(2,1)S(1)} %shard_map.67.refs_0_, bf16[48,7296]{1,0:T(8,128)(2,1)S(1)} %shard_map.68.refs_1_, bf16[48,7296]{1,0:T(8,128)(2,1)S(1)} %collective-permute-done.6.refs_2_, ...), custom_call_target="tpu_custom_call" | custom-call | flops 536870912 | bytes 1 | tf_op jit(solution)/shard_map/pallas_call | solution.py:264
  44.8 0.2 collective-permute-start.8
  45.0 1.5 %collective-permute-done.8.refs_1_ = bf16[48,3584]{1,0:T(8,128)(2,1)S(1)} collective-permute-done((bf16[48,3584]{1,0:T(8,128)(2,1)S(1)}, bf16[48,3584]{1,0:T(8,128)(2,1)S(1)}, u32[]{:S(2)}, u32[]{:S(2)}) %collective-permute-start.8) | collective-permute-done | bytes 344096 | tf_op jit(solution)/shard_map/ppermute | solution.py:30
  46.5 0.1 shard_map.70
  46.6 0.2 collective-permute-start.9
  46.8 0.1 shard_map.72
  46.9 1.6 %collective-permute-start.11 = (bf16[24,3584]{1,0:T(8,128)(2,1)S(1)}, bf16[24,3584]{1,0:T(8,128)(2,1)S(1)}, u32[]{:S(2)}, u32[]{:S(2)}) collective-permute-start(bf16[24,3584]{1,0:T(8,128)(2,1)S(1)} %get-tuple-element.22), channel_id=1, source_target_pairs={{0,2},{1,3},{2,0},{3,1},{4,6},{5,7},{6,4},{7,5},{8,10},{9,11},{10,... | collective-permute-start | bytes 516104 | tf_op jit(solution)/shard_map/ppermute | solution.py:30
  48.5 0.8 %collective-permute-done.9.refs_1_ = bf16[144,3584]{1,0:T(8,128)(2,1)S(1)} collective-permute-done((bf16[144,3584]{1,0:T(8,128)(2,1)S(1)}, bf16[144,3584]{1,0:T(8,128)(2,1)S(1)}, u32[]{:S(2)}, u32[]{:S(2)}) %collective-permute-start.9) | collective-permute-done | bytes 1032224 | tf_op jit(solution)/shard_map/ppermute | solution.py:30
  49.3 0.2 shard_map.71
  49.5 1.6 %collective-permute-start.13 = (bf16[24,3584]{1,0:T(8,128)(2,1)S(1)}, bf16[24,3584]{1,0:T(8,128)(2,1)S(1)}, u32[]{:S(2)}, u32[]{:S(2)}) collective-permute-start(bf16[24,3584]{1,0:T(8,128)(2,1)S(1)} %get-tuple-element.23), channel_id=1, source_target_pairs={{0,2},{1,3},{2,0},{3,1},{4,6},{5,7},{6,4},{7,5},{8,10},{9,11},{10,... | collective-permute-start | bytes 516104 | tf_op jit(solution)/shard_map/ppermute | solution.py:30
  51.1 0.5 collective-permute-start.15
  51.6 2.5 %collective-permute-done.11.refs_1_ = bf16[24,3584]{1,0:T(8,128)(2,1)S(1)} collective-permute-done((bf16[24,3584]{1,0:T(8,128)(2,1)S(1)}, bf16[24,3584]{1,0:T(8,128)(2,1)S(1)}, u32[]{:S(2)}, u32[]{:S(2)}) %collective-permute-start.11) | collective-permute-done | bytes 172064 | tf_op jit(solution)/shard_map/ppermute | solution.py:30
  54.2 2.7 %collective-permute-start.12 = (bf16[24,3584]{1,0:T(8,128)(2,1)S(1)}, bf16[24,3584]{1,0:T(8,128)(2,1)S(1)}, u32[]{:S(2)}, u32[]{:S(2)}) collective-permute-start(bf16[24,3584]{1,0:T(8,128)(2,1)S(1)} %shard_map.73), channel_id=1, source_target_pairs={{0,12},{1,13},{2,14},{3,15},{4,8},{5,9},{6,10},{7,11},{8,4},{9,5},... | collective-permute-start | bytes 516104 | tf_op jit(solution)/shard_map/ppermute | solution.py:30
  56.9 1.5 %collective-permute-start.10 = (bf16[24,3584]{1,0:T(8,128)(2,1)S(1)}, bf16[24,3584]{1,0:T(8,128)(2,1)S(1)}, u32[]{:S(2)}, u32[]{:S(2)}) collective-permute-start(bf16[24,3584]{1,0:T(8,128)(2,1)S(1)} %get-tuple-element.19), channel_id=1, source_target_pairs={{0,2},{1,3},{2,0},{3,1},{4,6},{5,7},{6,4},{7,5},{8,10},{9,11},{10,... | collective-permute-start | bytes 516104 | tf_op jit(solution)/shard_map/ppermute | solution.py:30
  58.4 0.0 collective-permute-done.13.refs_1_
  58.5 2.0 %collective-permute-start.14 = (bf16[24,3584]{1,0:T(8,128)(2,1)S(1)}, bf16[24,3584]{1,0:T(8,128)(2,1)S(1)}, u32[]{:S(2)}, u32[]{:S(2)}) collective-permute-start(bf16[24,3584]{1,0:T(8,128)(2,1)S(1)} %shard_map.75), channel_id=1, source_target_pairs={{0,8},{1,9},{2,10},{3,11},{4,12},{5,13},{6,14},{7,15},{8,0},{9,1},... | collective-permute-start | bytes 516104 | tf_op jit(solution)/shard_map/ppermute | solution.py:30
  60.5 1.1 %collective-permute-done.15.refs_1_ = bf16[24,3584]{1,0:T(8,128)(2,1)S(1)} collective-permute-done((bf16[24,3584]{1,0:T(8,128)(2,1)S(1)}, bf16[24,3584]{1,0:T(8,128)(2,1)S(1)}, u32[]{:S(2)}, u32[]{:S(2)}) %collective-permute-start.15) | collective-permute-done | bytes 172064 | tf_op jit(solution)/shard_map/ppermute | solution.py:30
  61.6 1.6 %collective-permute-start.16 = (bf16[24,3584]{1,0:T(8,128)(2,1)S(1)}, bf16[24,3584]{1,0:T(8,128)(2,1)S(1)}, u32[]{:S(2)}, u32[]{:S(2)}) collective-permute-start(bf16[24,3584]{1,0:T(8,128)(2,1)S(1)} %shard_map.76), channel_id=1, source_target_pairs={{0,4},{1,5},{2,6},{3,7},{4,0},{5,1},{6,2},{7,3},{8,12},{9,13},{10,... | collective-permute-start | bytes 516104 | tf_op jit(solution)/shard_map/ppermute | solution.py:30
  63.2 0.0 collective-permute-done.12.refs_0_
  63.2 1.5 %collective-permute-done.10.refs_1_ = bf16[24,3584]{1,0:T(8,128)(2,1)S(1)} collective-permute-done((bf16[24,3584]{1,0:T(8,128)(2,1)S(1)}, bf16[24,3584]{1,0:T(8,128)(2,1)S(1)}, u32[]{:S(2)}, u32[]{:S(2)}) %collective-permute-start.10) | collective-permute-done | bytes 172064 | tf_op jit(solution)/shard_map/ppermute | solution.py:30
  64.7 6.9 %collective-permute-done.14.refs_3_ = bf16[24,3584]{1,0:T(8,128)(2,1)S(1)} collective-permute-done((bf16[24,3584]{1,0:T(8,128)(2,1)S(1)}, bf16[24,3584]{1,0:T(8,128)(2,1)S(1)}, u32[]{:S(2)}, u32[]{:S(2)}) %collective-permute-start.14) | collective-permute-done | bytes 172064 | tf_op jit(solution)/shard_map/ppermute | solution.py:30
  71.6 0.0 collective-permute-done.16.refs_4_
  71.6 0.9 %shard_map.77 = bf16[12,7168]{1,0:T(8,128)(2,1)} custom-call(bf16[72,3584]{1,0:T(8,128)(2,1)S(1)} %get-tuple-element.18.refs_0_, bf16[24,3584]{1,0:T(8,128)(2,1)S(1)} %collective-permute-done.10.refs_1_, bf16[24,3584]{1,0:T(8,128)(2,1)S(1)} %shard_map.74.refs_2_, bf16[24,3584]{1,0:T(8,128)(2,1)S(1)} %collective-permute-done.14.refs_3_, ...), custom_call_target="tpu_custom_call" | custom-call | flops 1 | bytes 1 | tf_op jit(solution)/shard_map/pallas_call | solution.py:287
  (5 shorter events, 0.2 us)
Async XLA Ops:
  1.8 11.0 %copy-start.1 = (bf16[24,3712]{1,0:T(8,128)(2,1)S(1)}, bf16[24,3712]{1,0:T(8,128)(2,1)}, u32[]{:S(2)}) copy-start(bf16[24,3712]{1,0:T(8,128)(2,1)} %shard_map.64.refs_0_) | copy-start | bytes 534532
  1.8 11.0 %collective-permute-start = (bf16[24,3712]{1,0:T(8,128)(2,1)}, bf16[24,3712]{1,0:T(8,128)(2,1)S(1)}, u32[]{:S(2)}, u32[]{:S(2)}) collective-permute-start(bf16[24,3712]{1,0:T(8,128)(2,1)} %shard_map.64.refs_0_), channel_id=1, source_target_pairs={{0,4},{1,5},{2,6},{3,7},{4,0},{5,1},{6,2},{7,3},{8,12},{9,13},{10,... | collective-permute-start | bytes 534536 | tf_op jit(solution)/shard_map/ppermute | solution.py:30
  4.9 12.0 %collective-permute-start.3 = (bf16[24,3712]{1,0:T(8,128)(2,1)}, bf16[24,3712]{1,0:T(8,128)(2,1)S(1)}, u32[]{:S(2)}, u32[]{:S(2)}) collective-permute-start(bf16[24,3712]{1,0:T(8,128)(2,1)} %shard_map.64.refs_0_), channel_id=1, source_target_pairs={{0,12},{1,13},{2,14},{3,15},{4,8},{5,9},{6,10},{7,11},{8,4},{9,5},... | collective-permute-start | bytes 534536 | tf_op jit(solution)/shard_map/ppermute | solution.py:30
  7.4 16.0 %collective-permute-start.2 = (bf16[24,3712]{1,0:T(8,128)(2,1)}, bf16[24,3712]{1,0:T(8,128)(2,1)S(1)}, u32[]{:S(2)}, u32[]{:S(2)}) collective-permute-start(bf16[24,3712]{1,0:T(8,128)(2,1)} %shard_map.64.refs_0_), channel_id=1, source_target_pairs={{0,8},{1,9},{2,10},{3,11},{4,12},{5,13},{6,14},{7,15},{8,0},{9,1},... | collective-permute-start | bytes 534536 | tf_op jit(solution)/shard_map/ppermute | solution.py:30
  12.8 20.6 %copy-start = (bf16[2,7168,512]{2,1,0:T(8,128)(2,1)S(1)}, bf16[2,7168,512]{2,1,0:T(8,128)(2,1)}, u32[]{:S(2)}) copy-start(bf16[2,7168,512]{2,1,0:T(8,128)(2,1)} %refs_4_.1) | copy-start | bytes 44040196
  12.9 17.4 %collective-permute-start.1 = (bf16[48,3712]{1,0:T(8,128)(2,1)S(1)}, bf16[48,3712]{1,0:T(8,128)(2,1)S(1)}, u32[]{:S(2)}, u32[]{:S(2)}) collective-permute-start(bf16[48,3712]{1,0:T(8,128)(2,1)S(1)} %shard_map.66), channel_id=1, source_target_pairs={{0,2},{1,3},{2,0},{3,1},{4,6},{5,7},{6,4},{7,5},{8,10},{9,11},{10,... | collective-permute-start | bytes 1069064 | tf_op jit(solution)/shard_map/ppermute | solution.py:30
  16.9 10.6 %collective-permute-start.5 = (bf16[24,3712]{1,0:T(8,128)(2,1)S(1)}, bf16[24,3712]{1,0:T(8,128)(2,1)S(1)}, u32[]{:S(2)}, u32[]{:S(2)}) collective-permute-start(bf16[24,3712]{1,0:T(8,128)(2,1)S(1)} %collective-permute-done.3.refs_1_), channel_id=1, source_target_pairs={{0,2},{1,3},{2,0},{3,1},{4,6},{5,7},{6,4},{7,5},{8,10},{9,11},{10,... | collective-permute-start | bytes 534536 | tf_op jit(solution)/shard_map/ppermute | solution.py:30
  23.4 6.7 %collective-permute-start.4 = (bf16[24,3712]{1,0:T(8,128)(2,1)S(1)}, bf16[24,3712]{1,0:T(8,128)(2,1)S(1)}, u32[]{:S(2)}, u32[]{:S(2)}) collective-permute-start(bf16[24,3712]{1,0:T(8,128)(2,1)S(1)} %collective-permute-done.2.refs_0_), channel_id=1, source_target_pairs={{0,2},{1,3},{2,0},{3,1},{4,6},{5,7},{6,4},{7,5},{8,10},{9,11},{10,... | collective-permute-start | bytes 534536 | tf_op jit(solution)/shard_map/ppermute | solution.py:30
  30.2 2.2 %collective-permute-start.7 = (bf16[48,7296]{1,0:T(8,128)(2,1)S(1)}, bf16[48,7296]{1,0:T(8,128)(2,1)S(1)}, u32[]{:S(2)}, u32[]{:S(2)}) collective-permute-start(bf16[48,7296]{1,0:T(8,128)(2,1)S(1)} %shard_map.68.refs_1_), channel_id=1, source_target_pairs={{0,1},{1,0},{2,3},{3,2},{4,5},{5,4},{6,7},{7,6},{8,9},{9,8},{10,11... | collective-permute-start | bytes 2101256 | tf_op jit(solution)/shard_map/ppermute | solution.py:30
  30.4 3.0 %collective-permute-start.6 = (bf16[48,7296]{1,0:T(8,128)(2,1)S(1)}, bf16[48,7296]{1,0:T(8,128)(2,1)S(1)}, u32[]{:S(2)}, u32[]{:S(2)}) collective-permute-start(bf16[48,7296]{1,0:T(8,128)(2,1)S(1)} %shard_map.67.refs_0_), channel_id=1, source_target_pairs={{0,1},{1,0},{2,3},{3,2},{4,5},{5,4},{6,7},{7,6},{8,9},{9,8},{10,11... | collective-permute-start | bytes 2101256 | tf_op jit(solution)/shard_map/ppermute | solution.py:30
  44.8 1.7 %collective-permute-start.8 = (bf16[48,3584]{1,0:T(8,128)(2,1)S(1)}, bf16[48,3584]{1,0:T(8,128)(2,1)S(1)}, u32[]{:S(2)}, u32[]{:S(2)}) collective-permute-start(bf16[48,3584]{1,0:T(8,128)(2,1)S(1)} %get-tuple-element.17), channel_id=1, source_target_pairs={{0,1},{1,0},{2,3},{3,2},{4,5},{5,4},{6,7},{7,6},{8,9},{9,8},{10,11... | collective-permute-start | bytes 1032200 | tf_op jit(solution)/shard_map/ppermute | solution.py:30
  46.6 2.7 %collective-permute-start.9 = (bf16[144,3584]{1,0:T(8,128)(2,1)S(1)}, bf16[144,3584]{1,0:T(8,128)(2,1)S(1)}, u32[]{:S(2)}, u32[]{:S(2)}) collective-permute-start(bf16[144,3584]{1,0:T(8,128)(2,1)S(1)} %shard_map.70), channel_id=1, source_target_pairs={{0,1},{1,0},{2,3},{3,2},{4,5},{5,4},{6,7},{7,6},{8,9},{9,8},{10,11... | collective-permute-start | bytes 3096584 | tf_op jit(solution)/shard_map/ppermute | solution.py:30
  46.9 7.3 %collective-permute-start.11 = (bf16[24,3584]{1,0:T(8,128)(2,1)S(1)}, bf16[24,3584]{1,0:T(8,128)(2,1)S(1)}, u32[]{:S(2)}, u32[]{:S(2)}) collective-permute-start(bf16[24,3584]{1,0:T(8,128)(2,1)S(1)} %get-tuple-element.22), channel_id=1, source_target_pairs={{0,2},{1,3},{2,0},{3,1},{4,6},{5,7},{6,4},{7,5},{8,10},{9,11},{10,... | collective-permute-start | bytes 516104 | tf_op jit(solution)/shard_map/ppermute | solution.py:30
  49.5 8.9 %collective-permute-start.13 = (bf16[24,3584]{1,0:T(8,128)(2,1)S(1)}, bf16[24,3584]{1,0:T(8,128)(2,1)S(1)}, u32[]{:S(2)}, u32[]{:S(2)}) collective-permute-start(bf16[24,3584]{1,0:T(8,128)(2,1)S(1)} %get-tuple-element.23), channel_id=1, source_target_pairs={{0,2},{1,3},{2,0},{3,1},{4,6},{5,7},{6,4},{7,5},{8,10},{9,11},{10,... | collective-permute-start | bytes 516104 | tf_op jit(solution)/shard_map/ppermute | solution.py:30
  51.1 10.4 %collective-permute-start.15 = (bf16[24,3584]{1,0:T(8,128)(2,1)S(1)}, bf16[24,3584]{1,0:T(8,128)(2,1)S(1)}, u32[]{:S(2)}, u32[]{:S(2)}) collective-permute-start(bf16[24,3584]{1,0:T(8,128)(2,1)S(1)} %get-tuple-element.24), channel_id=1, source_target_pairs={{0,2},{1,3},{2,0},{3,1},{4,6},{5,7},{6,4},{7,5},{8,10},{9,11},{10,... | collective-permute-start | bytes 516104 | tf_op jit(solution)/shard_map/ppermute | solution.py:30
  54.2 9.0 %collective-permute-start.12 = (bf16[24,3584]{1,0:T(8,128)(2,1)S(1)}, bf16[24,3584]{1,0:T(8,128)(2,1)S(1)}, u32[]{:S(2)}, u32[]{:S(2)}) collective-permute-start(bf16[24,3584]{1,0:T(8,128)(2,1)S(1)} %shard_map.73), channel_id=1, source_target_pairs={{0,12},{1,13},{2,14},{3,15},{4,8},{5,9},{6,10},{7,11},{8,4},{9,5},... | collective-permute-start | bytes 516104 | tf_op jit(solution)/shard_map/ppermute | solution.py:30
  56.9 7.7 %collective-permute-start.10 = (bf16[24,3584]{1,0:T(8,128)(2,1)S(1)}, bf16[24,3584]{1,0:T(8,128)(2,1)S(1)}, u32[]{:S(2)}, u32[]{:S(2)}) collective-permute-start(bf16[24,3584]{1,0:T(8,128)(2,1)S(1)} %get-tuple-element.19), channel_id=1, source_target_pairs={{0,2},{1,3},{2,0},{3,1},{4,6},{5,7},{6,4},{7,5},{8,10},{9,11},{10,... | collective-permute-start | bytes 516104 | tf_op jit(solution)/shard_map/ppermute | solution.py:30
  58.5 13.1 %collective-permute-start.14 = (bf16[24,3584]{1,0:T(8,128)(2,1)S(1)}, bf16[24,3584]{1,0:T(8,128)(2,1)S(1)}, u32[]{:S(2)}, u32[]{:S(2)}) collective-permute-start(bf16[24,3584]{1,0:T(8,128)(2,1)S(1)} %shard_map.75), channel_id=1, source_target_pairs={{0,8},{1,9},{2,10},{3,11},{4,12},{5,13},{6,14},{7,15},{8,0},{9,1},... | collective-permute-start | bytes 516104 | tf_op jit(solution)/shard_map/ppermute | solution.py:30
  61.6 10.0 %collective-permute-start.16 = (bf16[24,3584]{1,0:T(8,128)(2,1)S(1)}, bf16[24,3584]{1,0:T(8,128)(2,1)S(1)}, u32[]{:S(2)}, u32[]{:S(2)}) collective-permute-start(bf16[24,3584]{1,0:T(8,128)(2,1)S(1)} %shard_map.76), channel_id=1, source_target_pairs={{0,4},{1,5},{2,6},{3,7},{4,0},{5,1},{6,2},{7,3},{8,12},{9,13},{10,... | collective-permute-start | bytes 516104 | tf_op jit(solution)/shard_map/ppermute | solution.py:30

commit v7 on v6

--- a/solution.py
+++ b/solution.py
@@ -16,7 +16,7 @@
 DOWN_CHUNKS = 4
 SMALL_VMEM = 8 * MIB
 PREPARE_VMEM = 58 * MIB
-FIRST_VMEM = 36 * MIB
+FIRST_VMEM = 30 * MIB
 STEP_VMEM = 15 * MIB
 DOWN_RING = 4
 SMALL_COST = pl.CostEstimate(flops=1, bytes_accessed=1, transcendentals=0)
@@ -364,8 +364,9 @@
     whole = prepare(tokens, expert_ids, gates)
     blocks = [whole] + [swap(whole, 4 * f, count) for f in range(1, far)]
     gate, up = w_gate, preload(w_up, FIRST_VMEM)
-    pair = swap(stack(blocks[:2], up), 2, count)
-    nexts = [(pair, 0), (pair, 1)] + [(swap(block, 2, count), 0) for block in blocks[2:]]
+    pair = swap(stack(blocks[:2]), 2, count)
+    nexts = [(pair, 0), (pair, 1)]
+    nexts += [(swap(hold(block, up) if f == far - 2 else block, 2, count), 0) for f, block in enumerate(blocks) if f > 1]
     blocks = [(block, 0) for block in blocks]
     mine = [unpack(blocks[f : f + 2] + nexts[f : f + 2], unit) for f in range(0, far, 2)]
     other = [swap(rows_of, 1, count) for rows_of in mine]

time: 72.6 us -> 71.4 us (0.983)
  starting transfers between devices: 22.8 us -> 21 us
  local copies, waits for them, and re-layouts: 0.01 us -> 0.95 us
    ppermute x17, starting transfers between devices: 22.8 us -> 21 us  [swap(): return lax.ppermute(block, 'wide', [(i, i ^ bits) for i in range(count)])]
    unnamed x4 -> x12, local copies, waits for them, and re-layouts: 0.01 us -> 0.95 us
    pallas_call x13 -> x14, Pallas kernels: 8.74 us -> 8.89 us  [call_small(): pl.pallas_call(body, out_shape=shapes, in_specs=[vmem] * len(args) + [pl....]
  transfers between devices with their start and end apart: 17 -> 17, of which waited for: 12 -> 12; matrix products, arithmetic and copies ran while one was open for 0% -> 0% of each run, Pallas kernels for 8% -> 9%
where the time goes in v7:
time: 71.4 us; the launch traced here: 71.3 us
  waiting for transfers between devices  28.9 us (40%)
  starting transfers between devices  21 us (29%)
  Pallas kernels  20.2 us (28%)
  local copies, waits for them, and re-layouts  0.95 us (1%)
    ppermute x17, waiting for transfers between devices, swap(): return lax.ppermute(block, 'wide', [(i, i ^ bits) for i in range(count)])  28.9 us
    ppermute x17, starting transfers between devices, swap(): return lax.ppermute(block, 'wide', [(i, i ^ bits) for i in range(count)])  21 us
    pallas_call x1, Pallas kernels, expert_step(): pl.pallas_call(functools.partial(expert_kernel, unit, far, len(blocks)),...  11.4 us
    pallas_call x14, Pallas kernels, call_small(): pl.pallas_call(body, out_shape=shapes, in_specs=[vmem] * len(args) + [pl....  8.89 us
  transfers between devices with their start and end apart: 17, of which 12 were waited for; matrix products, arithmetic and copies ran while one was open for 0% of the time, Pallas kernels for 9%

profile of v7, /device:TPU:0, one launch (start us, length us, event | category | flops | bytes accessed | tf_op | source)
XLA Modules:
  0.0 71.3 jit_solution(2493412986337380148)
XLA Ops:
  0.0 1.8 %shard_map.64.refs_0_ = bf16[24,3712]{1,0:T(8,128)(2,1)} custom-call(bf16[12,7168]{1,0:T(8,128)(2,1)} %refs_0_.2, s32[8,12]{1,0:T(8,128)} %bitcast.4, f32[8,12]{1,0:T(8,128)} %bitcast.5), custom_call_target="tpu_custom_call" | custom-call | flops 1 | bytes 1 | tf_op jit(solution)/shard_map/pallas_call | solution.py:287
  1.8 3.1 %collective-permute-start = (bf16[24,3712]{1,0:T(8,128)(2,1)}, bf16[24,3712]{1,0:T(8,128)(2,1)S(1)}, u32[]{:S(2)}, u32[]{:S(2)}) collective-permute-start(bf16[24,3712]{1,0:T(8,128)(2,1)} %shard_map.64.refs_0_), channel_id=1, source_target_pairs={{0,4},{1,5},{2,6},{3,7},{4,0},{5,1},{6,2},{7,3},{8,12},{9,13},{10,... | collective-permute-start | bytes 534536 | tf_op jit(solution)/shard_map/ppermute | solution.py:30
  4.9 2.5 %collective-permute-start.3 = (bf16[24,3712]{1,0:T(8,128)(2,1)}, bf16[24,3712]{1,0:T(8,128)(2,1)S(1)}, u32[]{:S(2)}, u32[]{:S(2)}) collective-permute-start(bf16[24,3712]{1,0:T(8,128)(2,1)} %shard_map.64.refs_0_), channel_id=1, source_target_pairs={{0,12},{1,13},{2,14},{3,15},{4,8},{5,9},{6,10},{7,11},{8,4},{9,5},... | collective-permute-start | bytes 534536 | tf_op jit(solution)/shard_map/ppermute | solution.py:30
  7.4 0.1 collective-permute-start.2
  7.5 2.6 %collective-permute-done.refs_1_ = bf16[24,3712]{1,0:T(8,128)(2,1)S(1)} collective-permute-done((bf16[24,3712]{1,0:T(8,128)(2,1)}, bf16[24,3712]{1,0:T(8,128)(2,1)S(1)}, u32[]{:S(2)}, u32[]{:S(2)}) %collective-permute-start) | collective-permute-done | bytes 178208 | tf_op jit(solution)/shard_map/ppermute | solution.py:30
  10.2 0.0 copy-start
  10.2 0.9 %copy-done = bf16[24,3712]{1,0:T(8,128)(2,1)S(1)} copy-done((bf16[24,3712]{1,0:T(8,128)(2,1)S(1)}, bf16[24,3712]{1,0:T(8,128)(2,1)}, u32[]{:S(2)}) %copy-start) | copy-done | bytes 178200
  11.1 1.6 %collective-permute-start.1 = (bf16[48,3712]{1,0:T(8,128)(2,1)S(1)}, bf16[48,3712]{1,0:T(8,128)(2,1)S(1)}, u32[]{:S(2)}, u32[]{:S(2)}) collective-permute-start(bf16[48,3712]{1,0:T(8,128)(2,1)S(1)} %shard_map.65), channel_id=1, source_target_pairs={{0,2},{1,3},{2,0},{3,1},{4,6},{5,7},{6,4},{7,5},{8,10},{9,11},{10,... | collective-permute-start | bytes 1069064 | tf_op jit(solution)/shard_map/ppermute | solution.py:30
  12.7 0.0 slice-start
  12.7 0.0 slice-start.1
  12.7 0.0 slice-start.2
  12.7 5.4 %shard_map.67.refs_1_.refs_5_ = bf16[2,7168,512]{2,1,0:T(8,128)(2,1)S(1)} custom-call(bf16[2,7168,512]{2,1,0:T(8,128)(2,1)} %refs_0_.3), custom_call_target="tpu_custom_call" | custom-call | flops 1 | bytes 16777216 | tf_op jit(solution)/shard_map/pallas_call | solution.py:287
  18.1 0.0 copy-start.1
  18.2 0.0 slice-start.3
  18.2 0.0 collective-permute-done.3.refs_1_
  18.2 0.6 collective-permute-start.5
  18.8 4.7 %collective-permute-done.2.refs_0_ = bf16[24,3712]{1,0:T(8,128)(2,1)S(1)} collective-permute-done((bf16[24,3712]{1,0:T(8,128)(2,1)}, bf16[24,3712]{1,0:T(8,128)(2,1)S(1)}, u32[]{:S(2)}, u32[]{:S(2)}) %collective-permute-start.2) | collective-permute-done | bytes 178208 | tf_op jit(solution)/shard_map/ppermute | solution.py:30
  23.5 1.6 %collective-permute-start.4 = (bf16[24,3712]{1,0:T(8,128)(2,1)S(1)}, bf16[24,3712]{1,0:T(8,128)(2,1)S(1)}, u32[]{:S(2)}, u32[]{:S(2)}) collective-permute-start(bf16[24,3712]{1,0:T(8,128)(2,1)S(1)} %shard_map.68), channel_id=1, source_target_pairs={{0,2},{1,3},{2,0},{3,1},{4,6},{5,7},{6,4},{7,5},{8,10},{9,11},{10,... | collective-permute-start | bytes 534536 | tf_op jit(solution)/shard_map/ppermute | solution.py:30
  25.0 0.0 collective-permute-done.5.refs_3_
  25.0 3.9 %collective-permute-done.4.refs_2_ = bf16[24,3712]{1,0:T(8,128)(2,1)S(1)} collective-permute-done((bf16[24,3712]{1,0:T(8,128)(2,1)S(1)}, bf16[24,3712]{1,0:T(8,128)(2,1)S(1)}, u32[]{:S(2)}, u32[]{:S(2)}) %collective-permute-start.4) | collective-permute-done | bytes 178208 | tf_op jit(solution)/shard_map/ppermute | solution.py:30
  29.0 0.1 shard_map.69.refs_1_
  29.1 0.1 collective-permute-start.7
  29.2 0.0 collective-permute-done.1.refs_2_.refs_3_
  29.2 0.0 copy-done.1
  29.2 0.1 shard_map.66.refs_0_
  29.3 0.5 collective-permute-start.6
  29.8 1.5 %collective-permute-done.7.refs_3_ = bf16[48,7296]{1,0:T(8,128)(2,1)S(1)} collective-permute-done((bf16[48,7296]{1,0:T(8,128)(2,1)S(1)}, bf16[48,7296]{1,0:T(8,128)(2,1)S(1)}, u32[]{:S(2)}, u32[]{:S(2)}) %collective-permute-start.7) | collective-permute-done | bytes 700448 | tf_op jit(solution)/shard_map/ppermute | solution.py:30
  31.3 1.0 %collective-permute-done.6.refs_2_ = bf16[48,7296]{1,0:T(8,128)(2,1)S(1)} collective-permute-done((bf16[48,7296]{1,0:T(8,128)(2,1)S(1)}, bf16[48,7296]{1,0:T(8,128)(2,1)S(1)}, u32[]{:S(2)}, u32[]{:S(2)}) %collective-permute-start.6) | collective-permute-done | bytes 700448 | tf_op jit(solution)/shard_map/ppermute | solution.py:30
  32.3 0.0 slice-done
  32.3 0.0 slice-done.1
  32.3 0.0 slice-done.2
  32.3 0.0 slice-done.3
  32.3 11.4 %shard_map.70 = (bf16[48,3584]{1,0:T(8,128)(2,1)S(1)}, bf16[48,3584]{1,0:T(8,128)(2,1)S(1)}, bf16[144,3584]{1,0:T(8,128)(2,1)S(1)}, bf16[144,3584]{1,0:T(8,128)(2,1)S(1)}) custom-call(bf16[48,7296]{1,0:T(8,128)(2,1)S(1)} %shard_map.66.refs_0_, bf16[48,7296]{1,0:T(8,128)(2,1)S(1)} %shard_map.69.refs_1_, bf16[48,7296]{1,0:T(8,128)(2,1)S(1)} %collective-permute-done.6.refs_2_, ...), custom_call_target="tpu_custom_call" | custom-call | flops 536870912 | bytes 1 | tf_op jit(solution)/shard_map/pallas_call | solution.py:264
  43.7 0.2 collective-permute-start.8
  43.9 1.5 %collective-permute-done.8.refs_1_ = bf16[48,3584]{1,0:T(8,128)(2,1)S(1)} collective-permute-done((bf16[48,3584]{1,0:T(8,128)(2,1)S(1)}, bf16[48,3584]{1,0:T(8,128)(2,1)S(1)}, u32[]{:S(2)}, u32[]{:S(2)}) %collective-permute-start.8) | collective-permute-done | bytes 344096 | tf_op jit(solution)/shard_map/ppermute | solution.py:30
  45.4 0.1 shard_map.71
  45.5 0.2 collective-permute-start.9
  45.7 0.1 shard_map.73
  45.8 1.6 %collective-permute-start.11 = (bf16[24,3584]{1,0:T(8,128)(2,1)S(1)}, bf16[24,3584]{1,0:T(8,128)(2,1)S(1)}, u32[]{:S(2)}, u32[]{:S(2)}) collective-permute-start(bf16[24,3584]{1,0:T(8,128)(2,1)S(1)} %get-tuple-element.22), channel_id=1, source_target_pairs={{0,2},{1,3},{2,0},{3,1},{4,6},{5,7},{6,4},{7,5},{8,10},{9,11},{10,... | collective-permute-start | bytes 516104 | tf_op jit(solution)/shard_map/ppermute | solution.py:30
  47.4 0.8 %collective-permute-done.9.refs_1_ = bf16[144,3584]{1,0:T(8,128)(2,1)S(1)} collective-permute-done((bf16[144,3584]{1,0:T(8,128)(2,1)S(1)}, bf16[144,3584]{1,0:T(8,128)(2,1)S(1)}, u32[]{:S(2)}, u32[]{:S(2)}) %collective-permute-start.9) | collective-permute-done | bytes 1032224 | tf_op jit(solution)/shard_map/ppermute | solution.py:30
  48.2 0.2 shard_map.72
  48.4 1.6 %collective-permute-start.13 = (bf16[24,3584]{1,0:T(8,128)(2,1)S(1)}, bf16[24,3584]{1,0:T(8,128)(2,1)S(1)}, u32[]{:S(2)}, u32[]{:S(2)}) collective-permute-start(bf16[24,3584]{1,0:T(8,128)(2,1)S(1)} %get-tuple-element.23), channel_id=1, source_target_pairs={{0,2},{1,3},{2,0},{3,1},{4,6},{5,7},{6,4},{7,5},{8,10},{9,11},{10,... | collective-permute-start | bytes 516104 | tf_op jit(solution)/shard_map/ppermute | solution.py:30
  50.0 0.5 collective-permute-start.15
  50.5 2.5 %collective-permute-done.11.refs_1_ = bf16[24,3584]{1,0:T(8,128)(2,1)S(1)} collective-permute-done((bf16[24,3584]{1,0:T(8,128)(2,1)S(1)}, bf16[24,3584]{1,0:T(8,128)(2,1)S(1)}, u32[]{:S(2)}, u32[]{:S(2)}) %collective-permute-start.11) | collective-permute-done | bytes 172064 | tf_op jit(solution)/shard_map/ppermute | solution.py:30
  53.1 4.2 %collective-permute-start.12 = (bf16[24,3584]{1,0:T(8,128)(2,1)S(1)}, bf16[24,3584]{1,0:T(8,128)(2,1)S(1)}, u32[]{:S(2)}, u32[]{:S(2)}) collective-permute-start(bf16[24,3584]{1,0:T(8,128)(2,1)S(1)} %shard_map.74), channel_id=1, source_target_pairs={{0,12},{1,13},{2,14},{3,15},{4,8},{5,9},{6,10},{7,11},{8,4},{9,5},... | collective-permute-start | bytes 516104 | tf_op jit(solution)/shard_map/ppermute | solution.py:30
  57.3 1.0 %collective-permute-start.10 = (bf16[24,3584]{1,0:T(8,128)(2,1)S(1)}, bf16[24,3584]{1,0:T(8,128)(2,1)S(1)}, u32[]{:S(2)}, u32[]{:S(2)}) collective-permute-start(bf16[24,3584]{1,0:T(8,128)(2,1)S(1)} %get-tuple-element.19), channel_id=1, source_target_pairs={{0,2},{1,3},{2,0},{3,1},{4,6},{5,7},{6,4},{7,5},{8,10},{9,11},{10,... | collective-permute-start | bytes 516104 | tf_op jit(solution)/shard_map/ppermute | solution.py:30
  58.4 0.0 collective-permute-done.13.refs_1_
  58.4 0.1 collective-permute-start.14
  58.5 1.9 %collective-permute-done.15.refs_1_ = bf16[24,3584]{1,0:T(8,128)(2,1)S(1)} collective-permute-done((bf16[24,3584]{1,0:T(8,128)(2,1)S(1)}, bf16[24,3584]{1,0:T(8,128)(2,1)S(1)}, u32[]{:S(2)}, u32[]{:S(2)}) %collective-permute-start.15) | collective-permute-done | bytes 172064 | tf_op jit(solution)/shard_map/ppermute | solution.py:30
  60.5 1.5 %collective-permute-start.16 = (bf16[24,3584]{1,0:T(8,128)(2,1)S(1)}, bf16[24,3584]{1,0:T(8,128)(2,1)S(1)}, u32[]{:S(2)}, u32[]{:S(2)}) collective-permute-start(bf16[24,3584]{1,0:T(8,128)(2,1)S(1)} %shard_map.77), channel_id=1, source_target_pairs={{0,4},{1,5},{2,6},{3,7},{4,0},{5,1},{6,2},{7,3},{8,12},{9,13},{10,... | collective-permute-start | bytes 516104 | tf_op jit(solution)/shard_map/ppermute | solution.py:30
  62.0 0.2 collective-permute-done.12.refs_0_
  62.2 1.4 %collective-permute-done.10.refs_1_ = bf16[24,3584]{1,0:T(8,128)(2,1)S(1)} collective-permute-done((bf16[24,3584]{1,0:T(8,128)(2,1)S(1)}, bf16[24,3584]{1,0:T(8,128)(2,1)S(1)}, u32[]{:S(2)}, u32[]{:S(2)}) %collective-permute-start.10) | collective-permute-done | bytes 172064 | tf_op jit(solution)/shard_map/ppermute | solution.py:30
  63.6 6.9 %collective-permute-done.14.refs_3_ = bf16[24,3584]{1,0:T(8,128)(2,1)S(1)} collective-permute-done((bf16[24,3584]{1,0:T(8,128)(2,1)S(1)}, bf16[24,3584]{1,0:T(8,128)(2,1)S(1)}, u32[]{:S(2)}, u32[]{:S(2)}) %collective-permute-start.14) | collective-permute-done | bytes 172064 | tf_op jit(solution)/shard_map/ppermute | solution.py:30
  70.4 0.0 collective-permute-done.16.refs_4_
  70.4 0.9 %shard_map.78 = bf16[12,7168]{1,0:T(8,128)(2,1)} custom-call(bf16[72,3584]{1,0:T(8,128)(2,1)S(1)} %get-tuple-element.18.refs_0_, bf16[24,3584]{1,0:T(8,128)(2,1)S(1)} %collective-permute-done.10.refs_1_, bf16[24,3584]{1,0:T(8,128)(2,1)S(1)} %shard_map.75.refs_2_, bf16[24,3584]{1,0:T(8,128)(2,1)S(1)} %collective-permute-done.14.refs_3_, ...), custom_call_target="tpu_custom_call" | custom-call | flops 1 | bytes 1 | tf_op jit(solution)/shard_map/pallas_call | solution.py:287
  (7 shorter events, 0.2 us)
Async XLA Ops:
  1.8 8.3 %collective-permute-start = (bf16[24,3712]{1,0:T(8,128)(2,1)}, bf16[24,3712]{1,0:T(8,128)(2,1)S(1)}, u32[]{:S(2)}, u32[]{:S(2)}) collective-permute-start(bf16[24,3712]{1,0:T(8,128)(2,1)} %shard_map.64.refs_0_), channel_id=1, source_target_pairs={{0,4},{1,5},{2,6},{3,7},{4,0},{5,1},{6,2},{7,3},{8,12},{9,13},{10,... | collective-permute-start | bytes 534536 | tf_op jit(solution)/shard_map/ppermute | solution.py:30
  4.9 13.3 %collective-permute-start.3 = (bf16[24,3712]{1,0:T(8,128)(2,1)}, bf16[24,3712]{1,0:T(8,128)(2,1)S(1)}, u32[]{:S(2)}, u32[]{:S(2)}) collective-permute-start(bf16[24,3712]{1,0:T(8,128)(2,1)} %shard_map.64.refs_0_), channel_id=1, source_target_pairs={{0,12},{1,13},{2,14},{3,15},{4,8},{5,9},{6,10},{7,11},{8,4},{9,5},... | collective-permute-start | bytes 534536 | tf_op jit(solution)/shard_map/ppermute | solution.py:30
  7.4 16.0 %collective-permute-start.2 = (bf16[24,3712]{1,0:T(8,128)(2,1)}, bf16[24,3712]{1,0:T(8,128)(2,1)S(1)}, u32[]{:S(2)}, u32[]{:S(2)}) collective-permute-start(bf16[24,3712]{1,0:T(8,128)(2,1)} %shard_map.64.refs_0_), channel_id=1, source_target_pairs={{0,8},{1,9},{2,10},{3,11},{4,12},{5,13},{6,14},{7,15},{8,0},{9,1},... | collective-permute-start | bytes 534536 | tf_op jit(solution)/shard_map/ppermute | solution.py:30
  10.2 0.9 %copy-start = (bf16[24,3712]{1,0:T(8,128)(2,1)S(1)}, bf16[24,3712]{1,0:T(8,128)(2,1)}, u32[]{:S(2)}) copy-start(bf16[24,3712]{1,0:T(8,128)(2,1)} %shard_map.64.refs_0_) | copy-start | bytes 534532
  11.1 18.1 %collective-permute-start.1 = (bf16[48,3712]{1,0:T(8,128)(2,1)S(1)}, bf16[48,3712]{1,0:T(8,128)(2,1)S(1)}, u32[]{:S(2)}, u32[]{:S(2)}) collective-permute-start(bf16[48,3712]{1,0:T(8,128)(2,1)S(1)} %shard_map.65), channel_id=1, source_target_pairs={{0,2},{1,3},{2,0},{3,1},{4,6},{5,7},{6,4},{7,5},{8,10},{9,11},{10,... | collective-permute-start | bytes 1069064 | tf_op jit(solution)/shard_map/ppermute | solution.py:30
  12.7 19.6 %slice-start = ((s8[14680064]{0:T(1024)(128)(4,1)}), s8[4194304]{0:T(1024)(128)(4,1)S(1)}, s32[]{:S(2)}) async-start(s8[14680064]{0:T(1024)(128)(4,1)} %bitcast.2), calls=%async_computation | async-start | bytes 8388608
  12.7 19.6 %slice-start.1 = ((s8[14680064]{0:T(1024)(128)(4,1)}), s8[4194304]{0:T(1024)(128)(4,1)S(1)}, s32[]{:S(2)}) async-start(s8[14680064]{0:T(1024)(128)(4,1)} %bitcast.2), calls=%async_computation.1 | async-start | bytes 8388608
  12.7 19.6 %slice-start.2 = ((s8[14680064]{0:T(1024)(128)(4,1)}), s8[4194304]{0:T(1024)(128)(4,1)S(1)}, s32[]{:S(2)}) async-start(s8[14680064]{0:T(1024)(128)(4,1)} %bitcast.2), calls=%async_computation.2 | async-start | bytes 8388608
  18.1 11.0 %copy-start.1 = (bf16[24,3712]{1,0:T(8,128)(2,1)S(1)}, bf16[24,3712]{1,0:T(8,128)(2,1)}, u32[]{:S(2)}) copy-start(bf16[24,3712]{1,0:T(8,128)(2,1)} %shard_map.64.refs_0_) | copy-start | bytes 534532
  18.2 14.2 %slice-start.3 = ((s8[14680064]{0:T(1024)(128)(4,1)}), s8[2097152]{0:T(1024)(128)(4,1)S(1)}, s32[]{:S(2)}) async-start(s8[14680064]{0:T(1024)(128)(4,1)} %bitcast.2), calls=%async_computation.3 | async-start | bytes 4194304
  18.2 6.9 %collective-permute-start.5 = (bf16[24,3712]{1,0:T(8,128)(2,1)S(1)}, bf16[24,3712]{1,0:T(8,128)(2,1)S(1)}, u32[]{:S(2)}, u32[]{:S(2)}) collective-permute-start(bf16[24,3712]{1,0:T(8,128)(2,1)S(1)} %collective-permute-done.3.refs_1_), channel_id=1, source_target_pairs={{0,2},{1,3},{2,0},{3,1},{4,6},{5,7},{6,4},{7,5},{8,10},{9,11},{10,... | collective-permute-start | bytes 534536 | tf_op jit(solution)/shard_map/ppermute | solution.py:30
  23.5 5.5 %collective-permute-start.4 = (bf16[24,3712]{1,0:T(8,128)(2,1)S(1)}, bf16[24,3712]{1,0:T(8,128)(2,1)S(1)}, u32[]{:S(2)}, u32[]{:S(2)}) collective-permute-start(bf16[24,3712]{1,0:T(8,128)(2,1)S(1)} %shard_map.68), channel_id=1, source_target_pairs={{0,2},{1,3},{2,0},{3,1},{4,6},{5,7},{6,4},{7,5},{8,10},{9,11},{10,... | collective-permute-start | bytes 534536 | tf_op jit(solution)/shard_map/ppermute | solution.py:30
  29.1 2.2 %collective-permute-start.7 = (bf16[48,7296]{1,0:T(8,128)(2,1)S(1)}, bf16[48,7296]{1,0:T(8,128)(2,1)S(1)}, u32[]{:S(2)}, u32[]{:S(2)}) collective-permute-start(bf16[48,7296]{1,0:T(8,128)(2,1)S(1)} %shard_map.69.refs_1_), channel_id=1, source_target_pairs={{0,1},{1,0},{2,3},{3,2},{4,5},{5,4},{6,7},{7,6},{8,9},{9,8},{10,11... | collective-permute-start | bytes 2101256 | tf_op jit(solution)/shard_map/ppermute | solution.py:30
  29.3 3.0 %collective-permute-start.6 = (bf16[48,7296]{1,0:T(8,128)(2,1)S(1)}, bf16[48,7296]{1,0:T(8,128)(2,1)S(1)}, u32[]{:S(2)}, u32[]{:S(2)}) collective-permute-start(bf16[48,7296]{1,0:T(8,128)(2,1)S(1)} %shard_map.66.refs_0_), channel_id=1, source_target_pairs={{0,1},{1,0},{2,3},{3,2},{4,5},{5,4},{6,7},{7,6},{8,9},{9,8},{10,11... | collective-permute-start | bytes 2101256 | tf_op jit(solution)/shard_map/ppermute | solution.py:30
  43.7 1.7 %collective-permute-start.8 = (bf16[48,3584]{1,0:T(8,128)(2,1)S(1)}, bf16[48,3584]{1,0:T(8,128)(2,1)S(1)}, u32[]{:S(2)}, u32[]{:S(2)}) collective-permute-start(bf16[48,3584]{1,0:T(8,128)(2,1)S(1)} %get-tuple-element.17), channel_id=1, source_target_pairs={{0,1},{1,0},{2,3},{3,2},{4,5},{5,4},{6,7},{7,6},{8,9},{9,8},{10,11... | collective-permute-start | bytes 1032200 | tf_op jit(solution)/shard_map/ppermute | solution.py:30
  45.5 2.7 %collective-permute-start.9 = (bf16[144,3584]{1,0:T(8,128)(2,1)S(1)}, bf16[144,3584]{1,0:T(8,128)(2,1)S(1)}, u32[]{:S(2)}, u32[]{:S(2)}) collective-permute-start(bf16[144,3584]{1,0:T(8,128)(2,1)S(1)} %shard_map.71), channel_id=1, source_target_pairs={{0,1},{1,0},{2,3},{3,2},{4,5},{5,4},{6,7},{7,6},{8,9},{9,8},{10,11... | collective-permute-start | bytes 3096584 | tf_op jit(solution)/shard_map/ppermute | solution.py:30
  45.8 7.3 %collective-permute-start.11 = (bf16[24,3584]{1,0:T(8,128)(2,1)S(1)}, bf16[24,3584]{1,0:T(8,128)(2,1)S(1)}, u32[]{:S(2)}, u32[]{:S(2)}) collective-permute-start(bf16[24,3584]{1,0:T(8,128)(2,1)S(1)} %get-tuple-element.22), channel_id=1, source_target_pairs={{0,2},{1,3},{2,0},{3,1},{4,6},{5,7},{6,4},{7,5},{8,10},{9,11},{10,... | collective-permute-start | bytes 516104 | tf_op jit(solution)/shard_map/ppermute | solution.py:30
  48.4 9.9 %collective-permute-start.13 = (bf16[24,3584]{1,0:T(8,128)(2,1)S(1)}, bf16[24,3584]{1,0:T(8,128)(2,1)S(1)}, u32[]{:S(2)}, u32[]{:S(2)}) collective-permute-start(bf16[24,3584]{1,0:T(8,128)(2,1)S(1)} %get-tuple-element.23), channel_id=1, source_target_pairs={{0,2},{1,3},{2,0},{3,1},{4,6},{5,7},{6,4},{7,5},{8,10},{9,11},{10,... | collective-permute-start | bytes 516104 | tf_op jit(solution)/shard_map/ppermute | solution.py:30
  50.0 10.4 %collective-permute-start.15 = (bf16[24,3584]{1,0:T(8,128)(2,1)S(1)}, bf16[24,3584]{1,0:T(8,128)(2,1)S(1)}, u32[]{:S(2)}, u32[]{:S(2)}) collective-permute-start(bf16[24,3584]{1,0:T(8,128)(2,1)S(1)} %get-tuple-element.24), channel_id=1, source_target_pairs={{0,2},{1,3},{2,0},{3,1},{4,6},{5,7},{6,4},{7,5},{8,10},{9,11},{10,... | collective-permute-start | bytes 516104 | tf_op jit(solution)/shard_map/ppermute | solution.py:30
  53.1 9.1 %collective-permute-start.12 = (bf16[24,3584]{1,0:T(8,128)(2,1)S(1)}, bf16[24,3584]{1,0:T(8,128)(2,1)S(1)}, u32[]{:S(2)}, u32[]{:S(2)}) collective-permute-start(bf16[24,3584]{1,0:T(8,128)(2,1)S(1)} %shard_map.74), channel_id=1, source_target_pairs={{0,12},{1,13},{2,14},{3,15},{4,8},{5,9},{6,10},{7,11},{8,4},{9,5},... | collective-permute-start | bytes 516104 | tf_op jit(solution)/shard_map/ppermute | solution.py:30
  57.3 6.2 %collective-permute-start.10 = (bf16[24,3584]{1,0:T(8,128)(2,1)S(1)}, bf16[24,3584]{1,0:T(8,128)(2,1)S(1)}, u32[]{:S(2)}, u32[]{:S(2)}) collective-permute-start(bf16[24,3584]{1,0:T(8,128)(2,1)S(1)} %get-tuple-element.19), channel_id=1, source_target_pairs={{0,2},{1,3},{2,0},{3,1},{4,6},{5,7},{6,4},{7,5},{8,10},{9,11},{10,... | collective-permute-start | bytes 516104 | tf_op jit(solution)/shard_map/ppermute | solution.py:30
  58.4 12.0 %collective-permute-start.14 = (bf16[24,3584]{1,0:T(8,128)(2,1)S(1)}, bf16[24,3584]{1,0:T(8,128)(2,1)S(1)}, u32[]{:S(2)}, u32[]{:S(2)}) collective-permute-start(bf16[24,3584]{1,0:T(8,128)(2,1)S(1)} %shard_map.76), channel_id=1, source_target_pairs={{0,8},{1,9},{2,10},{3,11},{4,12},{5,13},{6,14},{7,15},{8,0},{9,1},... | collective-permute-start | bytes 516104 | tf_op jit(solution)/shard_map/ppermute | solution.py:30
  60.5 10.0 %collective-permute-start.16 = (bf16[24,3584]{1,0:T(8,128)(2,1)S(1)}, bf16[24,3584]{1,0:T(8,128)(2,1)S(1)}, u32[]{:S(2)}, u32[]{:S(2)}) collective-permute-start(bf16[24,3584]{1,0:T(8,128)(2,1)S(1)} %shard_map.77), channel_id=1, source_target_pairs={{0,4},{1,5},{2,6},{3,7},{4,0},{5,1},{6,2},{7,3},{8,12},{9,13},{10,... | collective-permute-start | bytes 516104 | tf_op jit(solution)/shard_map/ppermute | solution.py:30

commit v8 on v7

--- a/solution.py
+++ b/solution.py
@@ -72,11 +72,10 @@
     ]
     for copy in copies:
         copy.start()
-    for copy in copies:
+    for copy in copies[1:]:
         copy.wait()
     rows, width = tokens_ref.shape
     half = width // 2
-    rows_ref[0:rows, :width] = tokens_ref[...].astype(f32)
     experts = GROUPS * EXP_G
     catalog = lax.broadcasted_iota(jnp.int32, (experts, rows), 0)
     weight = jnp.zeros((experts, rows), f32)
@@ -88,6 +87,8 @@
         weight.astype(bf16), eye, (((0,), (0,)), ((), ())), preferred_element_type=f32
     )
     rows_ref[:, width + LANES :] = jnp.zeros((rows_ref.shape[0], LANES), f32)
+    copies[0].wait()
+    rows_ref[0:rows, :width] = tokens_ref[...].astype(f32)
     out_ref[:, :half] = pack_columns(rows_ref, slice(0, half), slice(half, width))
     out_ref[:, half:] = pack_columns(rows_ref, slice(width, width + LANES), slice(width + LANES, width + 2 * LANES))
 

time: 71.4 us -> 71.4 us (level)
  no operation moved by 1% of the time
where the time goes in v8:
time: 71.4 us; the launch traced here: 71.2 us
  waiting for transfers between devices  29 us (41%)
  starting transfers between devices  20.9 us (29%)
  Pallas kernels  20.2 us (28%)
  local copies, waits for them, and re-layouts  0.95 us (1%)
    ppermute x17, waiting for transfers between devices, swap(): return lax.ppermute(block, 'wide', [(i, i ^ bits) for i in range(count)])  29 us
    ppermute x17, starting transfers between devices, swap(): return lax.ppermute(block, 'wide', [(i, i ^ bits) for i in range(count)])  20.9 us
    pallas_call x1, Pallas kernels, expert_step(): pl.pallas_call(functools.partial(expert_kernel, unit, far, len(blocks)),...  11.4 us
    pallas_call x14, Pallas kernels, call_small(): pl.pallas_call(body, out_shape=shapes, in_specs=[vmem] * len(args) + [pl....  8.79 us
  transfers between devices with their start and end apart: 17, of which 12 were waited for; matrix products, arithmetic and copies ran while one was open for 0% of the time, Pallas kernels for 9%

profile of v8, /device:TPU:0, one launch (start us, length us, event | category | flops | bytes accessed | tf_op | source)
XLA Modules:
  0.0 71.2 jit_solution(9985101267614540591)
XLA Ops:
  0.0 1.7 %shard_map.64.refs_0_ = bf16[24,3712]{1,0:T(8,128)(2,1)} custom-call(bf16[12,7168]{1,0:T(8,128)(2,1)} %refs_0_.2, s32[8,12]{1,0:T(8,128)} %bitcast.4, f32[8,12]{1,0:T(8,128)} %bitcast.5), custom_call_target="tpu_custom_call" | custom-call | flops 1 | bytes 1 | tf_op jit(solution)/shard_map/pallas_call | solution.py:288
  1.7 3.1 %collective-permute-start = (bf16[24,3712]{1,0:T(8,128)(2,1)}, bf16[24,3712]{1,0:T(8,128)(2,1)S(1)}, u32[]{:S(2)}, u32[]{:S(2)}) collective-permute-start(bf16[24,3712]{1,0:T(8,128)(2,1)} %shard_map.64.refs_0_), channel_id=1, source_target_pairs={{0,4},{1,5},{2,6},{3,7},{4,0},{5,1},{6,2},{7,3},{8,12},{9,13},{10,... | collective-permute-start | bytes 534536 | tf_op jit(solution)/shard_map/ppermute | solution.py:30
  4.8 2.5 %collective-permute-start.3 = (bf16[24,3712]{1,0:T(8,128)(2,1)}, bf16[24,3712]{1,0:T(8,128)(2,1)S(1)}, u32[]{:S(2)}, u32[]{:S(2)}) collective-permute-start(bf16[24,3712]{1,0:T(8,128)(2,1)} %shard_map.64.refs_0_), channel_id=1, source_target_pairs={{0,12},{1,13},{2,14},{3,15},{4,8},{5,9},{6,10},{7,11},{8,4},{9,5},... | collective-permute-start | bytes 534536 | tf_op jit(solution)/shard_map/ppermute | solution.py:30
  7.3 0.1 collective-permute-start.2
  7.4 2.6 %collective-permute-done.refs_1_ = bf16[24,3712]{1,0:T(8,128)(2,1)S(1)} collective-permute-done((bf16[24,3712]{1,0:T(8,128)(2,1)}, bf16[24,3712]{1,0:T(8,128)(2,1)S(1)}, u32[]{:S(2)}, u32[]{:S(2)}) %collective-permute-start) | collective-permute-done | bytes 178208 | tf_op jit(solution)/shard_map/ppermute | solution.py:30
  10.1 0.0 copy-start
  10.1 0.9 %copy-done = bf16[24,3712]{1,0:T(8,128)(2,1)S(1)} copy-done((bf16[24,3712]{1,0:T(8,128)(2,1)S(1)}, bf16[24,3712]{1,0:T(8,128)(2,1)}, u32[]{:S(2)}) %copy-start) | copy-done | bytes 178200
  11.0 1.6 %collective-permute-start.1 = (bf16[48,3712]{1,0:T(8,128)(2,1)S(1)}, bf16[48,3712]{1,0:T(8,128)(2,1)S(1)}, u32[]{:S(2)}, u32[]{:S(2)}) collective-permute-start(bf16[48,3712]{1,0:T(8,128)(2,1)S(1)} %shard_map.65), channel_id=1, source_target_pairs={{0,2},{1,3},{2,0},{3,1},{4,6},{5,7},{6,4},{7,5},{8,10},{9,11},{10,... | collective-permute-start | bytes 1069064 | tf_op jit(solution)/shard_map/ppermute | solution.py:30
  12.6 0.0 slice-start
  12.6 0.0 slice-start.1
  12.6 0.0 slice-start.2
  12.6 5.4 %shard_map.67.refs_1_.refs_5_ = bf16[2,7168,512]{2,1,0:T(8,128)(2,1)S(1)} custom-call(bf16[2,7168,512]{2,1,0:T(8,128)(2,1)} %refs_0_.3), custom_call_target="tpu_custom_call" | custom-call | flops 1 | bytes 16777216 | tf_op jit(solution)/shard_map/pallas_call | solution.py:288
  18.1 0.0 copy-start.1
  18.1 0.0 slice-start.3
  18.1 0.0 collective-permute-done.3.refs_1_
  18.1 0.6 collective-permute-start.5
  18.7 4.7 %collective-permute-done.2.refs_0_ = bf16[24,3712]{1,0:T(8,128)(2,1)S(1)} collective-permute-done((bf16[24,3712]{1,0:T(8,128)(2,1)}, bf16[24,3712]{1,0:T(8,128)(2,1)S(1)}, u32[]{:S(2)}, u32[]{:S(2)}) %collective-permute-start.2) | collective-permute-done | bytes 178208 | tf_op jit(solution)/shard_map/ppermute | solution.py:30
  23.4 1.6 %collective-permute-start.4 = (bf16[24,3712]{1,0:T(8,128)(2,1)S(1)}, bf16[24,3712]{1,0:T(8,128)(2,1)S(1)}, u32[]{:S(2)}, u32[]{:S(2)}) collective-permute-start(bf16[24,3712]{1,0:T(8,128)(2,1)S(1)} %shard_map.68), channel_id=1, source_target_pairs={{0,2},{1,3},{2,0},{3,1},{4,6},{5,7},{6,4},{7,5},{8,10},{9,11},{10,... | collective-permute-start | bytes 534536 | tf_op jit(solution)/shard_map/ppermute | solution.py:30
  24.9 0.0 collective-permute-done.5.refs_3_
  24.9 3.9 %collective-permute-done.4.refs_2_ = bf16[24,3712]{1,0:T(8,128)(2,1)S(1)} collective-permute-done((bf16[24,3712]{1,0:T(8,128)(2,1)S(1)}, bf16[24,3712]{1,0:T(8,128)(2,1)S(1)}, u32[]{:S(2)}, u32[]{:S(2)}) %collective-permute-start.4) | collective-permute-done | bytes 178208 | tf_op jit(solution)/shard_map/ppermute | solution.py:30
  28.9 0.1 shard_map.69.refs_1_
  29.0 0.1 collective-permute-start.7
  29.1 0.0 collective-permute-done.1.refs_2_.refs_3_
  29.1 0.0 copy-done.1
  29.1 0.1 shard_map.66.refs_0_
  29.2 0.5 collective-permute-start.6
  29.7 1.5 %collective-permute-done.7.refs_3_ = bf16[48,7296]{1,0:T(8,128)(2,1)S(1)} collective-permute-done((bf16[48,7296]{1,0:T(8,128)(2,1)S(1)}, bf16[48,7296]{1,0:T(8,128)(2,1)S(1)}, u32[]{:S(2)}, u32[]{:S(2)}) %collective-permute-start.7) | collective-permute-done | bytes 700448 | tf_op jit(solution)/shard_map/ppermute | solution.py:30
  31.2 1.0 %collective-permute-done.6.refs_2_ = bf16[48,7296]{1,0:T(8,128)(2,1)S(1)} collective-permute-done((bf16[48,7296]{1,0:T(8,128)(2,1)S(1)}, bf16[48,7296]{1,0:T(8,128)(2,1)S(1)}, u32[]{:S(2)}, u32[]{:S(2)}) %collective-permute-start.6) | collective-permute-done | bytes 700448 | tf_op jit(solution)/shard_map/ppermute | solution.py:30
  32.2 0.0 slice-done
  32.2 0.0 slice-done.1
  32.2 0.0 slice-done.2
  32.2 0.0 slice-done.3
  32.2 11.4 %shard_map.70 = (bf16[48,3584]{1,0:T(8,128)(2,1)S(1)}, bf16[48,3584]{1,0:T(8,128)(2,1)S(1)}, bf16[144,3584]{1,0:T(8,128)(2,1)S(1)}, bf16[144,3584]{1,0:T(8,128)(2,1)S(1)}) custom-call(bf16[48,7296]{1,0:T(8,128)(2,1)S(1)} %shard_map.66.refs_0_, bf16[48,7296]{1,0:T(8,128)(2,1)S(1)} %shard_map.69.refs_1_, bf16[48,7296]{1,0:T(8,128)(2,1)S(1)} %collective-permute-done.6.refs_2_, ...), custom_call_target="tpu_custom_call" | custom-call | flops 536870912 | bytes 1 | tf_op jit(solution)/shard_map/pallas_call | solution.py:265
  43.6 0.2 collective-permute-start.8
  43.8 1.5 %collective-permute-done.8.refs_1_ = bf16[48,3584]{1,0:T(8,128)(2,1)S(1)} collective-permute-done((bf16[48,3584]{1,0:T(8,128)(2,1)S(1)}, bf16[48,3584]{1,0:T(8,128)(2,1)S(1)}, u32[]{:S(2)}, u32[]{:S(2)}) %collective-permute-start.8) | collective-permute-done | bytes 344096 | tf_op jit(solution)/shard_map/ppermute | solution.py:30
  45.3 0.1 shard_map.71
  45.4 0.2 collective-permute-start.9
  45.6 0.1 shard_map.73
  45.7 1.6 %collective-permute-start.11 = (bf16[24,3584]{1,0:T(8,128)(2,1)S(1)}, bf16[24,3584]{1,0:T(8,128)(2,1)S(1)}, u32[]{:S(2)}, u32[]{:S(2)}) collective-permute-start(bf16[24,3584]{1,0:T(8,128)(2,1)S(1)} %get-tuple-element.22), channel_id=1, source_target_pairs={{0,2},{1,3},{2,0},{3,1},{4,6},{5,7},{6,4},{7,5},{8,10},{9,11},{10,... | collective-permute-start | bytes 516104 | tf_op jit(solution)/shard_map/ppermute | solution.py:30
  47.3 0.8 %collective-permute-done.9.refs_1_ = bf16[144,3584]{1,0:T(8,128)(2,1)S(1)} collective-permute-done((bf16[144,3584]{1,0:T(8,128)(2,1)S(1)}, bf16[144,3584]{1,0:T(8,128)(2,1)S(1)}, u32[]{:S(2)}, u32[]{:S(2)}) %collective-permute-start.9) | collective-permute-done | bytes 1032224 | tf_op jit(solution)/shard_map/ppermute | solution.py:30
  48.1 0.2 shard_map.72
  48.4 1.6 %collective-permute-start.13 = (bf16[24,3584]{1,0:T(8,128)(2,1)S(1)}, bf16[24,3584]{1,0:T(8,128)(2,1)S(1)}, u32[]{:S(2)}, u32[]{:S(2)}) collective-permute-start(bf16[24,3584]{1,0:T(8,128)(2,1)S(1)} %get-tuple-element.23), channel_id=1, source_target_pairs={{0,2},{1,3},{2,0},{3,1},{4,6},{5,7},{6,4},{7,5},{8,10},{9,11},{10,... | collective-permute-start | bytes 516104 | tf_op jit(solution)/shard_map/ppermute | solution.py:30
  49.9 0.5 collective-permute-start.15
  50.4 2.5 %collective-permute-done.11.refs_1_ = bf16[24,3584]{1,0:T(8,128)(2,1)S(1)} collective-permute-done((bf16[24,3584]{1,0:T(8,128)(2,1)S(1)}, bf16[24,3584]{1,0:T(8,128)(2,1)S(1)}, u32[]{:S(2)}, u32[]{:S(2)}) %collective-permute-start.11) | collective-permute-done | bytes 172064 | tf_op jit(solution)/shard_map/ppermute | solution.py:30
  53.0 4.2 %collective-permute-start.12 = (bf16[24,3584]{1,0:T(8,128)(2,1)S(1)}, bf16[24,3584]{1,0:T(8,128)(2,1)S(1)}, u32[]{:S(2)}, u32[]{:S(2)}) collective-permute-start(bf16[24,3584]{1,0:T(8,128)(2,1)S(1)} %shard_map.74), channel_id=1, source_target_pairs={{0,12},{1,13},{2,14},{3,15},{4,8},{5,9},{6,10},{7,11},{8,4},{9,5},... | collective-permute-start | bytes 516104 | tf_op jit(solution)/shard_map/ppermute | solution.py:30
  57.3 1.0 %collective-permute-start.10 = (bf16[24,3584]{1,0:T(8,128)(2,1)S(1)}, bf16[24,3584]{1,0:T(8,128)(2,1)S(1)}, u32[]{:S(2)}, u32[]{:S(2)}) collective-permute-start(bf16[24,3584]{1,0:T(8,128)(2,1)S(1)} %get-tuple-element.19), channel_id=1, source_target_pairs={{0,2},{1,3},{2,0},{3,1},{4,6},{5,7},{6,4},{7,5},{8,10},{9,11},{10,... | collective-permute-start | bytes 516104 | tf_op jit(solution)/shard_map/ppermute | solution.py:30
  58.3 0.0 collective-permute-done.13.refs_1_
  58.3 0.1 collective-permute-start.14
  58.4 2.0 %collective-permute-done.15.refs_1_ = bf16[24,3584]{1,0:T(8,128)(2,1)S(1)} collective-permute-done((bf16[24,3584]{1,0:T(8,128)(2,1)S(1)}, bf16[24,3584]{1,0:T(8,128)(2,1)S(1)}, u32[]{:S(2)}, u32[]{:S(2)}) %collective-permute-start.15) | collective-permute-done | bytes 172064 | tf_op jit(solution)/shard_map/ppermute | solution.py:30
  60.4 1.5 %collective-permute-start.16 = (bf16[24,3584]{1,0:T(8,128)(2,1)S(1)}, bf16[24,3584]{1,0:T(8,128)(2,1)S(1)}, u32[]{:S(2)}, u32[]{:S(2)}) collective-permute-start(bf16[24,3584]{1,0:T(8,128)(2,1)S(1)} %shard_map.77), channel_id=1, source_target_pairs={{0,4},{1,5},{2,6},{3,7},{4,0},{5,1},{6,2},{7,3},{8,12},{9,13},{10,... | collective-permute-start | bytes 516104 | tf_op jit(solution)/shard_map/ppermute | solution.py:30
  61.9 0.2 collective-permute-done.12.refs_0_
  62.1 1.4 %collective-permute-done.10.refs_1_ = bf16[24,3584]{1,0:T(8,128)(2,1)S(1)} collective-permute-done((bf16[24,3584]{1,0:T(8,128)(2,1)S(1)}, bf16[24,3584]{1,0:T(8,128)(2,1)S(1)}, u32[]{:S(2)}, u32[]{:S(2)}) %collective-permute-start.10) | collective-permute-done | bytes 172064 | tf_op jit(solution)/shard_map/ppermute | solution.py:30
  63.5 6.8 %collective-permute-done.14.refs_3_ = bf16[24,3584]{1,0:T(8,128)(2,1)S(1)} collective-permute-done((bf16[24,3584]{1,0:T(8,128)(2,1)S(1)}, bf16[24,3584]{1,0:T(8,128)(2,1)S(1)}, u32[]{:S(2)}, u32[]{:S(2)}) %collective-permute-start.14) | collective-permute-done | bytes 172064 | tf_op jit(solution)/shard_map/ppermute | solution.py:30
  70.3 0.0 collective-permute-done.16.refs_4_
  70.3 0.9 %shard_map.78 = bf16[12,7168]{1,0:T(8,128)(2,1)} custom-call(bf16[72,3584]{1,0:T(8,128)(2,1)S(1)} %get-tuple-element.18.refs_0_, bf16[24,3584]{1,0:T(8,128)(2,1)S(1)} %collective-permute-done.10.refs_1_, bf16[24,3584]{1,0:T(8,128)(2,1)S(1)} %shard_map.75.refs_2_, bf16[24,3584]{1,0:T(8,128)(2,1)S(1)} %collective-permute-done.14.refs_3_, ...), custom_call_target="tpu_custom_call" | custom-call | flops 1 | bytes 1 | tf_op jit(solution)/shard_map/pallas_call | solution.py:288
  (7 shorter events, 0.2 us)
Async XLA Ops:
  1.7 8.3 %collective-permute-start = (bf16[24,3712]{1,0:T(8,128)(2,1)}, bf16[24,3712]{1,0:T(8,128)(2,1)S(1)}, u32[]{:S(2)}, u32[]{:S(2)}) collective-permute-start(bf16[24,3712]{1,0:T(8,128)(2,1)} %shard_map.64.refs_0_), channel_id=1, source_target_pairs={{0,4},{1,5},{2,6},{3,7},{4,0},{5,1},{6,2},{7,3},{8,12},{9,13},{10,... | collective-permute-start | bytes 534536 | tf_op jit(solution)/shard_map/ppermute | solution.py:30
  4.8 13.3 %collective-permute-start.3 = (bf16[24,3712]{1,0:T(8,128)(2,1)}, bf16[24,3712]{1,0:T(8,128)(2,1)S(1)}, u32[]{:S(2)}, u32[]{:S(2)}) collective-permute-start(bf16[24,3712]{1,0:T(8,128)(2,1)} %shard_map.64.refs_0_), channel_id=1, source_target_pairs={{0,12},{1,13},{2,14},{3,15},{4,8},{5,9},{6,10},{7,11},{8,4},{9,5},... | collective-permute-start | bytes 534536 | tf_op jit(solution)/shard_map/ppermute | solution.py:30
  7.3 16.0 %collective-permute-start.2 = (bf16[24,3712]{1,0:T(8,128)(2,1)}, bf16[24,3712]{1,0:T(8,128)(2,1)S(1)}, u32[]{:S(2)}, u32[]{:S(2)}) collective-permute-start(bf16[24,3712]{1,0:T(8,128)(2,1)} %shard_map.64.refs_0_), channel_id=1, source_target_pairs={{0,8},{1,9},{2,10},{3,11},{4,12},{5,13},{6,14},{7,15},{8,0},{9,1},... | collective-permute-start | bytes 534536 | tf_op jit(solution)/shard_map/ppermute | solution.py:30
  10.1 0.9 %copy-start = (bf16[24,3712]{1,0:T(8,128)(2,1)S(1)}, bf16[24,3712]{1,0:T(8,128)(2,1)}, u32[]{:S(2)}) copy-start(bf16[24,3712]{1,0:T(8,128)(2,1)} %shard_map.64.refs_0_) | copy-start | bytes 534532
  11.0 18.1 %collective-permute-start.1 = (bf16[48,3712]{1,0:T(8,128)(2,1)S(1)}, bf16[48,3712]{1,0:T(8,128)(2,1)S(1)}, u32[]{:S(2)}, u32[]{:S(2)}) collective-permute-start(bf16[48,3712]{1,0:T(8,128)(2,1)S(1)} %shard_map.65), channel_id=1, source_target_pairs={{0,2},{1,3},{2,0},{3,1},{4,6},{5,7},{6,4},{7,5},{8,10},{9,11},{10,... | collective-permute-start | bytes 1069064 | tf_op jit(solution)/shard_map/ppermute | solution.py:30
  12.6 19.6 %slice-start = ((s8[14680064]{0:T(1024)(128)(4,1)}), s8[4194304]{0:T(1024)(128)(4,1)S(1)}, s32[]{:S(2)}) async-start(s8[14680064]{0:T(1024)(128)(4,1)} %bitcast.2), calls=%async_computation | async-start | bytes 8388608
  12.6 19.6 %slice-start.1 = ((s8[14680064]{0:T(1024)(128)(4,1)}), s8[4194304]{0:T(1024)(128)(4,1)S(1)}, s32[]{:S(2)}) async-start(s8[14680064]{0:T(1024)(128)(4,1)} %bitcast.2), calls=%async_computation.1 | async-start | bytes 8388608
  12.6 19.6 %slice-start.2 = ((s8[14680064]{0:T(1024)(128)(4,1)}), s8[4194304]{0:T(1024)(128)(4,1)S(1)}, s32[]{:S(2)}) async-start(s8[14680064]{0:T(1024)(128)(4,1)} %bitcast.2), calls=%async_computation.2 | async-start | bytes 8388608
  18.1 11.0 %copy-start.1 = (bf16[24,3712]{1,0:T(8,128)(2,1)S(1)}, bf16[24,3712]{1,0:T(8,128)(2,1)}, u32[]{:S(2)}) copy-start(bf16[24,3712]{1,0:T(8,128)(2,1)} %shard_map.64.refs_0_) | copy-start | bytes 534532
  18.1 14.2 %slice-start.3 = ((s8[14680064]{0:T(1024)(128)(4,1)}), s8[2097152]{0:T(1024)(128)(4,1)S(1)}, s32[]{:S(2)}) async-start(s8[14680064]{0:T(1024)(128)(4,1)} %bitcast.2), calls=%async_computation.3 | async-start | bytes 4194304
  18.1 6.9 %collective-permute-start.5 = (bf16[24,3712]{1,0:T(8,128)(2,1)S(1)}, bf16[24,3712]{1,0:T(8,128)(2,1)S(1)}, u32[]{:S(2)}, u32[]{:S(2)}) collective-permute-start(bf16[24,3712]{1,0:T(8,128)(2,1)S(1)} %collective-permute-done.3.refs_1_), channel_id=1, source_target_pairs={{0,2},{1,3},{2,0},{3,1},{4,6},{5,7},{6,4},{7,5},{8,10},{9,11},{10,... | collective-permute-start | bytes 534536 | tf_op jit(solution)/shard_map/ppermute | solution.py:30
  23.4 5.5 %collective-permute-start.4 = (bf16[24,3712]{1,0:T(8,128)(2,1)S(1)}, bf16[24,3712]{1,0:T(8,128)(2,1)S(1)}, u32[]{:S(2)}, u32[]{:S(2)}) collective-permute-start(bf16[24,3712]{1,0:T(8,128)(2,1)S(1)} %shard_map.68), channel_id=1, source_target_pairs={{0,2},{1,3},{2,0},{3,1},{4,6},{5,7},{6,4},{7,5},{8,10},{9,11},{10,... | collective-permute-start | bytes 534536 | tf_op jit(solution)/shard_map/ppermute | solution.py:30
  29.0 2.2 %collective-permute-start.7 = (bf16[48,7296]{1,0:T(8,128)(2,1)S(1)}, bf16[48,7296]{1,0:T(8,128)(2,1)S(1)}, u32[]{:S(2)}, u32[]{:S(2)}) collective-permute-start(bf16[48,7296]{1,0:T(8,128)(2,1)S(1)} %shard_map.69.refs_1_), channel_id=1, source_target_pairs={{0,1},{1,0},{2,3},{3,2},{4,5},{5,4},{6,7},{7,6},{8,9},{9,8},{10,11... | collective-permute-start | bytes 2101256 | tf_op jit(solution)/shard_map/ppermute | solution.py:30
  29.2 3.0 %collective-permute-start.6 = (bf16[48,7296]{1,0:T(8,128)(2,1)S(1)}, bf16[48,7296]{1,0:T(8,128)(2,1)S(1)}, u32[]{:S(2)}, u32[]{:S(2)}) collective-permute-start(bf16[48,7296]{1,0:T(8,128)(2,1)S(1)} %shard_map.66.refs_0_), channel_id=1, source_target_pairs={{0,1},{1,0},{2,3},{3,2},{4,5},{5,4},{6,7},{7,6},{8,9},{9,8},{10,11... | collective-permute-start | bytes 2101256 | tf_op jit(solution)/shard_map/ppermute | solution.py:30
  43.6 1.7 %collective-permute-start.8 = (bf16[48,3584]{1,0:T(8,128)(2,1)S(1)}, bf16[48,3584]{1,0:T(8,128)(2,1)S(1)}, u32[]{:S(2)}, u32[]{:S(2)}) collective-permute-start(bf16[48,3584]{1,0:T(8,128)(2,1)S(1)} %get-tuple-element.17), channel_id=1, source_target_pairs={{0,1},{1,0},{2,3},{3,2},{4,5},{5,4},{6,7},{7,6},{8,9},{9,8},{10,11... | collective-permute-start | bytes 1032200 | tf_op jit(solution)/shard_map/ppermute | solution.py:30
  45.4 2.7 %collective-permute-start.9 = (bf16[144,3584]{1,0:T(8,128)(2,1)S(1)}, bf16[144,3584]{1,0:T(8,128)(2,1)S(1)}, u32[]{:S(2)}, u32[]{:S(2)}) collective-permute-start(bf16[144,3584]{1,0:T(8,128)(2,1)S(1)} %shard_map.71), channel_id=1, source_target_pairs={{0,1},{1,0},{2,3},{3,2},{4,5},{5,4},{6,7},{7,6},{8,9},{9,8},{10,11... | collective-permute-start | bytes 3096584 | tf_op jit(solution)/shard_map/ppermute | solution.py:30
  45.7 7.3 %collective-permute-start.11 = (bf16[24,3584]{1,0:T(8,128)(2,1)S(1)}, bf16[24,3584]{1,0:T(8,128)(2,1)S(1)}, u32[]{:S(2)}, u32[]{:S(2)}) collective-permute-start(bf16[24,3584]{1,0:T(8,128)(2,1)S(1)} %get-tuple-element.22), channel_id=1, source_target_pairs={{0,2},{1,3},{2,0},{3,1},{4,6},{5,7},{6,4},{7,5},{8,10},{9,11},{10,... | collective-permute-start | bytes 516104 | tf_op jit(solution)/shard_map/ppermute | solution.py:30
  48.4 9.9 %collective-permute-start.13 = (bf16[24,3584]{1,0:T(8,128)(2,1)S(1)}, bf16[24,3584]{1,0:T(8,128)(2,1)S(1)}, u32[]{:S(2)}, u32[]{:S(2)}) collective-permute-start(bf16[24,3584]{1,0:T(8,128)(2,1)S(1)} %get-tuple-element.23), channel_id=1, source_target_pairs={{0,2},{1,3},{2,0},{3,1},{4,6},{5,7},{6,4},{7,5},{8,10},{9,11},{10,... | collective-permute-start | bytes 516104 | tf_op jit(solution)/shard_map/ppermute | solution.py:30
  49.9 10.4 %collective-permute-start.15 = (bf16[24,3584]{1,0:T(8,128)(2,1)S(1)}, bf16[24,3584]{1,0:T(8,128)(2,1)S(1)}, u32[]{:S(2)}, u32[]{:S(2)}) collective-permute-start(bf16[24,3584]{1,0:T(8,128)(2,1)S(1)} %get-tuple-element.24), channel_id=1, source_target_pairs={{0,2},{1,3},{2,0},{3,1},{4,6},{5,7},{6,4},{7,5},{8,10},{9,11},{10,... | collective-permute-start | bytes 516104 | tf_op jit(solution)/shard_map/ppermute | solution.py:30
  53.0 9.1 %collective-permute-start.12 = (bf16[24,3584]{1,0:T(8,128)(2,1)S(1)}, bf16[24,3584]{1,0:T(8,128)(2,1)S(1)}, u32[]{:S(2)}, u32[]{:S(2)}) collective-permute-start(bf16[24,3584]{1,0:T(8,128)(2,1)S(1)} %shard_map.74), channel_id=1, source_target_pairs={{0,12},{1,13},{2,14},{3,15},{4,8},{5,9},{6,10},{7,11},{8,4},{9,5},... | collective-permute-start | bytes 516104 | tf_op jit(solution)/shard_map/ppermute | solution.py:30
  57.3 6.2 %collective-permute-start.10 = (bf16[24,3584]{1,0:T(8,128)(2,1)S(1)}, bf16[24,3584]{1,0:T(8,128)(2,1)S(1)}, u32[]{:S(2)}, u32[]{:S(2)}) collective-permute-start(bf16[24,3584]{1,0:T(8,128)(2,1)S(1)} %get-tuple-element.19), channel_id=1, source_target_pairs={{0,2},{1,3},{2,0},{3,1},{4,6},{5,7},{6,4},{7,5},{8,10},{9,11},{10,... | collective-permute-start | bytes 516104 | tf_op jit(solution)/shard_map/ppermute | solution.py:30
  58.3 12.0 %collective-permute-start.14 = (bf16[24,3584]{1,0:T(8,128)(2,1)S(1)}, bf16[24,3584]{1,0:T(8,128)(2,1)S(1)}, u32[]{:S(2)}, u32[]{:S(2)}) collective-permute-start(bf16[24,3584]{1,0:T(8,128)(2,1)S(1)} %shard_map.76), channel_id=1, source_target_pairs={{0,8},{1,9},{2,10},{3,11},{4,12},{5,13},{6,14},{7,15},{8,0},{9,1},... | collective-permute-start | bytes 516104 | tf_op jit(solution)/shard_map/ppermute | solution.py:30
  60.4 9.9 %collective-permute-start.16 = (bf16[24,3584]{1,0:T(8,128)(2,1)S(1)}, bf16[24,3584]{1,0:T(8,128)(2,1)S(1)}, u32[]{:S(2)}, u32[]{:S(2)}) collective-permute-start(bf16[24,3584]{1,0:T(8,128)(2,1)S(1)} %shard_map.77), channel_id=1, source_target_pairs={{0,4},{1,5},{2,6},{3,7},{4,0},{5,1},{6,2},{7,3},{8,12},{9,13},{10,... | collective-permute-start | bytes 516104 | tf_op jit(solution)/shard_map/ppermute | solution.py:30
